TPU v7x, 32 devices: a whole 2x2x4 slice. The times are simulated.
32 devices in a mesh: grp: 2 (over y), chan: 2 (over x), tm: 4 (over z), pol: 2 (over core).
Axes of the slice: x: 2, y: 2, z: 4, core: 2. Of those that a mesh axis runs over, the one named last changes fastest.
Arguments:
- voltages: bfloat16 [4, 2, 256, 32768], P('grp', 'pol', 'chan', 'tm'), parts along dimension 0, may hold values from -6 to 6
- taps_filter: float32 [16, 2048], replicated, may hold values from -1.5 to 1.5
- tile_a: int32 [14, 64], replicated, may hold values from 0 to 255
- tile_b: int32 [14, 64], replicated, may hold values from 0 to 255
- tile_owner: int32 [14], replicated, may hold values from 0 to 1, as said below
- tile_flags: int32 [14, 16], replicated, may hold values 0 or 1
Outputs:
- visibility: float32 [16, 256, 4, 2, 64, 128], P('pol', ('chan', 'tm'), 'grp'), parts along dimension 2
There are 2 independent parts, one for each index of `grp`. A program takes and returns all parts, laid end to end along the dimension named above; an argument that names none is the same for every part. Nothing has to cross between parts.
Inputs may be any that keep to these rules, and one draw needn't show every extreme that they name: `tile_owner`: one owner holds exactly 8 tiles and the other owner holds all the rest.
All inputs are finite; a program needn't handle non-finite values.
Results may differ from a plain program's by a relative error of at most 0.0035.
Values may be sent and summed in bfloat16 or wider, within the bound.
No kernel may reach another device: no remote copies, remote signals or barrier semaphores. Data moves between devices by JAX's collectives and lax.ppermute only.
A program may use at most 128 MiB of HBM per device.

v0:
```python
import math

import jax
import jax.numpy as jnp
import numpy as np
from jax import lax
from jax.experimental import pallas as pl
from jax.experimental.pallas import tpu as pltpu
from jax.sharding import PartitionSpec as P

AVG = 8
CAP = 8
RADIX = 16
LANES = 128
ROWS = 16


radix_first = 32


def from_behind(value, axis, steps):
    count = lax.axis_size(axis)
    first, last = (max(0, -steps), min(count, count - steps))
    return lax.ppermute(value, axis, [(source, source + steps) for source in range(first, last)])


def fourier(filtered):
    length = filtered.shape[-1]
    second = length // radix_first
    exact_mode = lax.Precision.HIGHEST
    grid = filtered.reshape(filtered.shape[:-1] + (radix_first, second))
    outer = jnp.arange(radix_first, dtype=jnp.int32)
    inner = jnp.arange(second, dtype=jnp.int32)
    phase_one = (
        2.0
        * math.pi
        / radix_first
        * (outer[:, None] * outer[None, :] % radix_first).astype(jnp.float32)
    )
    phase_twist = 2.0 * math.pi / length * (outer[:, None] * inner[None, :]).astype(jnp.float32)
    phase_two = (
        2.0 * math.pi / second * (inner[:, None] * inner[None, :] % second).astype(jnp.float32)
    )
    cos_one, sin_one = (jnp.cos(phase_one), jnp.sin(phase_one))
    cos_twist, sin_twist = (jnp.cos(phase_twist), jnp.sin(phase_twist))
    cos_two, sin_two = (jnp.cos(phase_two), jnp.sin(phase_two))
    first_form = "fk,stkj->stfj"
    section_re = jnp.einsum(first_form, cos_one, grid[0], precision=exact_mode) + jnp.einsum(
        first_form, sin_one, grid[1], precision=exact_mode
    )
    section_im = jnp.einsum(first_form, cos_one, grid[1], precision=exact_mode) - jnp.einsum(
        first_form, sin_one, grid[0], precision=exact_mode
    )
    turned_re = section_re * cos_twist + section_im * sin_twist
    turned_im = section_im * cos_twist - section_re * sin_twist
    second_form = "gj,stfj->stgf"
    final_re = jnp.einsum(second_form, cos_two, turned_re, precision=exact_mode) + jnp.einsum(
        second_form, sin_two, turned_im, precision=exact_mode
    )
    final_im = jnp.einsum(second_form, cos_two, turned_im, precision=exact_mode) - jnp.einsum(
        second_form, sin_two, turned_re, precision=exact_mode
    )
    joined = jnp.stack([final_re, final_im]).reshape(filtered.shape)
    return joined * (1.0 / math.sqrt(length))


def correlate(full, rows_a, rows_b, flags, group_count):
    depth = full.shape[4]
    weight = jnp.tile(flags.astype(jnp.bfloat16), depth // flags.shape[0])
    left_rows = jnp.take(full, rows_a, axis=2) * weight
    right_rows = jnp.take(full, rows_b, axis=2)
    stacked_left = jnp.stack(
        [
            jnp.concatenate([left_rows[0], left_rows[1]], axis=-1),
            jnp.concatenate([left_rows[1], -left_rows[0]], axis=-1),
        ]
    )
    joined_right = jnp.concatenate([right_rows[0], right_rows[1]], axis=-1)
    result = jnp.einsum(
        "rpank,qbnk->nrpaqb", stacked_left, joined_right, preferred_element_type=jnp.float32
    )
    width = rows_a.shape[0]
    return result.reshape(group_count, 2, 2, width, 2 * width) * (1.0 / depth)


def on_device_any(voltages, taps_filter, tile_a, tile_b, tile_owner, tile_flags):
    history = taps_filter.shape[0] - 1
    length = taps_filter.shape[1]
    stations = voltages.shape[2]
    frames = voltages.shape[3] // length
    local_blocks = voltages.reshape(2, stations, frames, length)
    hop_count = -(-history // frames)
    sending = local_blocks
    extended = local_blocks
    for hop_index in range(hop_count):
        sending = from_behind(sending, "tm", 1)
        extended = jnp.concatenate([sending, extended], axis=2)
    extended = extended[:, :, extended.shape[2] - history - frames :]
    filtered = jnp.zeros((2, stations, frames, length), jnp.float32)
    for tap_index in range(history + 1):
        start = history - tap_index
        filtered = filtered + taps_filter[tap_index] * extended[
            :, :, start : start + frames
        ].astype(jnp.float32)
    spectra = fourier(filtered).astype(jnp.bfloat16)
    chan_count = lax.axis_size("chan")
    time_count = lax.axis_size("tm")
    narrow = length // (chan_count * time_count)
    outgoing = spectra.reshape(2, stations, frames, chan_count, time_count, narrow)
    outgoing = outgoing.transpose(0, 3, 4, 5, 1, 2)
    flat = outgoing.reshape(2, chan_count * time_count, narrow, stations * frames)
    moved = lax.all_to_all(flat, ("chan", "tm"), split_axis=1, concat_axis=1, tiled=True)
    moved = moved.reshape(2, chan_count, time_count, narrow, stations, frames)
    bands = narrow // AVG
    every_station = chan_count * stations
    spectra_count = time_count * frames
    arranged = moved.transpose(0, 1, 4, 3, 2, 5).reshape(
        2, 1, every_station, bands, AVG * spectra_count
    )
    full = lax.all_gather(arranged, "pol", axis=1, tiled=True)
    position = lax.axis_index("pol")
    width = tile_a.shape[1]
    capacity = CAP
    held = tile_owner == position
    listed = jnp.nonzero(held, size=capacity, fill_value=0)[0].astype(jnp.int32)
    tally = jnp.sum(held.astype(jnp.int32))
    initial = jnp.zeros((capacity, bands, 2, 2, width, 2 * width), jnp.float32)

    def fill_slot(slot, results):
        chosen_tile = listed[slot]
        return results.at[slot].set(
            correlate(
                full, tile_a[chosen_tile], tile_b[chosen_tile], tile_flags[chosen_tile], bands
            )
        )

    visibility = lax.fori_loop(0, tally, fill_slot, initial)
    return visibility


def fourier_tables(length):
    low = np.arange(RADIX)
    lane = np.arange(LANES)
    turn = 2.0 * np.pi / length * np.outer(low, lane)
    twiddle = np.stack([np.cos(turn), np.sin(turn)]).astype(np.float32)
    angle = 2.0 * np.pi / LANES * (np.outer(lane, lane) % LANES)
    cos, sin = np.cos(angle) / math.sqrt(length), np.sin(angle) / math.sqrt(length)
    matrix = np.block([[cos, sin], [-sin, cos]]).astype(np.float32)
    high = matrix.astype(jnp.bfloat16)
    rest = (matrix - high.astype(np.float32)).astype(jnp.bfloat16)
    return twiddle, np.stack([high, rest])


def butterflies(values):
    count = len(values)
    if count == 1:
        return values
    even, odd = butterflies(values[0::2]), butterflies(values[1::2])
    first, second = [], []
    for index in range(count // 2):
        (a, b), (c, d) = even[index], odd[index]
        if index == 0:
            e, f = c, d
        elif 4 * index == count:
            e, f = d, -c
        elif 8 * index == count:
            root = math.sqrt(0.5)
            e, f = (c + d) * root, (d - c) * root
        elif 8 * index == 3 * count:
            root = math.sqrt(0.5)
            e, f = (d - c) * root, -(c + d) * root
        else:
            turn = 2.0 * math.pi * index / count
            cos, sin = math.cos(turn), math.sin(turn)
            e, f = c * cos + d * sin, d * cos - c * sin
        first.append((a + e, b + f))
        second.append((a - e, b - f))
    return first + second


def channelise_kernel(frames, chunk, columns, plan, place_ref, own_ref, *refs):
    sources = refs[-6].shape[0]
    come_refs = refs[: sources - 1]
    taps_ref, twiddle_ref, matrix_ref = refs[sources - 1 : sources + 2]
    out_refs = refs[sources + 2 : -6]
    x_ref, fil_ref, zr_ref, zi_ref, w_ref, sems = refs[-6:]
    chan, tm = place_ref[0], place_ref[1]
    own_rows = pl.multiple_of((tm * (own_ref.shape[1] // (sources * ROWS)) + chunk) * ROWS, ROWS)
    copies = []
    for behind in range(sources):
        block = come_refs[behind - 1] if behind else own_ref.at[:, pl.ds(own_rows, ROWS), :]
        slot = lax.rem(tm - behind + sources, sources)
        copies.append(pltpu.make_async_copy(block, x_ref.at[slot], sems.at[behind]))
    for copy in copies:
        copy.start()
    for copy in copies:
        copy.wait()
    spectra = sources * frames
    length = taps_ref.shape[1]
    taps = taps_ref.shape[0]
    depth = RADIX * spectra
    z_refs = (zr_ref, zi_ref)

    @pl.loop(0, RADIX)
    def _(section):
        at = pl.multiple_of(section * LANES, LANES)
        weights = [taps_ref[pl.ds(m, 1), pl.ds(at, LANES)] for m in range(taps)]
        for part in range(2):
            blocks = []
            for t in range(spectra):
                lane = pl.multiple_of((t % frames) * length + section * LANES, LANES)
                blocks.append(x_ref[t // frames, part, :, pl.ds(lane, LANES)].astype(jnp.float32))
            for t in range(spectra):
                total = weights[0] * blocks[t]
                for m in range(1, min(t + 1, taps)):
                    total = total + weights[m] * blocks[t - m]
                fil_ref[section, t, part] = total

    @pl.loop(0, spectra)
    def _(t):
        for half in range(ROWS // 8):
            values = [
                tuple(fil_ref[section, t, part, pl.ds(half * 8, 8), :] for part in range(2))
                for section in range(RADIX)
            ]
            for low, (re, im) in enumerate(butterflies(values)):
                if low:
                    cos = twiddle_ref[0, pl.ds(low, 1), :]
                    sin = twiddle_ref[1, pl.ds(low, 1), :]
                    re, im = re * cos + im * sin, im * cos - re * sin
                rows = pl.ds(half * 8 * depth + low * spectra + t, 8, stride=depth)
                zr_ref[rows, :] = re
                zi_ref[rows, :] = im

    form = (((1,), (1,)), ((), ()))
    high_matrix, low_matrix = matrix_ref[0], matrix_ref[1]
    halves = depth // LANES

    @pl.loop(0, ROWS)
    def _(station):
        rows = pl.ds(pl.multiple_of(station * depth, depth), depth)
        value = jnp.concatenate([ref[rows, :] for ref in z_refs], axis=1)
        high = value.astype(jnp.bfloat16)
        rest = (value - high.astype(jnp.float32)).astype(jnp.bfloat16)
        total = lax.dot_general(high_matrix, high, form, preferred_element_type=jnp.float32)
        total += lax.dot_general(high_matrix, rest, form, preferred_element_type=jnp.float32)
        total += lax.dot_general(low_matrix, high, form, preferred_element_type=jnp.float32)
        for half in range(halves):
            for part in range(2):
                rows = pl.ds((half * 2 + part) * ROWS + station, LANES, stride=halves * 2 * ROWS)
                w_ref[rows, :] = total[
                    part * LANES : (part + 1) * LANES, half * LANES : (half + 1) * LANES
                ]

    share = w_ref.shape[0] // (columns * sources)
    band_rows = 2 * ROWS
    piece = 8 * band_rows
    for blocks, out_ref in zip(plan, out_refs):
        at = 0
        for across, along, start, stop in blocks:
            owner = lax.rem(chan + across, columns) * sources + lax.rem(tm + along, sources)
            for row in range(start * band_rows, stop * band_rows, piece):
                rows = pl.ds(pl.multiple_of(owner * share + row, piece), piece)
                out_ref[at : at + piece, :] = w_ref[rows, :].astype(jnp.bfloat16)
                at += piece


def channelise(place, chunk, voltages, come, taps_filter, tables, frames, columns, plan):
    sources = 1 + len(come)
    length = taps_filter.shape[1]
    spectra = sources * frames
    twiddle, matrix = tables
    out_rows = length // AVG * 2 * ROWS
    whole = pl.BlockSpec(memory_space=pltpu.VMEM)
    counts = [sum(stop - start for _, _, start, stop in blocks) for blocks in plan]
    flat = pl.pallas_call(
        lambda *refs: channelise_kernel(frames, chunk, columns, plan, *refs),
        out_shape=[
            jax.ShapeDtypeStruct((count * 2 * ROWS, LANES), jnp.bfloat16) for count in counts
        ],
        in_specs=[pl.BlockSpec(memory_space=pltpu.SMEM)]
        + [pl.BlockSpec(memory_space=pl.ANY)] * sources
        + [whole] * 3,
        out_specs=[whole] * len(plan),
        scratch_shapes=[
            pltpu.VMEM((sources, 2, ROWS, frames * length), jnp.bfloat16),
            pltpu.VMEM((RADIX, spectra, 2, ROWS, LANES), jnp.float32),
            pltpu.VMEM((ROWS * RADIX * spectra, LANES), jnp.float32),
            pltpu.VMEM((ROWS * RADIX * spectra, LANES), jnp.float32),
            pltpu.VMEM((out_rows, LANES), jnp.float32),
            pltpu.SemaphoreType.DMA((sources,)),
        ],
        compiler_params=pltpu.CompilerParams(vmem_limit_bytes=40 * 2**20),
        cost_estimate=pl.CostEstimate(
            flops=9 * 10**9, bytes_accessed=4 * 2**20, transcendentals=0
        ),
        name="channelise",
    )(place, voltages, *come, taps_filter, jnp.asarray(twiddle), jnp.asarray(matrix))
    return [piece.reshape(count, 2, ROWS, LANES) for piece, count in zip(flat, counts)]


def correlate_kernel(places, starts, width, place_ref, sel_ref, weight_ref, *refs):
    x_refs, (out_ref, x_all, rows_all, sems) = refs[: 2 * len(starts)], refs[-4:]
    tiles = out_ref.shape[0]
    band = pl.program_id(0)
    bands = x_all.shape[1]
    spans = [(0, 1), (1, bands)]

    def copies(span):
        first, last = spans[span]
        number = 0
        for index, (start, rows) in enumerate(zip(starts, places)):
            for side in range(2):
                x_ref = x_refs[2 * index + side]
                pol = lax.rem(place_ref[2] + side, 2)
                share = x_ref.shape[0] // len(rows)
                for block, at in enumerate(rows):
                    yield pltpu.make_async_copy(
                        x_ref.at[pl.ds(block * share + start + first, last - first)],
                        x_all.at[pol, pl.ds(first, last - first), :, pl.ds(at, ROWS), :],
                        sems.at[span, number],
                    )
                    number += 1

    @pl.when(band == 0)
    def _():
        for span in range(2):
            for copy in copies(span):
                copy.start()
        for copy in copies(0):
            copy.wait()

    @pl.when(band == 1)
    def _():
        for copy in copies(1):
            copy.wait()

    for pol in range(2):
        lanes = slice(pol * 2 * LANES, (pol + 1) * 2 * LANES)
        value = jnp.concatenate([x_all[pol, band, part] for part in range(2)], axis=1)
        picked = jnp.dot(sel_ref[...], value, preferred_element_type=jnp.float32)
        for tile in range(tiles):
            at = tile * 2 * width
            left = picked[at : at + width] * weight_ref[pl.ds(tile, 1), :]
            right = picked[at + width : at + 2 * width]
            rows_all[at : at + width, lanes] = left.astype(jnp.bfloat16)
            rows_all[at + width : at + 2 * width, lanes] = right.astype(jnp.bfloat16)
    form = (((1,), (1,)), ((), ()))
    for tile in range(tiles):
        at = tile * 2 * width
        left = jnp.concatenate(
            [rows_all[at : at + width, pol * 2 * LANES : (pol + 1) * 2 * LANES] for pol in range(2)]
        )
        at += width
        right = jnp.concatenate(
            [rows_all[at : at + width, pol * 2 * LANES : (pol + 1) * 2 * LANES] for pol in range(2)]
        )
        turned = jnp.concatenate([left[:, LANES:], -left[:, :LANES]], axis=1)
        both = jnp.concatenate([left, turned])
        result = lax.dot_general(both, right, form, preferred_element_type=jnp.float32)
        out_ref[tile, 0] = result.reshape(2, 2, width, 2 * width)


def correlate_tiles(
    place, select, weight, pieces, places, starts, width, first, count, bands, earlier
):
    tiles = weight.shape[0]
    whole = pl.BlockSpec(memory_space=pltpu.VMEM)
    more = [] if earlier is None else [earlier]
    blocks = 2 * sum(len(rows) for rows in places)
    return pl.pallas_call(
        lambda *refs: correlate_kernel(places, starts, width, *refs),
        grid=(count,),
        out_shape=jax.ShapeDtypeStruct((tiles, bands, 2, 2, width, 2 * width), jnp.float32),
        in_specs=[pl.BlockSpec(memory_space=pltpu.SMEM)]
        + [whole] * 2
        + [pl.BlockSpec(memory_space=pl.ANY)] * (len(pieces) + len(more)),
        out_specs=pl.BlockSpec(
            (tiles, 1, 2, 2, width, 2 * width), lambda g: (0, g + first, 0, 0, 0, 0)
        ),
        scratch_shapes=[
            pltpu.VMEM((2, count, 2, select.shape[1], LANES), jnp.bfloat16),
            pltpu.VMEM((tiles * 2 * width, 4 * LANES), jnp.bfloat16),
            pltpu.SemaphoreType.DMA((2, blocks)),
        ],
        input_output_aliases={3 + len(pieces): 0} if more else {},
        compiler_params=pltpu.CompilerParams(vmem_limit_bytes=32 * 2**20),
        cost_estimate=pl.CostEstimate(
            flops=13 * 10**9 * count // bands,
            bytes_accessed=42 * 2**20 * count // bands,
            transcendentals=0,
        ),
        name="correlate",
    )(place, select, weight, *pieces, *more)


def tile_tables(tile_a, tile_b, tile_owner, tile_flags, row_of):
    tiles = tile_owner.shape[0]
    held = tile_owner == lax.axis_index("pol")
    order = jnp.arange(tiles, dtype=jnp.int32)
    rank = jnp.sum((held[None, :] & (order[None, :] < order[:, None])).astype(jnp.int32), axis=1)
    slots = jnp.arange(CAP, dtype=jnp.int32)
    pick = (held[None, :] & (rank[None, :] == slots[:, None])).astype(jnp.int32)
    sides = jnp.stack([row_of(tile_a), row_of(tile_b)], axis=1) + 1
    rows = jnp.sum(pick[:, :, None, None] * sides[None], axis=1) - 1
    flags = jnp.sum(pick[:, :, None] * tile_flags[None], axis=1).astype(jnp.float32)
    return rows, flags


def on_device_chunks(voltages, taps_filter, tile_a, tile_b, tile_owner, tile_flags):
    length = taps_filter.shape[1]
    stations = voltages.shape[2]
    frames = voltages.shape[3] // length
    chan_count, time_count = lax.axis_size("chan"), lax.axis_size("tm")
    owners = chan_count * time_count
    chunk_count = stations // (time_count * ROWS)
    width = tile_a.shape[1]
    bands = length // AVG // owners
    tables = fourier_tables(length)

    chan, tm = lax.axis_index("chan"), lax.axis_index("tm")
    place = jnp.stack([chan, tm, lax.axis_index("pol")]).astype(jnp.int32)

    def row_of(station):
        column, rest = station // stations, station % stations
        block, inside = rest // (chunk_count * ROWS), rest % (chunk_count * ROWS)
        across = (chan - column) % chan_count
        behind = (tm - block) % time_count
        piece = across * time_count + behind
        return ((inside // ROWS) * owners + piece) * ROWS + inside % ROWS

    rows, flags = tile_tables(tile_a, tile_b, tile_owner, tile_flags, row_of)
    total_rows = chunk_count * owners * ROWS
    select = (rows[..., None] == jnp.arange(total_rows, dtype=jnp.int32)).astype(jnp.bfloat16)
    select = select.reshape(CAP * 2 * width, total_rows)
    depth = AVG * time_count * frames
    weight = jnp.tile(flags * (1.0 / depth), (1, 2 * AVG))

    samples = voltages.reshape(2, stations, frames * length)

    def travel(value, axes, distances):
        sizes = [lax.axis_size(axis) for axis in axes]
        pairs = []
        for index in np.ndindex(*sizes):
            target = [(i + d) % n for i, d, n in zip(index, distances, sizes)]
            pairs.append(tuple(int(np.ravel_multi_index(x, sizes)) for x in (index, target)))
        return lax.ppermute(value, axes, pairs)

    def after(values, earlier):
        return lax.optimization_barrier((list(values), list(earlier)))

    def block_for(values, chunk, distance):
        first = ((tm + distance) % time_count * chunk_count + chunk) * ROWS
        return lax.dynamic_slice(values, (0, first, 0), (2, ROWS, frames * length))

    def turn_time(blocks):
        return [travel(block, ("tm",), (d,)) for d, block in zip(distances, blocks)]

    def filtered(chunk, arrived, plan):
        arrived = [arrived[distances.index(d)] for d in range(1, time_count)]
        return channelise(
            place, chunk, samples, arrived, taps_filter, tables, frames, chan_count, plan
        )

    def across(values):
        return [travel(v, ("chan",), (1,)) for v in values]

    def columns(near, far):
        return jnp.stack([near, far])

    distances = [2, 1, 3]
    half = bands // 2
    spare = 1

    blocks = [block_for(samples, 0, d) for d in distances]
    blocks, (again,) = after(blocks, [samples])
    first = turn_time(blocks)
    blocks, held = after([block_for(again, 1, d) for d in distances], first[:-spare])
    first[:-spare] = held
    second = turn_time(blocks)

    plan = [[(x, z, 0, bands)] for x in range(2) for z in range(time_count)]
    spectra = filtered(0, first, plan)
    far, second[:1] = after(spectra[time_count:], second[:1])
    near, far = spectra[:time_count], across(far)
    mixed = [columns(near[z], far[z]) for z in range(time_count)]
    blocks, held = after([mixed[d] for d in distances], second[:-spare] + [select, weight])
    second[:-spare], (select, weight) = held[:-2], held[-2:]
    own_first = [mixed[0]] + turn_time(blocks)

    plan = [
        [(x, z, start, start + half) for z in range(time_count)]
        for start in (0, half)
        for x in range(2)
    ]
    spectra = filtered(1, second, plan)
    spectra = [v.reshape(time_count, half, 2, ROWS, LANES) for v in spectra]
    far, own_first[1:2] = after([spectra[1], spectra[3]], own_first[1:2])
    far_low, far_high = across(far)
    mixed = [columns(spectra[0][z], far_low[z]) for z in range(time_count)]
    blocks, held = after([mixed[d] for d in distances], own_first[1:-spare])
    own_first[1:-spare] = held
    own_low = [mixed[0]] + turn_time(blocks)
    mixed = [columns(spectra[2][z], far_high[z]) for z in range(time_count)]

    def with_other(values):
        values = [v.reshape((-1,) + v.shape[2:]) for v in values]
        return [side for v in values for side in (v, travel(v, ("pol",), (1,)))]

    both_first = with_other(own_first)
    blocks, held = after([mixed[d] for d in distances], own_low[1:-spare] + both_first[1::2])
    own_low[1:-spare], both_first[1::2] = held[: -time_count], held[-time_count:]
    own_high = [mixed[0]] + turn_time(blocks)

    both_low = with_other(own_low)
    places = [
        [((chunk * chan_count + x) * time_count + z) * ROWS for x in range(chan_count)]
        for chunk in range(chunk_count)
        for z in [0] + distances
    ]
    visibility = correlate_tiles(
        place, select, weight, both_first + both_low, places, [0] * 8, width,
        0, half, bands, None,
    )
    own_high, (visibility,) = after(own_high, [visibility])
    both_high = with_other(own_high)
    return correlate_tiles(
        place, select, weight, both_first + both_high, places, [half] * 4 + [0] * 4, width,
        half, half, bands, visibility,
    )


def on_device(voltages, taps_filter, tile_a, tile_b, tile_owner, tile_flags):
    taps, length = taps_filter.shape
    frames = voltages.shape[3] // length
    time_count = lax.axis_size("tm")
    fits = (
        length == RADIX * LANES
        and AVG * time_count * frames == LANES
        and 2 * tile_a.shape[1] == LANES
        and voltages.shape[2] == 2 * time_count * ROWS
        and (lax.axis_size("chan"), time_count) == (2, 4)
    )
    form = on_device_chunks if fits else on_device_any
    return form(voltages, taps_filter, tile_a, tile_b, tile_owner, tile_flags)


def solution(mesh):
    return jax.shard_map(
        on_device,
        mesh=mesh,
        in_specs=(P("grp", "pol", "chan", "tm"), P(), P(), P(), P(), P()),
        out_specs=P("pol", ("chan", "tm"), "grp", None, None, None),
        check_vma=False,
    )
```

profile of v0, /device:TPU:11, one launch (start us, length us, event | category | flops | bytes accessed | tf_op | source)
XLA Modules:
  0.0 223.7 jit_solution(9362278617384295688)
XLA Ops:
  0.0 2.3 %dynamic-slice_bitcast_fusion = (bf16[2,16,8192]{2,1,0:T(8,128)(2,1)S(1)}, bf16[2,16,8192]{2,1,0:T(8,128)(2,1)}, bf16[2,16,8192]{2,1,0:T(8,128)(2,1)S(1)}) fusion(bf16[2,1,128,8192]{3,2,1,0:T(8,128)(2,1)} %param.8, s32[]{:T(128)S(6)} %select_n.106, s32[]{:T(128)S(6)} %select_n.102, s32[]{:T(128)S(6)} %select_n.104), kind=kLoop, calls=%fused_computation.6 | loop fusion | bytes 3145740 | tf_op jit(solution)/shard_map/dynamic_slice | solution.py:454
  2.3 2.3 %collective-permute-start = (bf16[2,16,8192]{2,1,0:T(8,128)(2,1)}, bf16[2,16,8192]{2,1,0:T(8,128)(2,1)S(1)}, u32[]{:S(2)}, u32[]{:S(2)}) collective-permute-start(bf16[2,16,8192]{2,1,0:T(8,128)(2,1)} %get-tuple-element.61), channel_id=1, source_target_pairs={{0,4},{2,6},{4,0},{6,2},{1,5},{3,7},{5,1},{7,3},{8,12},{10,14},{12... | collective-permute-start | bytes 1572872 | tf_op jit(solution)/shard_map/ppermute | solution.py:447
  7.8 2.6 %constant_dynamic-slice_fusion = (bf16[2,16,8192]{2,1,0:T(8,128)(2,1)}, bf16[2,16,8192]{2,1,0:T(8,128)(2,1)}, bf16[2,16,8192]{2,1,0:T(8,128)(2,1)}) fusion(bf16[2,128,8192]{2,1,0:T(8,128)(2,1)} %bitcast.51, s32[]{:T(128)S(6)} %select_n.109, s32[]{:T(128)S(6)} %select_n.108, s32[]{:T(128)S(6)} %select_n.107), kind=kLoop, calls=%fused_computation.114 | loop fusion | bytes 3145740 | tf_op jit(solution)/shard_map/dynamic_slice | solution.py:454
  10.8 17.4 %collective-permute-done.refs_3_ = bf16[2,16,8192]{2,1,0:T(8,128)(2,1)S(1)} collective-permute-done((bf16[2,16,8192]{2,1,0:T(8,128)(2,1)}, bf16[2,16,8192]{2,1,0:T(8,128)(2,1)S(1)}, u32[]{:S(2)}, u32[]{:S(2)}) %collective-permute-start) | collective-permute-done | bytes 524320 | tf_op jit(solution)/shard_map/ppermute | solution.py:447
  28.2 21.9 %collective-permute-done.1.refs_2_ = bf16[2,16,8192]{2,1,0:T(8,128)(2,1)S(1)} collective-permute-done((bf16[2,16,8192]{2,1,0:T(8,128)(2,1)S(1)}, bf16[2,16,8192]{2,1,0:T(8,128)(2,1)S(1)}, u32[]{:S(2)}, u32[]{:S(2)}) %collective-permute-start.1) | collective-permute-done | bytes 524320 | tf_op jit(solution)/shard_map/ppermute | solution.py:447
  53.9 16.3 %channelise.2 = (bf16[1024,128]{1,0:T(8,128)(2,1)S(1)}, bf16[1024,128]{1,0:T(8,128)(2,1)S(1)}, bf16[1024,128]{1,0:T(8,128)(2,1)S(1)}, bf16[1024,128]{1,0:T(8,128...) custom-call(s32[3]{0:T(128)S(1)} %pad_add_fusion.refs_0_, ...), custom_call_target="tpu_custom_call" | custom-call | flops 8999999488 | bytes 4194304 | tf_op jit(solution)/shard_map/channelise/pallas_call | solution.py:276
  70.3 2.5 %collective-permute-done.3.refs_3_ = bf16[2,16,8192]{2,1,0:T(8,128)(2,1)S(1)} collective-permute-done((bf16[2,16,8192]{2,1,0:T(8,128)(2,1)}, bf16[2,16,8192]{2,1,0:T(8,128)(2,1)S(1)}, u32[]{:S(2)}, u32[]{:S(2)}) %collective-permute-start.3) | collective-permute-done | bytes 524320 | tf_op jit(solution)/shard_map/ppermute | solution.py:447
  73.9 2.6 %collective-permute-start.7 = (bf16[2,16,8192]{2,1,0:T(8,128)(2,1)}, bf16[2,16,8192]{2,1,0:T(8,128)(2,1)S(1)}, u32[]{:S(2)}, u32[]{:S(2)}) collective-permute-start(bf16[2,16,8192]{2,1,0:T(8,128)(2,1)} %get-tuple-element.78), channel_id=1, source_target_pairs={{0,2},{2,4},{4,6},{6,0},{1,3},{3,5},{5,7},{7,1},{8,10},{10,12},{12... | collective-permute-start | bytes 1572872 | tf_op jit(solution)/shard_map/ppermute | solution.py:447
  82.2 4.6 %collective-permute-done.5 = bf16[32,2,16,128]{3,2,1,0:T(8,128)(2,1)} collective-permute-done((bf16[32,2,16,128]{3,2,1,0:T(8,128)(2,1)}, bf16[32,2,16,128]{3,2,1,0:T(8,128)(2,1)}, u32[]{:S(2)}, u32[]{:S(2)}) %collective-permute-start.5) | collective-permute-done | bytes 262176 | tf_op jit(solution)/shard_map/ppermute | solution.py:447
  87.8 4.6 %collective-permute-done.6 = bf16[32,2,16,128]{3,2,1,0:T(8,128)(2,1)} collective-permute-done((bf16[32,2,16,128]{3,2,1,0:T(8,128)(2,1)}, bf16[32,2,16,128]{3,2,1,0:T(8,128)(2,1)}, u32[]{:S(2)}, u32[]{:S(2)}) %collective-permute-start.6) | collective-permute-done | bytes 262176 | tf_op jit(solution)/shard_map/ppermute | solution.py:447
  93.4 2.5 %collective-permute-start.10 = (bf16[2,32,2,16,128]{4,3,2,1,0:T(8,128)(2,1)S(1)}, bf16[2,32,2,16,128]{4,3,2,1,0:T(8,128)(2,1)S(1)}, u32[]{:S(2)}, u32[]{:S(2)}) collective-permute-start(bf16[2,32,2,16,128]{4,3,2,1,0:T(8,128)(2,1)S(1)} %pad_maximum_fusion), channel_id=1, source_target_pairs={{0,4},{2,6},{4,0},{6,2},{1,5},{3,7},{5,1},{7,3},{8,12},{10,14},{12... | collective-permute-start | bytes 1572872 | tf_op jit(solution)/shard_map/ppermute | solution.py:447
  97.8 2.8 %collective-permute-done.9.refs_4_ = bf16[2,16,8192]{2,1,0:T(8,128)(2,1)S(1)} collective-permute-done((bf16[2,16,8192]{2,1,0:T(8,128)(2,1)}, bf16[2,16,8192]{2,1,0:T(8,128)(2,1)S(1)}, u32[]{:S(2)}, u32[]{:S(2)}) %collective-permute-start.9) | collective-permute-done | bytes 524320 | tf_op jit(solution)/shard_map/ppermute | solution.py:447
  100.6 2.2 copy-done.1
  105.5 15.5 %channelise.3 = (bf16[2048,128]{1,0:T(8,128)(2,1)S(1)}, bf16[2048,128]{1,0:T(8,128)(2,1)S(1)}, bf16[2048,128]{1,0:T(8,128)(2,1)S(1)}, bf16[2048,128]{1,0:T(8,128)(2,1)S(1)}) custom-call(s32[3]{0:T(128)S(1)} %pad_add_fusion.refs_0_, bf16[2,128,8192]{2,1,0:T(8,128)(2,1)S(1)} %bitcast.53, bf16[2,16,8192]{2,1,0:T(8,128)(2,1)S(1)} %collective-permute-done.7.refs_2_, ...), custom_call_target="tpu_custom_call" | custom-call | flops 8999999488 | bytes 4194304 | tf_op jit(solution)/shard_map/channelise/pallas_call | solution.py:276
  121.1 13.8 %collective-permute-done.10 = bf16[2,32,2,16,128]{4,3,2,1,0:T(8,128)(2,1)S(1)} collective-permute-done((bf16[2,32,2,16,128]{4,3,2,1,0:T(8,128)(2,1)S(1)}, bf16[2,32,2,16,128]{4,3,2,1,0:T(8,128)(2,1)S(1)}, u32[]{:S(2)}, u32[]{:S(2)}) %collective-permute-start.10) | collective-permute-done | bytes 524320 | tf_op jit(solution)/shard_map/ppermute | solution.py:447
  137.4 10.4 %collective-permute-done.12 = bf16[4,16,2,16,128]{4,3,2,1,0:T(8,128)(2,1)S(1)} collective-permute-done((bf16[4,16,2,16,128]{4,3,2,1,0:T(8,128)(2,1)S(1)}, bf16[4,16,2,16,128]{4,3,2,1,0:T(8,128)(2,1)S(1)}, u32[]{:S(2)}, u32[]{:S(2)}) %collective-permute-start.12) | collective-permute-done | bytes 524320 | tf_op jit(solution)/shard_map/ppermute | solution.py:447
  148.0 2.5 %collective-permute-done.13 = bf16[2,32,2,16,128]{4,3,2,1,0:T(8,128)(2,1)S(1)} collective-permute-done((bf16[2,32,2,16,128]{4,3,2,1,0:T(8,128)(2,1)S(1)}, bf16[2,32,2,16,128]{4,3,2,1,0:T(8,128)(2,1)S(1)}, u32[]{:S(2)}, u32[]{:S(2)}) %collective-permute-start.13) | collective-permute-done | bytes 524320 | tf_op jit(solution)/shard_map/ppermute | solution.py:447
  150.4 3.1 %collective-permute-start.14 = (bf16[2,16,2,16,128]{4,3,2,1,0:T(8,128)(2,1)S(1)}, bf16[2,16,2,16,128]{4,3,2,1,0:T(8,128)(2,1)S(1)}, u32[]{:S(2)}, u32[]{:S(2)}) collective-permute-start(bf16[2,16,2,16,128]{4,3,2,1,0:T(8,128)(2,1)S(1)} %pad_maximum_fusion.7), channel_id=1, source_target_pairs={{0,4},{2,6},{4,0},{6,2},{1,5},{3,7},{5,1},{7,3},{8,12},{10,14},{12... | collective-permute-start | bytes 786440 | tf_op jit(solution)/shard_map/ppermute | solution.py:447
  154.6 4.4 %collective-permute-done.11 = bf16[4,16,2,16,128]{4,3,2,1,0:T(8,128)(2,1)S(1)} collective-permute-done((bf16[4,16,2,16,128]{4,3,2,1,0:T(8,128)(2,1)S(1)}, bf16[4,16,2,16,128]{4,3,2,1,0:T(8,128)(2,1)S(1)}, u32[]{:S(2)}, u32[]{:S(2)}) %collective-permute-start.11) | collective-permute-done | bytes 524320 | tf_op jit(solution)/shard_map/ppermute | solution.py:447
  162.1 2.7 %collective-permute-done.14 = bf16[2,16,2,16,128]{4,3,2,1,0:T(8,128)(2,1)S(1)} collective-permute-done((bf16[2,16,2,16,128]{4,3,2,1,0:T(8,128)(2,1)S(1)}, bf16[2,16,2,16,128]{4,3,2,1,0:T(8,128)(2,1)S(1)}, u32[]{:S(2)}, u32[]{:S(2)}) %collective-permute-start.14) | collective-permute-done | bytes 262176 | tf_op jit(solution)/shard_map/ppermute | solution.py:447
  165.4 11.8 %collective-permute-done.27 = bf16[2,16,2,16,128]{4,3,2,1,0:T(8,128)(2,1)S(1)} collective-permute-done((bf16[2,16,2,16,128]{4,3,2,1,0:T(8,128)(2,1)S(1)}, bf16[2,16,2,16,128]{4,3,2,1,0:T(8,128)(2,1)S(1)}, u32[]{:S(2)}, u32[]{:S(2)}) %collective-permute-start.27) | collective-permute-done | bytes 262176 | tf_op jit(solution)/shard_map/ppermute | solution.py:447
  181.3 16.6 %correlate.2.refs_19_ = f32[8,32,2,2,64,128]{5,4,3,2,1,0:T(8,128)} custom-call(s32[3]{0:T(128)S(1)} %pad_add_fusion.refs_0_, bf16[1024,256]{1,0:T(8,128)(2,1)S(1)} %fusion.refs_1_, f32[8,256]{1,0:T(8,128)S(1)} %tile.10.refs_2_, bf16[64,2,16,128]{3,2,1,0:T(8,128)(2,1)S(1)} %bitcast.49, bf16[64,2,16,128]{3,2,1,0:T(8,128)(2,1)S(1)} %collective-permute-done.16.refs_4_, ...), custom_call_target="tpu_custom_call" | custom-call | flops 6499999744 | bytes 22020096 | tf_op jit(solution)/shard_map/correlate/pallas_call | solution.py:371
  197.9 4.8 %collective-permute-done.22 = bf16[2,16,2,16,128]{4,3,2,1,0:T(8,128)(2,1)S(1)} collective-permute-done((bf16[2,16,2,16,128]{4,3,2,1,0:T(8,128)(2,1)S(1)}, bf16[2,16,2,16,128]{4,3,2,1,0:T(8,128)(2,1)S(1)}, u32[]{:S(2)}, u32[]{:S(2)}) %collective-permute-start.22) | collective-permute-done | bytes 262176 | tf_op jit(solution)/shard_map/ppermute | solution.py:447
  207.1 16.6 %correlate.3 = f32[8,32,2,2,64,128]{5,4,3,2,1,0:T(8,128)} custom-call(s32[3]{0:T(128)S(1)} %pad_add_fusion.refs_0_, bf16[1024,256]{1,0:T(8,128)(2,1)S(1)} %fusion.refs_1_, f32[8,256]{1,0:T(8,128)S(1)} %tile.10.refs_2_, bf16[64,2,16,128]{3,2,1,0:T(8,128)(2,1)S(1)} %bitcast.50, ...), custom_call_target="tpu_custom_call", output_to_operand_aliasing={{}: (19, {})} | custom-call | flops 6499999744 | bytes 22020096 | tf_op jit(solution)/shard_map/correlate/pallas_call | solution.py:371
  (100 shorter events, 36.8 us)
Async XLA Ops:
  2.3 25.9 %collective-permute-start = (bf16[2,16,8192]{2,1,0:T(8,128)(2,1)}, bf16[2,16,8192]{2,1,0:T(8,128)(2,1)S(1)}, u32[]{:S(2)}, u32[]{:S(2)}) collective-permute-start(bf16[2,16,8192]{2,1,0:T(8,128)(2,1)} %get-tuple-element.61), channel_id=1, source_target_pairs={{0,4},{2,6},{4,0},{6,2},{1,5},{3,7},{5,1},{7,3},{8,12},{10,14},{12... | collective-permute-start | bytes 1572872 | tf_op jit(solution)/shard_map/ppermute | solution.py:447
  4.6 45.4 %collective-permute-start.1 = (bf16[2,16,8192]{2,1,0:T(8,128)(2,1)S(1)}, bf16[2,16,8192]{2,1,0:T(8,128)(2,1)S(1)}, u32[]{:S(2)}, u32[]{:S(2)}) collective-permute-start(bf16[2,16,8192]{2,1,0:T(8,128)(2,1)S(1)} %get-tuple-element.62), channel_id=1, source_target_pairs={{0,2},{2,4},{4,6},{6,0},{1,3},{3,5},{5,7},{7,1},{8,10},{10,12},{12... | collective-permute-start | bytes 1572872 | tf_op jit(solution)/shard_map/ppermute | solution.py:447
  4.6 45.5 %collective-permute-start.2 = (bf16[2,16,8192]{2,1,0:T(8,128)(2,1)S(1)}, bf16[2,16,8192]{2,1,0:T(8,128)(2,1)S(1)}, u32[]{:S(2)}, u32[]{:S(2)}) collective-permute-start(bf16[2,16,8192]{2,1,0:T(8,128)(2,1)S(1)} %get-tuple-element.65), channel_id=1, source_target_pairs={{0,6},{2,0},{4,2},{6,4},{1,7},{3,1},{5,3},{7,5},{8,14},{10,8},{12,... | collective-permute-start | bytes 1572872 | tf_op jit(solution)/shard_map/ppermute | solution.py:447
  50.0 22.7 %collective-permute-start.3 = (bf16[2,16,8192]{2,1,0:T(8,128)(2,1)}, bf16[2,16,8192]{2,1,0:T(8,128)(2,1)S(1)}, u32[]{:S(2)}, u32[]{:S(2)}) collective-permute-start(bf16[2,16,8192]{2,1,0:T(8,128)(2,1)} %get-tuple-element.71), channel_id=1, source_target_pairs={{0,4},{2,6},{4,0},{6,2},{1,5},{3,7},{5,1},{7,3},{8,12},{10,14},{12... | collective-permute-start | bytes 1572872 | tf_op jit(solution)/shard_map/ppermute | solution.py:447
  73.9 19.6 %collective-permute-start.7 = (bf16[2,16,8192]{2,1,0:T(8,128)(2,1)}, bf16[2,16,8192]{2,1,0:T(8,128)(2,1)S(1)}, u32[]{:S(2)}, u32[]{:S(2)}) collective-permute-start(bf16[2,16,8192]{2,1,0:T(8,128)(2,1)} %get-tuple-element.78), channel_id=1, source_target_pairs={{0,2},{2,4},{4,6},{6,0},{1,3},{3,5},{5,7},{7,1},{8,10},{10,12},{12... | collective-permute-start | bytes 1572872 | tf_op jit(solution)/shard_map/ppermute | solution.py:447
  76.5 24.1 %collective-permute-start.9 = (bf16[2,16,8192]{2,1,0:T(8,128)(2,1)}, bf16[2,16,8192]{2,1,0:T(8,128)(2,1)S(1)}, u32[]{:S(2)}, u32[]{:S(2)}) collective-permute-start(bf16[2,16,8192]{2,1,0:T(8,128)(2,1)} %get-tuple-element.85), channel_id=1, source_target_pairs={{0,6},{2,0},{4,2},{6,4},{1,7},{3,1},{5,3},{7,5},{8,14},{10,8},{12,... | collective-permute-start | bytes 1572872 | tf_op jit(solution)/shard_map/ppermute | solution.py:447
  79.6 12.9 %collective-permute-start.6 = (bf16[32,2,16,128]{3,2,1,0:T(8,128)(2,1)}, bf16[32,2,16,128]{3,2,1,0:T(8,128)(2,1)}, u32[]{:S(2)}, u32[]{:S(2)}) collective-permute-start(bf16[32,2,16,128]{3,2,1,0:T(8,128)(2,1)} %bitcast.11), channel_id=1, source_target_pairs={{0,8},{8,0},{1,9},{9,1},{2,10},{10,2},{3,11},{11,3},{4,12},{12,4},... | collective-permute-start | bytes 786440 | tf_op jit(solution)/shard_map/ppermute | solution.py:447
  80.6 55.4 %collective-permute-start.8 = (bf16[32,2,16,128]{3,2,1,0:T(8,128)(2,1)S(1)}, bf16[32,2,16,128]{3,2,1,0:T(8,128)(2,1)S(1)}, u32[]{:S(2)}, u32[]{:S(2)}) collective-permute-start(bf16[32,2,16,128]{3,2,1,0:T(8,128)(2,1)S(1)} %bitcast.85), channel_id=1, source_target_pairs={{0,8},{8,0},{1,9},{9,1},{2,10},{10,2},{3,11},{11,3},{4,12},{12,4},... | collective-permute-start | bytes 786440 | tf_op jit(solution)/shard_map/ppermute | solution.py:447
  93.4 41.4 %collective-permute-start.10 = (bf16[2,32,2,16,128]{4,3,2,1,0:T(8,128)(2,1)S(1)}, bf16[2,32,2,16,128]{4,3,2,1,0:T(8,128)(2,1)S(1)}, u32[]{:S(2)}, u32[]{:S(2)}) collective-permute-start(bf16[2,32,2,16,128]{4,3,2,1,0:T(8,128)(2,1)S(1)} %pad_maximum_fusion), channel_id=1, source_target_pairs={{0,4},{2,6},{4,0},{6,2},{1,5},{3,7},{5,1},{7,3},{8,12},{10,14},{12... | collective-permute-start | bytes 1572872 | tf_op jit(solution)/shard_map/ppermute | solution.py:447
  95.9 41.1 %collective-permute-start.19 = (bf16[2,32,2,16,128]{4,3,2,1,0:T(8,128)(2,1)S(1)}, bf16[2,32,2,16,128]{4,3,2,1,0:T(8,128)(2,1)S(1)}, u32[]{:S(2)}, u32[]{:S(2)}) collective-permute-start(bf16[2,32,2,16,128]{4,3,2,1,0:T(8,128)(2,1)S(1)} %pad_maximum_fusion.2), channel_id=1, source_target_pairs={{0,6},{2,0},{4,2},{6,4},{1,7},{3,1},{5,3},{7,5},{8,14},{10,8},{12,... | collective-permute-start | bytes 1572872 | tf_op jit(solution)/shard_map/ppermute | solution.py:447
  134.8 13.0 %collective-permute-start.12 = (bf16[4,16,2,16,128]{4,3,2,1,0:T(8,128)(2,1)S(1)}, bf16[4,16,2,16,128]{4,3,2,1,0:T(8,128)(2,1)S(1)}, u32[]{:S(2)}, u32[]{:S(2)}) collective-permute-start(bf16[4,16,2,16,128]{4,3,2,1,0:T(8,128)(2,1)S(1)} %bitcast.84), channel_id=1, source_target_pairs={{0,8},{8,0},{1,9},{9,1},{2,10},{10,2},{3,11},{11,3},{4,12},{12,4},... | collective-permute-start | bytes 1572872 | tf_op jit(solution)/shard_map/ppermute | solution.py:447
  136.1 24.4 %collective-permute-start.16 = (bf16[64,2,16,128]{3,2,1,0:T(8,128)(2,1)S(1)}, bf16[64,2,16,128]{3,2,1,0:T(8,128)(2,1)S(1)}, u32[]{:S(2)}, u32[]{:S(2)}) collective-permute-start(bf16[64,2,16,128]{3,2,1,0:T(8,128)(2,1)S(1)} %bitcast.48), channel_id=1, source_target_pairs={{0,1},{1,0},{2,3},{3,2},{4,5},{5,4},{6,7},{7,6},{8,9},{9,8},{10,11... | collective-permute-start | bytes 1572872 | tf_op jit(solution)/shard_map/ppermute | solution.py:447
  136.9 13.5 %collective-permute-start.13 = (bf16[2,32,2,16,128]{4,3,2,1,0:T(8,128)(2,1)S(1)}, bf16[2,32,2,16,128]{4,3,2,1,0:T(8,128)(2,1)S(1)}, u32[]{:S(2)}, u32[]{:S(2)}) collective-permute-start(bf16[2,32,2,16,128]{4,3,2,1,0:T(8,128)(2,1)S(1)} %pad_maximum_fusion.1), channel_id=1, source_target_pairs={{0,2},{2,4},{4,6},{6,0},{1,3},{3,5},{5,7},{7,1},{8,10},{10,12},{12... | collective-permute-start | bytes 1572872 | tf_op jit(solution)/shard_map/ppermute | solution.py:447
  137.0 23.5 %collective-permute-start.20 = (bf16[64,2,16,128]{3,2,1,0:T(8,128)(2,1)S(1)}, bf16[64,2,16,128]{3,2,1,0:T(8,128)(2,1)S(1)}, u32[]{:S(2)}, u32[]{:S(2)}) collective-permute-start(bf16[64,2,16,128]{3,2,1,0:T(8,128)(2,1)S(1)} %bitcast.57), channel_id=1, source_target_pairs={{0,1},{1,0},{2,3},{3,2},{4,5},{5,4},{6,7},{7,6},{8,9},{9,8},{10,11... | collective-permute-start | bytes 1572872 | tf_op jit(solution)/shard_map/ppermute | solution.py:447
  137.2 21.9 %collective-permute-start.11 = (bf16[4,16,2,16,128]{4,3,2,1,0:T(8,128)(2,1)S(1)}, bf16[4,16,2,16,128]{4,3,2,1,0:T(8,128)(2,1)S(1)}, u32[]{:S(2)}, u32[]{:S(2)}) collective-permute-start(bf16[4,16,2,16,128]{4,3,2,1,0:T(8,128)(2,1)S(1)} %bitcast.83), channel_id=1, source_target_pairs={{0,8},{8,0},{1,9},{9,1},{2,10},{10,2},{3,11},{11,3},{4,12},{12,4},... | collective-permute-start | bytes 1572872 | tf_op jit(solution)/shard_map/ppermute | solution.py:447
  150.4 14.4 %collective-permute-start.14 = (bf16[2,16,2,16,128]{4,3,2,1,0:T(8,128)(2,1)S(1)}, bf16[2,16,2,16,128]{4,3,2,1,0:T(8,128)(2,1)S(1)}, u32[]{:S(2)}, u32[]{:S(2)}) collective-permute-start(bf16[2,16,2,16,128]{4,3,2,1,0:T(8,128)(2,1)S(1)} %pad_maximum_fusion.7), channel_id=1, source_target_pairs={{0,4},{2,6},{4,0},{6,2},{1,5},{3,7},{5,1},{7,3},{8,12},{10,14},{12... | collective-permute-start | bytes 786440 | tf_op jit(solution)/shard_map/ppermute | solution.py:447
  153.5 24.2 %collective-permute-start.17 = (bf16[64,2,16,128]{3,2,1,0:T(8,128)(2,1)S(1)}, bf16[64,2,16,128]{3,2,1,0:T(8,128)(2,1)S(1)}, u32[]{:S(2)}, u32[]{:S(2)}) collective-permute-start(bf16[64,2,16,128]{3,2,1,0:T(8,128)(2,1)S(1)} %bitcast.54), channel_id=1, source_target_pairs={{0,1},{1,0},{2,3},{3,2},{4,5},{5,4},{6,7},{7,6},{8,9},{9,8},{10,11... | collective-permute-start | bytes 1572872 | tf_op jit(solution)/shard_map/ppermute | solution.py:447
  159.0 18.6 %collective-permute-start.18 = (bf16[64,2,16,128]{3,2,1,0:T(8,128)(2,1)S(1)}, bf16[64,2,16,128]{3,2,1,0:T(8,128)(2,1)S(1)}, u32[]{:S(2)}, u32[]{:S(2)}) collective-permute-start(bf16[64,2,16,128]{3,2,1,0:T(8,128)(2,1)S(1)} %bitcast.60), channel_id=1, source_target_pairs={{0,1},{1,0},{2,3},{3,2},{4,5},{5,4},{6,7},{7,6},{8,9},{9,8},{10,11... | collective-permute-start | bytes 1572872 | tf_op jit(solution)/shard_map/ppermute | solution.py:447
  160.5 17.2 %collective-permute-start.15 = (bf16[2,16,2,16,128]{4,3,2,1,0:T(8,128)(2,1)S(1)}, bf16[2,16,2,16,128]{4,3,2,1,0:T(8,128)(2,1)S(1)}, u32[]{:S(2)}, u32[]{:S(2)}) collective-permute-start(bf16[2,16,2,16,128]{4,3,2,1,0:T(8,128)(2,1)S(1)} %pad_maximum_fusion.8), channel_id=1, source_target_pairs={{0,2},{2,4},{4,6},{6,0},{1,3},{3,5},{5,7},{7,1},{8,10},{10,12},{12... | collective-permute-start | bytes 786440 | tf_op jit(solution)/shard_map/ppermute | solution.py:447
  160.5 16.6 %collective-permute-start.27 = (bf16[2,16,2,16,128]{4,3,2,1,0:T(8,128)(2,1)S(1)}, bf16[2,16,2,16,128]{4,3,2,1,0:T(8,128)(2,1)S(1)}, u32[]{:S(2)}, u32[]{:S(2)}) collective-permute-start(bf16[2,16,2,16,128]{4,3,2,1,0:T(8,128)(2,1)S(1)} %pad_maximum_fusion.9), channel_id=1, source_target_pairs={{0,6},{2,0},{4,2},{6,4},{1,7},{3,1},{5,3},{7,5},{8,14},{10,8},{12,... | collective-permute-start | bytes 786440 | tf_op jit(solution)/shard_map/ppermute | solution.py:447
  164.8 15.0 %collective-permute-start.24 = (bf16[32,2,16,128]{3,2,1,0:T(8,128)(2,1)S(1)}, bf16[32,2,16,128]{3,2,1,0:T(8,128)(2,1)S(1)}, u32[]{:S(2)}, u32[]{:S(2)}) collective-permute-start(bf16[32,2,16,128]{3,2,1,0:T(8,128)(2,1)S(1)} %bitcast.65), channel_id=1, source_target_pairs={{0,1},{1,0},{2,3},{3,2},{4,5},{5,4},{6,7},{7,6},{8,9},{9,8},{10,11... | collective-permute-start | bytes 786440 | tf_op jit(solution)/shard_map/ppermute | solution.py:447
  178.3 19.6 %collective-permute-start.21 = (bf16[2,16,2,16,128]{4,3,2,1,0:T(8,128)(2,1)S(1)}, bf16[2,16,2,16,128]{4,3,2,1,0:T(8,128)(2,1)S(1)}, u32[]{:S(2)}, u32[]{:S(2)}) collective-permute-start(bf16[2,16,2,16,128]{4,3,2,1,0:T(8,128)(2,1)S(1)} %pad_maximum_fusion.4), channel_id=1, source_target_pairs={{0,4},{2,6},{4,0},{6,2},{1,5},{3,7},{5,1},{7,3},{8,12},{10,14},{12... | collective-permute-start | bytes 786440 | tf_op jit(solution)/shard_map/ppermute | solution.py:447
  179.8 22.9 %collective-permute-start.22 = (bf16[2,16,2,16,128]{4,3,2,1,0:T(8,128)(2,1)S(1)}, bf16[2,16,2,16,128]{4,3,2,1,0:T(8,128)(2,1)S(1)}, u32[]{:S(2)}, u32[]{:S(2)}) collective-permute-start(bf16[2,16,2,16,128]{4,3,2,1,0:T(8,128)(2,1)S(1)} %pad_maximum_fusion.5), channel_id=1, source_target_pairs={{0,2},{2,4},{4,6},{6,0},{1,3},{3,5},{5,7},{7,1},{8,10},{10,12},{12... | collective-permute-start | bytes 786440 | tf_op jit(solution)/shard_map/ppermute | solution.py:447
  180.7 23.6 %collective-permute-start.23 = (bf16[2,16,2,16,128]{4,3,2,1,0:T(8,128)(2,1)S(1)}, bf16[2,16,2,16,128]{4,3,2,1,0:T(8,128)(2,1)S(1)}, u32[]{:S(2)}, u32[]{:S(2)}) collective-permute-start(bf16[2,16,2,16,128]{4,3,2,1,0:T(8,128)(2,1)S(1)} %pad_maximum_fusion.6), channel_id=1, source_target_pairs={{0,6},{2,0},{4,2},{6,4},{1,7},{3,1},{5,3},{7,5},{8,14},{10,8},{12,... | collective-permute-start | bytes 786440 | tf_op jit(solution)/shard_map/ppermute | solution.py:447
  (19 other events, 112.6 us)
where the time goes:
time: 224 us
  waiting for transfers between devices  108 us (48%)
  Pallas kernels  65.1 us (29%)
  starting transfers between devices  30.2 us (13%)
  local copies, waits for them, and re-layouts  14.7 us (7%)
  other arithmetic  5.36 us (2%)
    ppermute x33, waiting for transfers between devices, travel(): return lax.ppermute(value, axes, pairs)  108 us
    pallas_call x2, Pallas kernels, correlate_tiles(): pl.pallas_call(lambda *refs: correlate_kernel(places, starts, width, *ref...  33.2 us
    pallas_call x2, Pallas kernels, channelise(): pl.pallas_call(lambda *refs: channelise_kernel(frames, chunk, columns, pl...  31.9 us
    ppermute x33, starting transfers between devices, travel(): return lax.ppermute(value, axes, pairs)  30.2 us
    unnamed x20, local copies, waits for them, and re-layouts  9.54 us
    dynamic_slice x2, local copies, waits for them, and re-layouts, block_for(): return lax.dynamic_slice(values, (0, first, 0), (2, ROWS, frames * length))  4.85 us
  transfers between devices with their start and end apart: 33, of which 19 were waited for; matrix products, arithmetic and copies ran while one was open for 4% of the time, Pallas kernels for 22%

commit v1 on v0

--- a/solution.py
+++ b/solution.py
@@ -254,7 +254,7 @@
 
     share = w_ref.shape[0] // (columns * sources)
     band_rows = 2 * ROWS
-    piece = 8 * band_rows
+    piece = 4 * band_rows
     for blocks, out_ref in zip(plan, out_refs):
         at = 0
         for across, along, start, stop in blocks:
@@ -453,7 +453,7 @@
         first = ((tm + distance) % time_count * chunk_count + chunk) * ROWS
         return lax.dynamic_slice(values, (0, first, 0), (2, ROWS, frames * length))
 
-    def turn_time(blocks):
+    def turn_time(blocks, distances):
         return [travel(block, ("tm",), (d,)) for d, block in zip(distances, blocks)]
 
     def filtered(chunk, arrived, plan):
@@ -465,69 +465,92 @@
     def across(values):
         return [travel(v, ("chan",), (1,)) for v in values]
 
-    def columns(near, far):
-        return jnp.stack([near, far])
-
     distances = [2, 1, 3]
-    half = bands // 2
     spare = 1
-
-    blocks = [block_for(samples, 0, d) for d in distances]
-    blocks, (again,) = after(blocks, [samples])
-    first = turn_time(blocks)
-    blocks, held = after([block_for(again, 1, d) for d in distances], first[:-spare])
+    cuts = [0, bands * 3 // 8, bands * 3 // 4, bands]
+    spans = list(zip(cuts[:-1], cuts[1:]))
+
+    head, (again,) = after([block_for(samples, 0, distances[0])], [samples])
+    first = turn_time(head, distances[:1])
+    blocks, (again,) = after([block_for(again, 0, d) for d in distances[1:]], [again])
+    first += turn_time(blocks, distances[1:])
+    blocks, held = after([block_for(again, 1, d) for d in distances[1:]], first[:-spare])
     first[:-spare] = held
-    second = turn_time(blocks)
-
-    plan = [[(x, z, 0, bands)] for x in range(2) for z in range(time_count)]
-    spectra = filtered(0, first, plan)
-    far, second[:1] = after(spectra[time_count:], second[:1])
-    near, far = spectra[:time_count], across(far)
-    mixed = [columns(near[z], far[z]) for z in range(time_count)]
-    blocks, held = after([mixed[d] for d in distances], second[:-spare] + [select, weight])
-    second[:-spare], (select, weight) = held[:-2], held[-2:]
-    own_first = [mixed[0]] + turn_time(blocks)
-
-    plan = [
-        [(x, z, start, start + half) for z in range(time_count)]
-        for start in (0, half)
-        for x in range(2)
+    second = turn_time(blocks, distances[1:])
+    blocks, held = after([block_for(again, 1, distances[0])], second[:1])
+    second[:1] = held
+    second = turn_time(blocks, distances[:1]) + second
+
+    def parts_of(spans):
+        return [
+            [(x, z, *span) for z in [0] + distances] for span in spans for x in range(chan_count)
+        ]
+
+    def columns(spans, near, far):
+        mixed = []
+        for (start, stop), near_part, far_part in zip(spans, near, far):
+            shape = (time_count, stop - start, 2, ROWS, LANES)
+            near_part, far_part = near_part.reshape(shape), far_part.reshape(shape)
+            mixed.append([jnp.stack([near_part[z], far_part[z]]) for z in range(time_count)])
+        return mixed
+
+    def part_of(value, group, span):
+        value = value.reshape((time_count, group[1] - group[0]) + value.shape[1:])
+        return value[:, span[0] - group[0] : span[1] - group[0]]
+
+    whole = [(0, bands)]
+    spectra = filtered(0, first, parts_of(whole))
+    far, second[1:] = after(spectra[1::2], second[1:])
+    (mixed,) = columns(whole, spectra[0::2], across(far))
+    blocks, held = after(mixed[1:], second[:1] + [select, weight])
+    second[:1], (select, weight) = held[:1], held[1:]
+    moved = turn_time(blocks, distances)
+
+    groups = [spans[0], (spans[0][1], bands)]
+    spectra = filtered(1, second, parts_of(groups))
+    far, moved[:1] = after(spectra[1::2], moved[:1])
+    early = [mixed[0]] + moved
+    far = across(far)
+    near = [part_of(spectra[0], groups[0], spans[0])]
+    near += [part_of(spectra[2], groups[1], span) for span in spans[1:]]
+    far = [part_of(far[0], groups[0], spans[0])] + [
+        part_of(far[1], groups[1], span) for span in spans[1:]
     ]
-    spectra = filtered(1, second, plan)
-    spectra = [v.reshape(time_count, half, 2, ROWS, LANES) for v in spectra]
-    far, own_first[1:2] = after([spectra[1], spectra[3]], own_first[1:2])
-    far_low, far_high = across(far)
-    mixed = [columns(spectra[0][z], far_low[z]) for z in range(time_count)]
-    blocks, held = after([mixed[d] for d in distances], own_first[1:-spare])
-    own_first[1:-spare] = held
-    own_low = [mixed[0]] + turn_time(blocks)
-    mixed = [columns(spectra[2][z], far_high[z]) for z in range(time_count)]
+    mixed = columns(spans, near, far)
 
     def with_other(values):
-        values = [v.reshape((-1,) + v.shape[2:]) for v in values]
+        values = [v.reshape((-1,) + v.shape[-3:]) for v in values]
         return [side for v in values for side in (v, travel(v, ("pol",), (1,)))]
 
-    both_first = with_other(own_first)
-    blocks, held = after([mixed[d] for d in distances], own_low[1:-spare] + both_first[1::2])
-    own_low[1:-spare], both_first[1::2] = held[: -time_count], held[-time_count:]
-    own_high = [mixed[0]] + turn_time(blocks)
-
-    both_low = with_other(own_low)
-    places = [
-        [((chunk * chan_count + x) * time_count + z) * ROWS for x in range(chan_count)]
-        for chunk in range(chunk_count)
-        for z in [0] + distances
-    ]
-    visibility = correlate_tiles(
-        place, select, weight, both_first + both_low, places, [0] * 8, width,
-        0, half, bands, None,
-    )
-    own_high, (visibility,) = after(own_high, [visibility])
-    both_high = with_other(own_high)
-    return correlate_tiles(
-        place, select, weight, both_first + both_high, places, [half] * 4 + [0] * 4, width,
-        half, half, bands, visibility,
-    )
+    def row(chunk, x, z):
+        return ((chunk * chan_count + x) * time_count + z) * ROWS
+
+    blocks, held = after(mixed[0][1:], early[1:-spare])
+    early[1:-spare] = held
+    late = [[mixed[0][0]] + turn_time(blocks, distances)]
+    early = with_other([jnp.stack(early)])
+    order = [0] + distances
+    early_places = [[row(0, x, z) for z in order for x in range(chan_count)]]
+    late_places = [[row(1, x, z) for x in range(chan_count)] for z in order]
+
+    visibility = None
+    for number, (start, stop) in enumerate(spans):
+        pieces, places = late[number], late_places
+        if visibility is not None:
+            pieces, (visibility,) = after(pieces, [visibility])
+        if number + 1 < len(spans):
+            held = pieces[1:-spare] + (early[1:] if number == 0 else [])
+            blocks, held = after(mixed[number + 1][1:], held)
+            pieces[1:-spare] = held[: time_count - 1 - spare]
+            if number == 0:
+                early[1:] = held[time_count - 1 - spare :]
+            late.append([mixed[number + 1][0]] + turn_time(blocks, distances))
+            pieces, places = [jnp.stack(pieces)], [sum(late_places, [])]
+        visibility = correlate_tiles(
+            place, select, weight, early + with_other(pieces), early_places + places,
+            [start] + [0] * len(places), width, start, stop - start, bands, visibility,
+        )
+    return visibility
 
 
 def on_device(voltages, taps_filter, tile_a, tile_b, tile_owner, tile_flags):

time: 224 us -> 234 us (1.045); the launches traced: 224 us -> 229 us
  starting transfers between devices: 30.2 us -> 36.6 us
    ppermute x33 -> x28, starting transfers between devices: 30.2 us -> 36.6 us  [travel(): return lax.ppermute(value, axes, pairs)]
    unnamed x20 -> x28, local copies, waits for them, and re-layouts: 9.54 us -> 6.38 us
    another operation x12 -> x18, other arithmetic: 3.26 us -> 0.89 us  [the longest x13 0.36 us: columns(): jnp.stack([near_part[z], far_part[z]])]
    pallas_call x2 -> x3, Pallas kernels: 33.2 us -> 35.1 us  [correlate_tiles(): pl.pallas_call(lambda *refs: correlate_kernel(places, starts, width, *ref...]
    ppermute x33 -> x28, waiting for transfers between devices: 108 us -> 109 us  [travel(): return lax.ppermute(value, axes, pairs)]
    dynamic_slice x2 -> x3, local copies, waits for them, and re-layouts: 4.85 us -> 4.64 us  [block_for(): return lax.dynamic_slice(values, (0, first, 0), (2, ROWS, frames * length))]
  transfers between devices with their start and end apart: 33 -> 28, of which waited for: 19 -> 18; matrix products, arithmetic and copies ran while one was open for 4% -> 4% of each run, Pallas kernels for 22% -> 25%
where the time goes in v1:
time: 234 us; the launch traced here: 229 us
  waiting for transfers between devices  109 us (47%)
  Pallas kernels  66.2 us (28%)
  starting transfers between devices  36.6 us (16%)
  local copies, waits for them, and re-layouts  13.5 us (6%)
  other arithmetic  3.03 us (1%)
    ppermute x28, waiting for transfers between devices, travel(): return lax.ppermute(value, axes, pairs)  109 us
    ppermute x28, starting transfers between devices, travel(): return lax.ppermute(value, axes, pairs)  36.6 us
    pallas_call x3, Pallas kernels, correlate_tiles(): pl.pallas_call(lambda *refs: correlate_kernel(places, starts, width, *ref...  35.1 us
    pallas_call x2, Pallas kernels, channelise(): pl.pallas_call(lambda *refs: channelise_kernel(frames, chunk, columns, pl...  31.1 us
    unnamed x28, local copies, waits for them, and re-layouts  6.38 us
  transfers between devices with their start and end apart: 28, of which 18 were waited for; matrix products, arithmetic and copies ran while one was open for 4% of the time, Pallas kernels for 25%

profile of v1, /device:TPU:11, one launch (start us, length us, event | category | flops | bytes accessed | tf_op | source)
XLA Modules:
  0.0 229.1 jit_solution(2003423490158647493)
XLA Ops:
  1.1 2.4 %collective-permute-start = (bf16[2,16,8192]{2,1,0:T(8,128)(2,1)S(1)}, bf16[2,16,8192]{2,1,0:T(8,128)(2,1)S(1)}, u32[]{:S(2)}, u32[]{:S(2)}) collective-permute-start(bf16[2,16,8192]{2,1,0:T(8,128)(2,1)S(1)} %dynamic-slice_bitcast_fusion), channel_id=1, source_target_pairs={{0,4},{2,6},{4,0},{6,2},{1,5},{3,7},{5,1},{7,3},{8,12},{10,14},{12... | collective-permute-start | bytes 1572872 | tf_op jit(solution)/shard_map/ppermute | solution.py:447
  4.8 1.5 collective-permute-start.2
  7.7 2.3 constant_dynamic-slice_fusion
  10.4 16.5 %collective-permute-done.refs_3_ = bf16[2,16,8192]{2,1,0:T(8,128)(2,1)S(1)} collective-permute-done((bf16[2,16,8192]{2,1,0:T(8,128)(2,1)S(1)}, bf16[2,16,8192]{2,1,0:T(8,128)(2,1)S(1)}, u32[]{:S(2)}, u32[]{:S(2)}) %collective-permute-start) | collective-permute-done | bytes 524320 | tf_op jit(solution)/shard_map/ppermute | solution.py:447
  26.8 21.9 %collective-permute-done.1.refs_2_ = bf16[2,16,8192]{2,1,0:T(8,128)(2,1)S(1)} collective-permute-done((bf16[2,16,8192]{2,1,0:T(8,128)(2,1)S(1)}, bf16[2,16,8192]{2,1,0:T(8,128)(2,1)S(1)}, u32[]{:S(2)}, u32[]{:S(2)}) %collective-permute-start.1) | collective-permute-done | bytes 524320 | tf_op jit(solution)/shard_map/ppermute | solution.py:447
  48.8 2.2 collective-permute-start.3
  51.0 7.9 %collective-permute-done.2.refs_4_ = bf16[2,16,8192]{2,1,0:T(8,128)(2,1)S(1)} collective-permute-done((bf16[2,16,8192]{2,1,0:T(8,128)(2,1)S(1)}, bf16[2,16,8192]{2,1,0:T(8,128)(2,1)S(1)}, u32[]{:S(2)}, u32[]{:S(2)}) %collective-permute-start.2) | collective-permute-done | bytes 524320 | tf_op jit(solution)/shard_map/ppermute | solution.py:447
  59.6 2.2 copy-done
  63.6 15.6 %channelise.2 = (bf16[4096,128]{1,0:T(8,128)(2,1)S(1)}, bf16[4096,128]{1,0:T(8,128)(2,1)S(1)}) custom-call(s32[3]{0:T(128)S(1)} %pad_add_fusion.refs_0_, bf16[2,128,8192]{2,1,0:T(8,128)(2,1)S(1)} %bitcast.70, bf16[2,16,8192]{2,1,0:T(8,128)(2,1)S(1)} %collective-permute-done.1.refs_2_, bf16[2,16,8192]{2,1,0:T(8,128)(2,1)S(1)} %collective-permute-done.refs_3_, ...), custom_call_target="tpu_custom_call" | custom-call | flops 8999999488 | bytes 4194304 | tf_op jit(solution)/shard_map/channelise/pallas_call | solution.py:276
  82.7 20.2 %collective-permute-done.5 = bf16[128,2,16,128]{3,2,1,0:T(8,128)(2,1)} collective-permute-done((bf16[128,2,16,128]{3,2,1,0:T(8,128)(2,1)S(1)}, bf16[128,2,16,128]{3,2,1,0:T(8,128)(2,1)}, u32[]{:S(2)}, u32[]{:S(2)}) %collective-permute-start.5) | collective-permute-done | bytes 1048608 | tf_op jit(solution)/shard_map/ppermute | solution.py:447
  102.9 1.5 slice_bitcast_fusion
  105.7 14.2 %collective-permute-start.7 = (bf16[2,32,2,16,128]{4,3,2,1,0:T(8,128)(2,1)S(1)}, bf16[2,32,2,16,128]{4,3,2,1,0:T(8,128)(2,1)S(1)}, u32[]{:S(2)}, u32[]{:S(2)}) collective-permute-start(bf16[2,32,2,16,128]{4,3,2,1,0:T(8,128)(2,1)S(1)} %get-tuple-element.82), channel_id=1, source_target_pairs={{0,4},{2,6},{4,0},{6,2},{1,5},{3,7},{5,1},{7,3},{8,12},{10,14},{12... | collective-permute-start | bytes 1572872 | tf_op jit(solution)/shard_map/ppermute | solution.py:447
  119.9 15.5 %channelise.3 = (bf16[1536,128]{1,0:T(8,128)(2,1)S(1)}, bf16[1536,128]{1,0:T(8,128)(2,1)S(1)}, bf16[2560,128]{1,0:T(8,128)(2,1)S(1)}, bf16[2560,128]{1,0:T(8,128)(2,1)S(1)}) custom-call(s32[3]{0:T(128)S(1)} %pad_add_fusion.refs_0_, bf16[2,128,8192]{2,1,0:T(8,128)(2,1)S(1)} %bitcast.71, bf16[2,16,8192]{2,1,0:T(8,128)(2,1)S(1)} %copy-done.5, ...), custom_call_target="tpu_custom_call" | custom-call | flops 8999999488 | bytes 4194304 | tf_op jit(solution)/shard_map/channelise/pallas_call | solution.py:276
  137.1 8.1 %collective-permute-done.8 = bf16[48,2,16,128]{3,2,1,0:T(8,128)(2,1)S(1)} collective-permute-done((bf16[48,2,16,128]{3,2,1,0:T(8,128)(2,1)S(1)}, bf16[48,2,16,128]{3,2,1,0:T(8,128)(2,1)S(1)}, u32[]{:S(2)}, u32[]{:S(2)}) %collective-permute-start.8) | collective-permute-done | bytes 393248 | tf_op jit(solution)/shard_map/ppermute | solution.py:447
  145.3 1.5 collective-permute-done.9
  146.7 12.4 %collective-permute-done.10 = bf16[2,32,2,16,128]{4,3,2,1,0:T(8,128)(2,1)S(1)} collective-permute-done((bf16[2,32,2,16,128]{4,3,2,1,0:T(8,128)(2,1)S(1)}, bf16[2,32,2,16,128]{4,3,2,1,0:T(8,128)(2,1)S(1)}, u32[]{:S(2)}, u32[]{:S(2)}) %collective-permute-start.10) | collective-permute-done | bytes 524320 | tf_op jit(solution)/shard_map/ppermute | solution.py:447
  161.5 3.6 %collective-permute-start.12 = (bf16[2,12,2,16,128]{4,3,2,1,0:T(8,128)(2,1)S(1)}, bf16[2,12,2,16,128]{4,3,2,1,0:T(8,128)(2,1)S(1)}, u32[]{:S(2)}, u32[]{:S(2)}) collective-permute-start(bf16[2,12,2,16,128]{4,3,2,1,0:T(8,128)(2,1)S(1)} %pad_maximum_fusion.6), channel_id=1, source_target_pairs={{0,4},{2,6},{4,0},{6,2},{1,5},{3,7},{5,1},{7,3},{8,12},{10,14},{12... | collective-permute-start | bytes 589832 | tf_op jit(solution)/shard_map/ppermute | solution.py:447
  165.1 1.5 collective-permute-start.18
  166.5 9.8 %collective-permute-done.11 = bf16[80,2,16,128]{3,2,1,0:T(8,128)(2,1)S(1)} collective-permute-done((bf16[80,2,16,128]{3,2,1,0:T(8,128)(2,1)S(1)}, bf16[80,2,16,128]{3,2,1,0:T(8,128)(2,1)S(1)}, u32[]{:S(2)}, u32[]{:S(2)}) %collective-permute-start.11) | collective-permute-done | bytes 655392 | tf_op jit(solution)/shard_map/ppermute | solution.py:447
  176.5 3.6 %collective-permute-done.13 = bf16[2,12,2,16,128]{4,3,2,1,0:T(8,128)(2,1)S(1)} collective-permute-done((bf16[2,12,2,16,128]{4,3,2,1,0:T(8,128)(2,1)S(1)}, bf16[2,12,2,16,128]{4,3,2,1,0:T(8,128)(2,1)S(1)}, u32[]{:S(2)}, u32[]{:S(2)}) %collective-permute-start.13) | collective-permute-done | bytes 196640 | tf_op jit(solution)/shard_map/ppermute | solution.py:447
  184.5 12.9 %correlate.3.refs_7_ = f32[8,32,2,2,64,128]{5,4,3,2,1,0:T(8,128)} custom-call(s32[3]{0:T(128)S(1)} %pad_add_fusion.refs_0_, bf16[1024,256]{1,0:T(8,128)(2,1)S(1)} %fusion.refs_1_, f32[8,256]{1,0:T(8,128)S(1)} %tile.10.refs_2_, bf16[256,2,16,128]{3,2,1,0:T(8,128)(2,1)S(1)} %bitcast.61, bf16[256,2,16,128]{3,2,1,0:T(8,128)(2,1)S(1)} %collective-permute-done.14.refs_4_, ...), custom_call_target="tpu_custom_call" | custom-call | flops 4874999808 | bytes 16515072 | tf_op jit(solution)/shard_map/correlate/pallas_call | solution.py:371
  197.4 2.6 %collective-permute-done.16 = bf16[2,12,2,16,128]{4,3,2,1,0:T(8,128)(2,1)S(1)} collective-permute-done((bf16[2,12,2,16,128]{4,3,2,1,0:T(8,128)(2,1)S(1)}, bf16[2,12,2,16,128]{4,3,2,1,0:T(8,128)(2,1)S(1)}, u32[]{:S(2)}, u32[]{:S(2)}) %collective-permute-start.16) | collective-permute-done | bytes 196640 | tf_op jit(solution)/shard_map/ppermute | solution.py:447
  204.3 12.9 %correlate.4.refs_13_ = f32[8,32,2,2,64,128]{5,4,3,2,1,0:T(8,128)} custom-call(s32[3]{0:T(128)S(1)} %pad_add_fusion.refs_0_, bf16[1024,256]{1,0:T(8,128)(2,1)S(1)} %fusion.refs_1_, f32[8,256]{1,0:T(8,128)S(1)} %tile.10.refs_2_, bf16[256,2,16,128]{3,2,1,0:T(8,128)(2,1)S(1)} %bitcast.62, ...), custom_call_target="tpu_custom_call", output_to_operand_aliasing={{}: (7, {})} | custom-call | flops 4874999808 | bytes 16515072 | tf_op jit(solution)/shard_map/correlate/pallas_call | solution.py:371
  219.7 9.4 %correlate.5 = f32[8,32,2,2,64,128]{5,4,3,2,1,0:T(8,128)} custom-call(s32[3]{0:T(128)S(1)} %pad_add_fusion.refs_0_, bf16[1024,256]{1,0:T(8,128)(2,1)S(1)} %fusion.refs_1_, f32[8,256]{1,0:T(8,128)S(1)} %tile.10.refs_2_, bf16[256,2,16,128]{3,2,1,0:T(8,128)(2,1)S(1)} %bitcast.63, ...), custom_call_target="tpu_custom_call", output_to_operand_aliasing={{}: (13, {})} | custom-call | flops 3249999872 | bytes 11010048 | tf_op jit(solution)/shard_map/correlate/pallas_call | solution.py:371
  (110 shorter events, 26.7 us)
Async XLA Ops:
  1.1 25.7 %collective-permute-start = (bf16[2,16,8192]{2,1,0:T(8,128)(2,1)S(1)}, bf16[2,16,8192]{2,1,0:T(8,128)(2,1)S(1)}, u32[]{:S(2)}, u32[]{:S(2)}) collective-permute-start(bf16[2,16,8192]{2,1,0:T(8,128)(2,1)S(1)} %dynamic-slice_bitcast_fusion), channel_id=1, source_target_pairs={{0,4},{2,6},{4,0},{6,2},{1,5},{3,7},{5,1},{7,3},{8,12},{10,14},{12... | collective-permute-start | bytes 1572872 | tf_op jit(solution)/shard_map/ppermute | solution.py:447
  4.8 44.0 %collective-permute-start.1 = (bf16[2,16,8192]{2,1,0:T(8,128)(2,1)S(1)}, bf16[2,16,8192]{2,1,0:T(8,128)(2,1)S(1)}, u32[]{:S(2)}, u32[]{:S(2)}) collective-permute-start(bf16[2,16,8192]{2,1,0:T(8,128)(2,1)S(1)} %get-tuple-element.63), channel_id=1, source_target_pairs={{0,2},{2,4},{4,6},{6,0},{1,3},{3,5},{5,7},{7,1},{8,10},{10,12},{12... | collective-permute-start | bytes 1572872 | tf_op jit(solution)/shard_map/ppermute | solution.py:447
  4.8 54.0 %collective-permute-start.2 = (bf16[2,16,8192]{2,1,0:T(8,128)(2,1)S(1)}, bf16[2,16,8192]{2,1,0:T(8,128)(2,1)S(1)}, u32[]{:S(2)}, u32[]{:S(2)}) collective-permute-start(bf16[2,16,8192]{2,1,0:T(8,128)(2,1)S(1)} %get-tuple-element.66), channel_id=1, source_target_pairs={{0,6},{2,0},{4,2},{6,4},{1,7},{3,1},{5,3},{7,5},{8,14},{10,8},{12,... | collective-permute-start | bytes 1572872 | tf_op jit(solution)/shard_map/ppermute | solution.py:447
  48.8 30.4 %collective-permute-start.3 = (bf16[2,16,8192]{2,1,0:T(8,128)(2,1)S(1)}, bf16[2,16,8192]{2,1,0:T(8,128)(2,1)S(1)}, u32[]{:S(2)}, u32[]{:S(2)}) collective-permute-start(bf16[2,16,8192]{2,1,0:T(8,128)(2,1)S(1)} %get-tuple-element.69), channel_id=1, source_target_pairs={{0,2},{2,4},{4,6},{6,0},{1,3},{3,5},{5,7},{7,1},{8,10},{10,12},{12... | collective-permute-start | bytes 1572872 | tf_op jit(solution)/shard_map/ppermute | solution.py:447
  51.0 29.0 %collective-permute-start.4 = (bf16[2,16,8192]{2,1,0:T(8,128)(2,1)S(1)}, bf16[2,16,8192]{2,1,0:T(8,128)(2,1)S(1)}, u32[]{:S(2)}, u32[]{:S(2)}) collective-permute-start(bf16[2,16,8192]{2,1,0:T(8,128)(2,1)S(1)} %get-tuple-element.71), channel_id=1, source_target_pairs={{0,6},{2,0},{4,2},{6,4},{1,7},{3,1},{5,3},{7,5},{8,14},{10,8},{12,... | collective-permute-start | bytes 1572872 | tf_op jit(solution)/shard_map/ppermute | solution.py:447
  80.8 22.1 %collective-permute-start.5 = (bf16[128,2,16,128]{3,2,1,0:T(8,128)(2,1)S(1)}, bf16[128,2,16,128]{3,2,1,0:T(8,128)(2,1)}, u32[]{:S(2)}, u32[]{:S(2)}) collective-permute-start(bf16[128,2,16,128]{3,2,1,0:T(8,128)(2,1)S(1)} %bitcast.82), channel_id=1, source_target_pairs={{0,8},{8,0},{1,9},{9,1},{2,10},{10,2},{3,11},{11,3},{4,12},{12,4},... | collective-permute-start | bytes 3145736 | tf_op jit(solution)/shard_map/ppermute | solution.py:447
  82.5 23.2 %collective-permute-start.6 = (bf16[2,16,8192]{2,1,0:T(8,128)(2,1)}, bf16[2,16,8192]{2,1,0:T(8,128)(2,1)S(1)}, u32[]{:S(2)}, u32[]{:S(2)}) collective-permute-start(bf16[2,16,8192]{2,1,0:T(8,128)(2,1)} %get-tuple-element.73), channel_id=1, source_target_pairs={{0,4},{2,6},{4,0},{6,2},{1,5},{3,7},{5,1},{7,3},{8,12},{10,14},{12... | collective-permute-start | bytes 1572872 | tf_op jit(solution)/shard_map/ppermute | solution.py:447
  105.7 29.7 %collective-permute-start.7 = (bf16[2,32,2,16,128]{4,3,2,1,0:T(8,128)(2,1)S(1)}, bf16[2,32,2,16,128]{4,3,2,1,0:T(8,128)(2,1)S(1)}, u32[]{:S(2)}, u32[]{:S(2)}) collective-permute-start(bf16[2,32,2,16,128]{4,3,2,1,0:T(8,128)(2,1)S(1)} %get-tuple-element.82), channel_id=1, source_target_pairs={{0,4},{2,6},{4,0},{6,2},{1,5},{3,7},{5,1},{7,3},{8,12},{10,14},{12... | collective-permute-start | bytes 1572872 | tf_op jit(solution)/shard_map/ppermute | solution.py:447
  135.4 9.7 %collective-permute-start.8 = (bf16[48,2,16,128]{3,2,1,0:T(8,128)(2,1)S(1)}, bf16[48,2,16,128]{3,2,1,0:T(8,128)(2,1)S(1)}, u32[]{:S(2)}, u32[]{:S(2)}) collective-permute-start(bf16[48,2,16,128]{3,2,1,0:T(8,128)(2,1)S(1)} %bitcast.84), channel_id=1, source_target_pairs={{0,8},{8,0},{1,9},{9,1},{2,10},{10,2},{3,11},{11,3},{4,12},{12,4},... | collective-permute-start | bytes 1179656 | tf_op jit(solution)/shard_map/ppermute | solution.py:447
  135.5 11.2 %collective-permute-start.9 = (bf16[2,32,2,16,128]{4,3,2,1,0:T(8,128)(2,1)S(1)}, bf16[2,32,2,16,128]{4,3,2,1,0:T(8,128)(2,1)S(1)}, u32[]{:S(2)}, u32[]{:S(2)}) collective-permute-start(bf16[2,32,2,16,128]{4,3,2,1,0:T(8,128)(2,1)S(1)} %get-tuple-element.85), channel_id=1, source_target_pairs={{0,2},{2,4},{4,6},{6,0},{1,3},{3,5},{5,7},{7,1},{8,10},{10,12},{12... | collective-permute-start | bytes 1572872 | tf_op jit(solution)/shard_map/ppermute | solution.py:447
  135.6 23.6 %collective-permute-start.10 = (bf16[2,32,2,16,128]{4,3,2,1,0:T(8,128)(2,1)S(1)}, bf16[2,32,2,16,128]{4,3,2,1,0:T(8,128)(2,1)S(1)}, u32[]{:S(2)}, u32[]{:S(2)}) collective-permute-start(bf16[2,32,2,16,128]{4,3,2,1,0:T(8,128)(2,1)S(1)} %pad_maximum_fusion.5), channel_id=1, source_target_pairs={{0,6},{2,0},{4,2},{6,4},{1,7},{3,1},{5,3},{7,5},{8,14},{10,8},{12,... | collective-permute-start | bytes 1572872 | tf_op jit(solution)/shard_map/ppermute | solution.py:447
  159.5 20.6 %collective-permute-start.14 = (bf16[256,2,16,128]{3,2,1,0:T(8,128)(2,1)S(1)}, bf16[256,2,16,128]{3,2,1,0:T(8,128)(2,1)S(1)}, u32[]{:S(2)}, u32[]{:S(2)}) collective-permute-start(bf16[256,2,16,128]{3,2,1,0:T(8,128)(2,1)S(1)} %bitcast.60), channel_id=1, source_target_pairs={{0,1},{1,0},{2,3},{3,2},{4,5},{5,4},{6,7},{7,6},{8,9},{9,8},{10,11... | collective-permute-start | bytes 6291464 | tf_op jit(solution)/shard_map/ppermute | solution.py:447
  160.0 16.3 %collective-permute-start.11 = (bf16[80,2,16,128]{3,2,1,0:T(8,128)(2,1)S(1)}, bf16[80,2,16,128]{3,2,1,0:T(8,128)(2,1)S(1)}, u32[]{:S(2)}, u32[]{:S(2)}) collective-permute-start(bf16[80,2,16,128]{3,2,1,0:T(8,128)(2,1)S(1)} %bitcast.83), channel_id=1, source_target_pairs={{0,8},{8,0},{1,9},{9,1},{2,10},{10,2},{3,11},{11,3},{4,12},{12,4},... | collective-permute-start | bytes 1966088 | tf_op jit(solution)/shard_map/ppermute | solution.py:447
  161.5 15.0 %collective-permute-start.12 = (bf16[2,12,2,16,128]{4,3,2,1,0:T(8,128)(2,1)S(1)}, bf16[2,12,2,16,128]{4,3,2,1,0:T(8,128)(2,1)S(1)}, u32[]{:S(2)}, u32[]{:S(2)}) collective-permute-start(bf16[2,12,2,16,128]{4,3,2,1,0:T(8,128)(2,1)S(1)} %pad_maximum_fusion.6), channel_id=1, source_target_pairs={{0,4},{2,6},{4,0},{6,2},{1,5},{3,7},{5,1},{7,3},{8,12},{10,14},{12... | collective-permute-start | bytes 589832 | tf_op jit(solution)/shard_map/ppermute | solution.py:447
  165.1 15.0 %collective-permute-start.13 = (bf16[2,12,2,16,128]{4,3,2,1,0:T(8,128)(2,1)S(1)}, bf16[2,12,2,16,128]{4,3,2,1,0:T(8,128)(2,1)S(1)}, u32[]{:S(2)}, u32[]{:S(2)}) collective-permute-start(bf16[2,12,2,16,128]{4,3,2,1,0:T(8,128)(2,1)S(1)} %pad_maximum_fusion.7), channel_id=1, source_target_pairs={{0,2},{2,4},{4,6},{6,0},{1,3},{3,5},{5,7},{7,1},{8,10},{10,12},{12... | collective-permute-start | bytes 589832 | tf_op jit(solution)/shard_map/ppermute | solution.py:447
  165.1 16.2 %collective-permute-start.18 = (bf16[2,12,2,16,128]{4,3,2,1,0:T(8,128)(2,1)S(1)}, bf16[2,12,2,16,128]{4,3,2,1,0:T(8,128)(2,1)S(1)}, u32[]{:S(2)}, u32[]{:S(2)}) collective-permute-start(bf16[2,12,2,16,128]{4,3,2,1,0:T(8,128)(2,1)S(1)} %pad_maximum_fusion.8), channel_id=1, source_target_pairs={{0,6},{2,0},{4,2},{6,4},{1,7},{3,1},{5,3},{7,5},{8,14},{10,8},{12,... | collective-permute-start | bytes 589832 | tf_op jit(solution)/shard_map/ppermute | solution.py:447
  181.4 3.2 %collective-permute-start.19 = (bf16[96,2,16,128]{3,2,1,0:T(8,128)(2,1)S(1)}, bf16[96,2,16,128]{3,2,1,0:T(8,128)(2,1)S(1)}, u32[]{:S(2)}, u32[]{:S(2)}) collective-permute-start(bf16[96,2,16,128]{3,2,1,0:T(8,128)(2,1)S(1)} %bitcast.66), channel_id=1, source_target_pairs={{0,1},{1,0},{2,3},{3,2},{4,5},{5,4},{6,7},{7,6},{8,9},{9,8},{10,11... | collective-permute-start | bytes 2359304 | tf_op jit(solution)/shard_map/ppermute | solution.py:447
  182.8 14.6 %collective-permute-start.15 = (bf16[2,12,2,16,128]{4,3,2,1,0:T(8,128)(2,1)S(1)}, bf16[2,12,2,16,128]{4,3,2,1,0:T(8,128)(2,1)S(1)}, u32[]{:S(2)}, u32[]{:S(2)}) collective-permute-start(bf16[2,12,2,16,128]{4,3,2,1,0:T(8,128)(2,1)S(1)} %pad_maximum_fusion.9), channel_id=1, source_target_pairs={{0,4},{2,6},{4,0},{6,2},{1,5},{3,7},{5,1},{7,3},{8,12},{10,14},{12... | collective-permute-start | bytes 589832 | tf_op jit(solution)/shard_map/ppermute | solution.py:447
  182.8 17.2 %collective-permute-start.16 = (bf16[2,12,2,16,128]{4,3,2,1,0:T(8,128)(2,1)S(1)}, bf16[2,12,2,16,128]{4,3,2,1,0:T(8,128)(2,1)S(1)}, u32[]{:S(2)}, u32[]{:S(2)}) collective-permute-start(bf16[2,12,2,16,128]{4,3,2,1,0:T(8,128)(2,1)S(1)} %pad_maximum_fusion.10), channel_id=1, source_target_pairs={{0,2},{2,4},{4,6},{6,0},{1,3},{3,5},{5,7},{7,1},{8,10},{10,12},{12... | collective-permute-start | bytes 589832 | tf_op jit(solution)/shard_map/ppermute | solution.py:447
  183.2 17.8 %collective-permute-start.17 = (bf16[2,12,2,16,128]{4,3,2,1,0:T(8,128)(2,1)S(1)}, bf16[2,12,2,16,128]{4,3,2,1,0:T(8,128)(2,1)S(1)}, u32[]{:S(2)}, u32[]{:S(2)}) collective-permute-start(bf16[2,12,2,16,128]{4,3,2,1,0:T(8,128)(2,1)S(1)} %pad_maximum_fusion.11), channel_id=1, source_target_pairs={{0,6},{2,0},{4,2},{6,4},{1,7},{3,1},{5,3},{7,5},{8,14},{10,8},{12,... | collective-permute-start | bytes 589832 | tf_op jit(solution)/shard_map/ppermute | solution.py:447
  201.1 3.2 %collective-permute-start.23 = (bf16[96,2,16,128]{3,2,1,0:T(8,128)(2,1)S(1)}, bf16[96,2,16,128]{3,2,1,0:T(8,128)(2,1)S(1)}, u32[]{:S(2)}, u32[]{:S(2)}) collective-permute-start(bf16[96,2,16,128]{3,2,1,0:T(8,128)(2,1)S(1)} %bitcast.64), channel_id=1, source_target_pairs={{0,1},{1,0},{2,3},{3,2},{4,5},{5,4},{6,7},{7,6},{8,9},{9,8},{10,11... | collective-permute-start | bytes 2359304 | tf_op jit(solution)/shard_map/ppermute | solution.py:447
  201.8 15.3 %collective-permute-start.20 = (bf16[2,8,2,16,128]{4,3,2,1,0:T(8,128)(2,1)S(1)}, bf16[2,8,2,16,128]{4,3,2,1,0:T(8,128)(2,1)S(1)}, u32[]{:S(2)}, u32[]{:S(2)}) collective-permute-start(bf16[2,8,2,16,128]{4,3,2,1,0:T(8,128)(2,1)S(1)} %pad_maximum_fusion.14), channel_id=1, source_target_pairs={{0,4},{2,6},{4,0},{6,2},{1,5},{3,7},{5,1},{7,3},{8,12},{10,14},{12... | collective-permute-start | bytes 393224 | tf_op jit(solution)/shard_map/ppermute | solution.py:447
  201.9 15.3 %collective-permute-start.21 = (bf16[2,8,2,16,128]{4,3,2,1,0:T(8,128)(2,1)S(1)}, bf16[2,8,2,16,128]{4,3,2,1,0:T(8,128)(2,1)S(1)}, u32[]{:S(2)}, u32[]{:S(2)}) collective-permute-start(bf16[2,8,2,16,128]{4,3,2,1,0:T(8,128)(2,1)S(1)} %pad_maximum_fusion.15), channel_id=1, source_target_pairs={{0,2},{2,4},{4,6},{6,0},{1,3},{3,5},{5,7},{7,1},{8,10},{10,12},{12... | collective-permute-start | bytes 393224 | tf_op jit(solution)/shard_map/ppermute | solution.py:447
  203.2 14.0 %collective-permute-start.22 = (bf16[2,8,2,16,128]{4,3,2,1,0:T(8,128)(2,1)S(1)}, bf16[2,8,2,16,128]{4,3,2,1,0:T(8,128)(2,1)S(1)}, u32[]{:S(2)}, u32[]{:S(2)}) collective-permute-start(bf16[2,8,2,16,128]{4,3,2,1,0:T(8,128)(2,1)S(1)} %pad_maximum_fusion.16), channel_id=1, source_target_pairs={{0,6},{2,0},{4,2},{6,4},{1,7},{3,1},{5,3},{7,5},{8,14},{10,8},{12,... | collective-permute-start | bytes 393224 | tf_op jit(solution)/shard_map/ppermute | solution.py:447
  (18 other events, 195.4 us)

commit v2 on v0

--- a/solution.py
+++ b/solution.py
@@ -254,7 +254,7 @@
 
     share = w_ref.shape[0] // (columns * sources)
     band_rows = 2 * ROWS
-    piece = 8 * band_rows
+    piece = 4 * band_rows
     for blocks, out_ref in zip(plan, out_refs):
         at = 0
         for across, along, start, stop in blocks:
@@ -299,89 +299,103 @@
     return [piece.reshape(count, 2, ROWS, LANES) for piece, count in zip(flat, counts)]
 
 
-def correlate_kernel(places, starts, width, place_ref, sel_ref, weight_ref, *refs):
-    x_refs, (out_ref, x_all, rows_all, sems) = refs[: 2 * len(starts)], refs[-4:]
+def correlate_kernel(starts, width, place_ref, sel_ref, weight_ref, *refs):
+    x_refs, (out_ref, x_all, even_rows, odd_rows, sems) = refs[: 2 * len(starts)], refs[-5:]
     tiles = out_ref.shape[0]
-    band = pl.program_id(0)
-    bands = x_all.shape[1]
-    spans = [(0, 1), (1, bands)]
+    step = pl.program_id(0)
+    bands = x_all.shape[2]
+    spans = [(0, 2), (2, bands)]
 
     def copies(span):
         first, last = spans[span]
-        number = 0
-        for index, (start, rows) in enumerate(zip(starts, places)):
+        block = 0
+        for index, start in enumerate(starts):
+            blocks = x_refs[2 * index].shape[0]
             for side in range(2):
-                x_ref = x_refs[2 * index + side]
-                pol = lax.rem(place_ref[2] + side, 2)
-                share = x_ref.shape[0] // len(rows)
-                for block, at in enumerate(rows):
-                    yield pltpu.make_async_copy(
-                        x_ref.at[pl.ds(block * share + start + first, last - first)],
-                        x_all.at[pol, pl.ds(first, last - first), :, pl.ds(at, ROWS), :],
-                        sems.at[span, number],
-                    )
-                    number += 1
-
-    @pl.when(band == 0)
+                yield pltpu.make_async_copy(
+                    x_refs[2 * index + side].at[:, pl.ds(start + first, last - first)],
+                    x_all.at[
+                        lax.rem(place_ref[2] + side, 2),
+                        pl.ds(block, blocks),
+                        pl.ds(first, last - first),
+                    ],
+                    sems.at[span, 2 * index + side],
+                )
+            block += blocks
+
+    def gather(band, rows_ref):
+        for pol in range(2):
+            lanes = slice(pol * 2 * LANES, (pol + 1) * 2 * LANES)
+            value = jnp.concatenate(
+                [
+                    jnp.concatenate([x_all[pol, block, band, part] for part in range(2)], axis=1)
+                    for block in range(x_all.shape[1])
+                ]
+            )
+            picked = jnp.dot(sel_ref[...], value, preferred_element_type=jnp.float32)
+            for tile in range(tiles):
+                at = tile * 2 * width
+                left = picked[at : at + width] * weight_ref[pl.ds(tile, 1), :]
+                right = picked[at + width : at + 2 * width]
+                rows_ref[at : at + width, lanes] = left.astype(jnp.bfloat16)
+                rows_ref[at + width : at + 2 * width, lanes] = right.astype(jnp.bfloat16)
+
+    form = (((1,), (1,)), ((), ()))
+
+    def multiply(number, rows_ref):
+        for tile in range(tiles):
+            at = tile * 2 * width
+            left, right = (
+                jnp.concatenate(
+                    [
+                        rows_ref[at + first : at + first + width, lanes : lanes + 2 * LANES]
+                        for lanes in (0, 2 * LANES)
+                    ]
+                )
+                for first in (0, width)
+            )
+            turned = jnp.concatenate([left[:, LANES:], -left[:, :LANES]], axis=1)
+            both = jnp.concatenate([left, turned])
+            result = lax.dot_general(both, right, form, preferred_element_type=jnp.float32)
+            out_ref[tile, number] = result.reshape(2, 2, width, 2 * width)
+
+    @pl.when(step == 0)
     def _():
         for span in range(2):
             for copy in copies(span):
                 copy.start()
         for copy in copies(0):
             copy.wait()
-
-    @pl.when(band == 1)
-    def _():
+        gather(0, even_rows)
         for copy in copies(1):
             copy.wait()
 
-    for pol in range(2):
-        lanes = slice(pol * 2 * LANES, (pol + 1) * 2 * LANES)
-        value = jnp.concatenate([x_all[pol, band, part] for part in range(2)], axis=1)
-        picked = jnp.dot(sel_ref[...], value, preferred_element_type=jnp.float32)
-        for tile in range(tiles):
-            at = tile * 2 * width
-            left = picked[at : at + width] * weight_ref[pl.ds(tile, 1), :]
-            right = picked[at + width : at + 2 * width]
-            rows_all[at : at + width, lanes] = left.astype(jnp.bfloat16)
-            rows_all[at + width : at + 2 * width, lanes] = right.astype(jnp.bfloat16)
-    form = (((1,), (1,)), ((), ()))
-    for tile in range(tiles):
-        at = tile * 2 * width
-        left = jnp.concatenate(
-            [rows_all[at : at + width, pol * 2 * LANES : (pol + 1) * 2 * LANES] for pol in range(2)]
-        )
-        at += width
-        right = jnp.concatenate(
-            [rows_all[at : at + width, pol * 2 * LANES : (pol + 1) * 2 * LANES] for pol in range(2)]
-        )
-        turned = jnp.concatenate([left[:, LANES:], -left[:, :LANES]], axis=1)
-        both = jnp.concatenate([left, turned])
-        result = lax.dot_general(both, right, form, preferred_element_type=jnp.float32)
-        out_ref[tile, 0] = result.reshape(2, 2, width, 2 * width)
-
-
-def correlate_tiles(
-    place, select, weight, pieces, places, starts, width, first, count, bands, earlier
-):
+    gather(2 * step + 1, odd_rows)
+    multiply(0, even_rows)
+    gather(jnp.minimum(2 * step + 2, bands - 1), even_rows)
+    multiply(1, odd_rows)
+
+
+def correlate_tiles(place, select, weight, pieces, starts, width, first, count, bands, earlier):
     tiles = weight.shape[0]
     whole = pl.BlockSpec(memory_space=pltpu.VMEM)
     more = [] if earlier is None else [earlier]
-    blocks = 2 * sum(len(rows) for rows in places)
+    rows = pltpu.VMEM((tiles * 2 * width, 4 * LANES), jnp.bfloat16)
     return pl.pallas_call(
-        lambda *refs: correlate_kernel(places, starts, width, *refs),
-        grid=(count,),
+        lambda *refs: correlate_kernel(starts, width, *refs),
+        grid=(count // 2,),
         out_shape=jax.ShapeDtypeStruct((tiles, bands, 2, 2, width, 2 * width), jnp.float32),
         in_specs=[pl.BlockSpec(memory_space=pltpu.SMEM)]
         + [whole] * 2
         + [pl.BlockSpec(memory_space=pl.ANY)] * (len(pieces) + len(more)),
         out_specs=pl.BlockSpec(
-            (tiles, 1, 2, 2, width, 2 * width), lambda g: (0, g + first, 0, 0, 0, 0)
+            (tiles, 2, 2, 2, width, 2 * width), lambda g: (0, g + first // 2, 0, 0, 0, 0)
         ),
         scratch_shapes=[
-            pltpu.VMEM((2, count, 2, select.shape[1], LANES), jnp.bfloat16),
-            pltpu.VMEM((tiles * 2 * width, 4 * LANES), jnp.bfloat16),
-            pltpu.SemaphoreType.DMA((2, blocks)),
+            pltpu.VMEM((2, select.shape[1] // ROWS, count, 2, ROWS, LANES), jnp.bfloat16),
+            rows,
+            rows,
+            pltpu.SemaphoreType.DMA((2, len(pieces))),
         ],
         input_output_aliases={3 + len(pieces): 0} if more else {},
         compiler_params=pltpu.CompilerParams(vmem_limit_bytes=32 * 2**20),
@@ -426,7 +440,7 @@
         block, inside = rest // (chunk_count * ROWS), rest % (chunk_count * ROWS)
         across = (chan - column) % chan_count
         behind = (tm - block) % time_count
-        piece = across * time_count + behind
+        piece = behind * chan_count + across
         return ((inside // ROWS) * owners + piece) * ROWS + inside % ROWS
 
     rows, flags = tile_tables(tile_a, tile_b, tile_owner, tile_flags, row_of)
@@ -453,80 +467,80 @@
         first = ((tm + distance) % time_count * chunk_count + chunk) * ROWS
         return lax.dynamic_slice(values, (0, first, 0), (2, ROWS, frames * length))
 
-    def turn_time(blocks):
-        return [travel(block, ("tm",), (d,)) for d, block in zip(distances, blocks)]
-
     def filtered(chunk, arrived, plan):
-        arrived = [arrived[distances.index(d)] for d in range(1, time_count)]
         return channelise(
             place, chunk, samples, arrived, taps_filter, tables, frames, chan_count, plan
         )
 
-    def across(values):
+    sent = []
+
+    def over_tm(value, distance, guard):
+        if guard <= len(sent):
+            (value,), sent[-guard : len(sent) - guard + 1] = after([value], [sent[-guard]])
+        sent.append(travel(value, ("tm",), (distance,)))
+
+    def over_chan(values, guard):
+        values, sent[guard : guard + 1] = after(values, [sent[guard]])
         return [travel(v, ("chan",), (1,)) for v in values]
 
     def columns(near, far):
         return jnp.stack([near, far])
 
-    distances = [2, 1, 3]
+    hops = range(1, time_count)
     half = bands // 2
-    spare = 1
-
-    blocks = [block_for(samples, 0, d) for d in distances]
-    blocks, (again,) = after(blocks, [samples])
-    first = turn_time(blocks)
-    blocks, held = after([block_for(again, 1, d) for d in distances], first[:-spare])
-    first[:-spare] = held
-    second = turn_time(blocks)
-
-    plan = [[(x, z, 0, bands)] for x in range(2) for z in range(time_count)]
-    spectra = filtered(0, first, plan)
-    far, second[:1] = after(spectra[time_count:], second[:1])
-    near, far = spectra[:time_count], across(far)
-    mixed = [columns(near[z], far[z]) for z in range(time_count)]
-    blocks, held = after([mixed[d] for d in distances], second[:-spare] + [select, weight])
-    second[:-spare], (select, weight) = held[:-2], held[-2:]
-    own_first = [mixed[0]] + turn_time(blocks)
-
-    plan = [
-        [(x, z, start, start + half) for z in range(time_count)]
-        for start in (0, half)
-        for x in range(2)
-    ]
-    spectra = filtered(1, second, plan)
-    spectra = [v.reshape(time_count, half, 2, ROWS, LANES) for v in spectra]
-    far, own_first[1:2] = after([spectra[1], spectra[3]], own_first[1:2])
-    far_low, far_high = across(far)
-    mixed = [columns(spectra[0][z], far_low[z]) for z in range(time_count)]
-    blocks, held = after([mixed[d] for d in distances], own_first[1:-spare])
-    own_first[1:-spare] = held
-    own_low = [mixed[0]] + turn_time(blocks)
-    mixed = [columns(spectra[2][z], far_high[z]) for z in range(time_count)]
+    spans = [(0, half), (half, bands)]
+
+    values = samples
+    for distance in hops:
+        block = block_for(values, 0, distance)
+        over_tm(block, distance, 2)
+        if distance == 1:
+            (block,), (values,) = after([block], [samples])
+    for distance in hops:
+        over_tm(block_for(values, 1, distance), distance, 2)
+
+    order = [1, 2, 3, 0]
+    plan = [[(x, z, 0, bands) for z in order] for x in range(chan_count)]
+    plan = plan[:1] + [plan[1][:2], plan[1][2:]]
+    near, *far = filtered(0, sent[:3], plan)
+    near = near.reshape(time_count, bands, 2, ROWS, LANES)
+    far = over_chan(far[:1], 3) + over_chan(far[1:], 4)
+    far = [v.reshape(2, bands, 2, ROWS, LANES) for v in far]
+    mixed = {z: columns(near[i], far[i // 2][i % 2]) for i, z in enumerate(order)}
+    sent[4:5], (select, weight) = after([sent[4]], [select, weight])
+    for distance in hops:
+        over_tm(mixed[distance], distance, 2)
+    home = mixed[0]
+
+    plan = [[(x, z, *span) for z in range(time_count)] for span in spans for x in range(2)]
+    low, far_low, high, far_high = filtered(1, sent[3:6], plan)
+    far = over_chan([far_low], 6) + over_chan([far_high], 7)
+    shape = (time_count, half, 2, ROWS, LANES)
+    low, high, far_low, far_high = (v.reshape(shape) for v in (low, high, *far))
+    low = [columns(low[z], far_low[z]) for z in range(time_count)]
+    high = [columns(high[z], far_high[z]) for z in range(time_count)]
+    for distance in hops:
+        over_tm(low[distance], distance, 2)
+
+    def flat(values):
+        return jnp.stack(values).reshape((-1,) + values[0].shape[1:])
 
     def with_other(values):
-        values = [v.reshape((-1,) + v.shape[2:]) for v in values]
         return [side for v in values for side in (v, travel(v, ("pol",), (1,)))]
 
-    both_first = with_other(own_first)
-    blocks, held = after([mixed[d] for d in distances], own_low[1:-spare] + both_first[1::2])
-    own_low[1:-spare], both_first[1::2] = held[: -time_count], held[-time_count:]
-    own_high = [mixed[0]] + turn_time(blocks)
-
-    both_low = with_other(own_low)
-    places = [
-        [((chunk * chan_count + x) * time_count + z) * ROWS for x in range(chan_count)]
-        for chunk in range(chunk_count)
-        for z in [0] + distances
-    ]
+    early = with_other([flat([home] + sent[6:9])])
+    blocks, held = after(high[1:], sent[10:12] + early[1:])
+    sent[10:12], early[1:] = held[:2], held[2:]
+    for distance, block in zip(hops, blocks):
+        over_tm(block, distance, len(sent) + 1)
     visibility = correlate_tiles(
-        place, select, weight, both_first + both_low, places, [0] * 8, width,
-        0, half, bands, None,
-    )
-    own_high, (visibility,) = after(own_high, [visibility])
-    both_high = with_other(own_high)
+        place, select, weight, early + with_other([flat([low[0]] + sent[9:12])]),
+        [0, 0], width, 0, half, bands, None,
+    )
+    last, (visibility,) = after([high[0]] + sent[12:15], [visibility])
     return correlate_tiles(
-        place, select, weight, both_first + both_high, places, [half] * 4 + [0] * 4, width,
-        half, half, bands, visibility,
+        place, select, weight, early + with_other(last),
+        [half] + [0] * 4, width, half, half, bands, visibility,
     )
 
 

time: 224 us -> 234 us (1.045)
  starting transfers between devices: 30.2 us -> 45.7 us
  waiting for transfers between devices: 108 us -> 114 us
  Pallas kernels: 65.1 us -> 59.5 us
  local copies, waits for them, and re-layouts: 14.7 us -> 10.3 us
  other arithmetic: 5.36 us -> 2.26 us
    ppermute x33 -> x25, starting transfers between devices: 30.2 us -> 45.7 us  [travel(): return lax.ppermute(value, axes, pairs)]
    ppermute x33 -> x25, waiting for transfers between devices: 108 us -> 114 us  [travel(): return lax.ppermute(value, axes, pairs)]
    pallas_call x2, Pallas kernels: 33.2 us -> 27.6 us  [correlate_tiles(): pl.pallas_call(lambda *refs: correlate_kernel(starts, width, *refs), grid...]
    unnamed x20, local copies, waits for them, and re-layouts: 9.54 us -> 4.78 us
    another operation x12 -> x10, other arithmetic: 3.26 us -> 0.34 us  [columns(): return jnp.stack([near, far])]
  transfers between devices with their start and end apart: 33 -> 25, of which waited for: 19 -> 16; matrix products, arithmetic and copies ran while one was open for 4% -> 3% of each run, Pallas kernels for 22% -> 19%
where the time goes in v2:
time: 234 us; the launch traced here: 233 us
  waiting for transfers between devices  114 us (49%)
  Pallas kernels  59.5 us (25%)
  starting transfers between devices  45.7 us (20%)
  local copies, waits for them, and re-layouts  10.3 us (4%)
    ppermute x25, waiting for transfers between devices, travel(): return lax.ppermute(value, axes, pairs)  114 us
    ppermute x25, starting transfers between devices, travel(): return lax.ppermute(value, axes, pairs)  45.7 us
    pallas_call x2, Pallas kernels, channelise(): pl.pallas_call(lambda *refs: channelise_kernel(frames, chunk, columns, pl...  31.9 us
    pallas_call x2, Pallas kernels, correlate_tiles(): pl.pallas_call(lambda *refs: correlate_kernel(starts, width, *refs), grid...  27.6 us
    unnamed x20, local copies, waits for them, and re-layouts  4.78 us
  transfers between devices with their start and end apart: 25, of which 16 were waited for; matrix products, arithmetic and copies ran while one was open for 3% of the time, Pallas kernels for 19%

profile of v2, /device:TPU:11, one launch (start us, length us, event | category | flops | bytes accessed | tf_op | source)
XLA Modules:
  0.0 232.5 jit_solution(9015168023673712332)
XLA Ops:
  2.4 2.9 %constant_dynamic-slice_fusion = (bf16[2,16,8192]{2,1,0:T(8,128)(2,1)}, bf16[2,16,8192]{2,1,0:T(8,128)(2,1)}, bf16[2,16,8192]{2,1,0:T(8,128)(2,1)S(1)}, bf16[2,1...) fusion(bf16[2,128,8192]{2,1,0:T(8,128)(2,1)} %bitcast.67, s32[]{:T(128)S(6)} %select_n.125, s32[]{:T(128)S(6)} %select_n.108, ...), kind=kLoop, calls=%fused_computation.126 | loop fusion | bytes 5242900 | tf_op jit(solution)/shard_map/dynamic_slice | solution.py:468
  7.5 6.4 %collective-permute-done.refs_2_ = bf16[2,16,8192]{2,1,0:T(8,128)(2,1)S(1)} collective-permute-done((bf16[2,16,8192]{2,1,0:T(8,128)(2,1)S(1)}, bf16[2,16,8192]{2,1,0:T(8,128)(2,1)S(1)}, u32[]{:S(2)}, u32[]{:S(2)}) %collective-permute-start) | collective-permute-done | bytes 524320 | tf_op jit(solution)/shard_map/ppermute | solution.py:461
  13.9 2.1 collective-permute-start.2
  16.1 30.7 %collective-permute-done.1.refs_3_ = bf16[2,16,8192]{2,1,0:T(8,128)(2,1)S(1)} collective-permute-done((bf16[2,16,8192]{2,1,0:T(8,128)(2,1)S(1)}, bf16[2,16,8192]{2,1,0:T(8,128)(2,1)S(1)}, u32[]{:S(2)}, u32[]{:S(2)}) %collective-permute-start.1) | collective-permute-done | bytes 524320 | tf_op jit(solution)/shard_map/ppermute | solution.py:461
  47.8 3.2 %collective-permute-start.3 = (bf16[2,16,8192]{2,1,0:T(8,128)(2,1)}, bf16[2,16,8192]{2,1,0:T(8,128)(2,1)S(1)}, u32[]{:S(2)}, u32[]{:S(2)}) collective-permute-start(bf16[2,16,8192]{2,1,0:T(8,128)(2,1)} %get-tuple-element.61), channel_id=1, source_target_pairs={{0,4},{2,6},{4,0},{6,2},{1,5},{3,7},{5,1},{7,3},{8,12},{10,14},{12... | collective-permute-start | bytes 1572872 | tf_op jit(solution)/shard_map/ppermute | solution.py:461
  51.0 8.4 %collective-permute-done.5.refs_2_ = bf16[2,16,8192]{2,1,0:T(8,128)(2,1)S(1)} collective-permute-done((bf16[2,16,8192]{2,1,0:T(8,128)(2,1)S(1)}, bf16[2,16,8192]{2,1,0:T(8,128)(2,1)S(1)}, u32[]{:S(2)}, u32[]{:S(2)}) %collective-permute-start.5) | collective-permute-done | bytes 524320 | tf_op jit(solution)/shard_map/ppermute | solution.py:461
  59.4 2.2 copy-done
  63.4 16.3 %channelise.2 = (bf16[4096,128]{1,0:T(8,128)(2,1)S(1)}, bf16[2048,128]{1,0:T(8,128)(2,1)}, bf16[2048,128]{1,0:T(8,128)(2,1)S(1)}) custom-call(s32[3]{0:T(128)S(1)} %pad_add_fusion.refs_0_, bf16[2,128,8192]{2,1,0:T(8,128)(2,1)S(1)} %bitcast.68, bf16[2,16,8192]{2,1,0:T(8,128)(2,1)S(1)} %collective-permute-done.refs_2_, bf16[2,16,8192]{2,1,0:T(8,128)(2,1)S(1)} %copy-done.3, ...), custom_call_target="tpu_custom_call" | custom-call | flops 8999999488 | bytes 4194304 | tf_op jit(solution)/shard_map/channelise/pallas_call | solution.py:276
  80.4 3.2 %collective-permute-start.7 = (bf16[2,16,8192]{2,1,0:T(8,128)(2,1)}, bf16[2,16,8192]{2,1,0:T(8,128)(2,1)S(1)}, u32[]{:S(2)}, u32[]{:S(2)}) collective-permute-start(bf16[2,16,8192]{2,1,0:T(8,128)(2,1)} %get-tuple-element.74), channel_id=1, source_target_pairs={{0,6},{2,0},{4,2},{6,4},{1,7},{3,1},{5,3},{7,5},{8,14},{10,8},{12,... | collective-permute-start | bytes 1572872 | tf_op jit(solution)/shard_map/ppermute | solution.py:461
  85.0 3.1 %collective-permute-done.6 = bf16[64,2,16,128]{3,2,1,0:T(8,128)(2,1)} collective-permute-done((bf16[64,2,16,128]{3,2,1,0:T(8,128)(2,1)}, bf16[64,2,16,128]{3,2,1,0:T(8,128)(2,1)}, u32[]{:S(2)}, u32[]{:S(2)}) %collective-permute-start.6) | collective-permute-done | bytes 524320 | tf_op jit(solution)/shard_map/ppermute | solution.py:461
  89.3 1.7 collective-permute-done.7.refs_4_
  91.7 5.1 %collective-permute-start.10 = (bf16[2,32,2,16,128]{4,3,2,1,0:T(8,128)(2,1)S(1)}, bf16[2,32,2,16,128]{4,3,2,1,0:T(8,128)(2,1)S(1)}, u32[]{:S(2)}, u32[]{:S(2)}) collective-permute-start(bf16[2,32,2,16,128]{4,3,2,1,0:T(8,128)(2,1)S(1)} %pad_maximum_fusion.3), channel_id=1, source_target_pairs={{0,4},{2,6},{4,0},{6,2},{1,5},{3,7},{5,1},{7,3},{8,12},{10,14},{12... | collective-permute-start | bytes 1572872 | tf_op jit(solution)/shard_map/ppermute | solution.py:461
  96.8 15.5 %channelise.3 = (bf16[2048,128]{1,0:T(8,128)(2,1)S(1)}, bf16[2048,128]{1,0:T(8,128)(2,1)S(1)}, bf16[2048,128]{1,0:T(8,128)(2,1)S(1)}, bf16[2048,128]{1,0:T(8,128)(2,1)S(1)}) custom-call(s32[3]{0:T(128)S(1)} %pad_add_fusion.refs_0_, bf16[2,128,8192]{2,1,0:T(8,128)(2,1)S(1)} %bitcast.69, bf16[2,16,8192]{2,1,0:T(8,128)(2,1)S(1)} %collective-permute-done.5.refs_2_, ...), custom_call_target="tpu_custom_call" | custom-call | flops 8999999488 | bytes 4194304 | tf_op jit(solution)/shard_map/channelise/pallas_call | solution.py:276
  115.2 5.6 %collective-permute-done.9 = bf16[64,2,16,128]{3,2,1,0:T(8,128)(2,1)S(1)} collective-permute-done((bf16[64,2,16,128]{3,2,1,0:T(8,128)(2,1)S(1)}, bf16[64,2,16,128]{3,2,1,0:T(8,128)(2,1)S(1)}, u32[]{:S(2)}, u32[]{:S(2)}) %collective-permute-start.9) | collective-permute-done | bytes 524320 | tf_op jit(solution)/shard_map/ppermute | solution.py:461
  120.9 16.9 %collective-permute-done.11 = bf16[2,32,2,16,128]{4,3,2,1,0:T(8,128)(2,1)S(1)} collective-permute-done((bf16[2,32,2,16,128]{4,3,2,1,0:T(8,128)(2,1)S(1)}, bf16[2,32,2,16,128]{4,3,2,1,0:T(8,128)(2,1)S(1)}, u32[]{:S(2)}, u32[]{:S(2)}) %collective-permute-start.11) | collective-permute-done | bytes 524320 | tf_op jit(solution)/shard_map/ppermute | solution.py:461
  138.2 16.2 %collective-permute-start.16 = (bf16[8,32,2,16,128]{4,3,2,1,0:T(8,128)(2,1)S(1)}, bf16[8,32,2,16,128]{4,3,2,1,0:T(8,128)(2,1)S(1)}, u32[]{:S(2)}, u32[]{:S(2)}) collective-permute-start(bf16[8,32,2,16,128]{4,3,2,1,0:T(8,128)(2,1)S(1)} %bitcast.62), channel_id=1, source_target_pairs={{0,1},{1,0},{2,3},{3,2},{4,5},{5,4},{6,7},{7,6},{8,9},{9,8},{10,11... | collective-permute-start | bytes 6291464 | tf_op jit(solution)/shard_map/ppermute | solution.py:461
  154.9 3.1 %collective-permute-start.13 = (bf16[2,16,2,16,128]{4,3,2,1,0:T(8,128)(2,1)S(1)}, bf16[2,16,2,16,128]{4,3,2,1,0:T(8,128)(2,1)S(1)}, u32[]{:S(2)}, u32[]{:S(2)}) collective-permute-start(bf16[2,16,2,16,128]{4,3,2,1,0:T(8,128)(2,1)S(1)} %pad_maximum_fusion.6), channel_id=1, source_target_pairs={{0,4},{2,6},{4,0},{6,2},{1,5},{3,7},{5,1},{7,3},{8,12},{10,14},{12... | collective-permute-start | bytes 786440 | tf_op jit(solution)/shard_map/ppermute | solution.py:461
  158.1 9.8 %collective-permute-done.12 = bf16[64,2,16,128]{3,2,1,0:T(8,128)(2,1)S(1)} collective-permute-done((bf16[64,2,16,128]{3,2,1,0:T(8,128)(2,1)S(1)}, bf16[64,2,16,128]{3,2,1,0:T(8,128)(2,1)S(1)}, u32[]{:S(2)}, u32[]{:S(2)}) %collective-permute-start.12) | collective-permute-done | bytes 524320 | tf_op jit(solution)/shard_map/ppermute | solution.py:461
  168.0 12.5 %collective-permute-done.14 = bf16[2,16,2,16,128]{4,3,2,1,0:T(8,128)(2,1)S(1)} collective-permute-done((bf16[2,16,2,16,128]{4,3,2,1,0:T(8,128)(2,1)S(1)}, bf16[2,16,2,16,128]{4,3,2,1,0:T(8,128)(2,1)S(1)}, u32[]{:S(2)}, u32[]{:S(2)}) %collective-permute-start.14) | collective-permute-done | bytes 262176 | tf_op jit(solution)/shard_map/ppermute | solution.py:461
  180.6 8.3 %collective-permute-done.15 = bf16[2,16,2,16,128]{4,3,2,1,0:T(8,128)(2,1)S(1)} collective-permute-done((bf16[2,16,2,16,128]{4,3,2,1,0:T(8,128)(2,1)S(1)}, bf16[2,16,2,16,128]{4,3,2,1,0:T(8,128)(2,1)S(1)}, u32[]{:S(2)}, u32[]{:S(2)}) %collective-permute-start.15) | collective-permute-done | bytes 262176 | tf_op jit(solution)/shard_map/ppermute | solution.py:461
  190.2 1.5 collective-permute-start.17
  193.0 13.1 %correlate.2.refs_13_ = f32[8,32,2,2,64,128]{5,4,3,2,1,0:T(8,128)} custom-call(s32[3]{0:T(128)S(1)} %pad_add_fusion.refs_0_, bf16[1024,256]{1,0:T(8,128)(2,1)S(1)} %fusion.refs_1_, f32[8,256]{1,0:T(8,128)S(1)} %tile.10.refs_2_, bf16[8,32,2,16,128]{4,3,2,1,0:T(8,128)(2,1)S(1)} %bitcast.63, bf16[8,32,2,16,128]{4,3,2,1,0:T(8,128)(2,1)S(1)} %collective-permute-done.16.refs_4_, ...), custom_call_target="tpu_custom_call" | custom-call | flops 6499999744 | bytes 22020096 | tf_op jit(solution)/shard_map/correlate/pallas_call | solution.py:384
  206.1 8.2 %collective-permute-done.18.refs_9_ = bf16[2,16,2,16,128]{4,3,2,1,0:T(8,128)(2,1)S(1)} collective-permute-done((bf16[2,16,2,16,128]{4,3,2,1,0:T(8,128)(2,1)S(1)}, bf16[2,16,2,16,128]{4,3,2,1,0:T(8,128)(2,1)S(1)}, u32[]{:S(2)}, u32[]{:S(2)}) %collective-permute-start.18) | collective-permute-done | bytes 262176 | tf_op jit(solution)/shard_map/ppermute | solution.py:461
  218.0 14.5 %correlate.3 = f32[8,32,2,2,64,128]{5,4,3,2,1,0:T(8,128)} custom-call(s32[3]{0:T(128)S(1)} %pad_add_fusion.refs_0_, bf16[1024,256]{1,0:T(8,128)(2,1)S(1)} %fusion.refs_1_, f32[8,256]{1,0:T(8,128)S(1)} %tile.10.refs_2_, bf16[8,32,2,16,128]{4,3,2,1,0:T(8,128)(2,1)S(1)} %bitcast.64, ...), custom_call_target="tpu_custom_call", output_to_operand_aliasing={{}: (13, {})} | custom-call | flops 6499999744 | bytes 22020096 | tf_op jit(solution)/shard_map/correlate/pallas_call | solution.py:384
  (89 shorter events, 21.4 us)
Async XLA Ops:
  1.1 12.8 %collective-permute-start = (bf16[2,16,8192]{2,1,0:T(8,128)(2,1)S(1)}, bf16[2,16,8192]{2,1,0:T(8,128)(2,1)S(1)}, u32[]{:S(2)}, u32[]{:S(2)}) collective-permute-start(bf16[2,16,8192]{2,1,0:T(8,128)(2,1)S(1)} %dynamic-slice_bitcast_fusion), channel_id=1, source_target_pairs={{0,2},{2,4},{4,6},{6,0},{1,3},{3,5},{5,7},{7,1},{8,10},{10,12},{12... | collective-permute-start | bytes 1572872 | tf_op jit(solution)/shard_map/ppermute | solution.py:461
  5.4 41.4 %collective-permute-start.1 = (bf16[2,16,8192]{2,1,0:T(8,128)(2,1)S(1)}, bf16[2,16,8192]{2,1,0:T(8,128)(2,1)S(1)}, u32[]{:S(2)}, u32[]{:S(2)}) collective-permute-start(bf16[2,16,8192]{2,1,0:T(8,128)(2,1)S(1)} %get-tuple-element.107), channel_id=1, source_target_pairs={{0,4},{2,6},{4,0},{6,2},{1,5},{3,7},{5,1},{7,3},{8,12},{10,14},{12... | collective-permute-start | bytes 1572872 | tf_op jit(solution)/shard_map/ppermute | solution.py:461
  13.9 33.9 %collective-permute-start.2 = (bf16[2,16,8192]{2,1,0:T(8,128)(2,1)S(1)}, bf16[2,16,8192]{2,1,0:T(8,128)(2,1)S(1)}, u32[]{:S(2)}, u32[]{:S(2)}) collective-permute-start(bf16[2,16,8192]{2,1,0:T(8,128)(2,1)S(1)} %get-tuple-element.58), channel_id=1, source_target_pairs={{0,6},{2,0},{4,2},{6,4},{1,7},{3,1},{5,3},{7,5},{8,14},{10,8},{12,... | collective-permute-start | bytes 1572872 | tf_op jit(solution)/shard_map/ppermute | solution.py:461
  47.5 11.9 %collective-permute-start.5 = (bf16[2,16,8192]{2,1,0:T(8,128)(2,1)S(1)}, bf16[2,16,8192]{2,1,0:T(8,128)(2,1)S(1)}, u32[]{:S(2)}, u32[]{:S(2)}) collective-permute-start(bf16[2,16,8192]{2,1,0:T(8,128)(2,1)S(1)} %get-tuple-element.68), channel_id=1, source_target_pairs={{0,2},{2,4},{4,6},{6,0},{1,3},{3,5},{5,7},{7,1},{8,10},{10,12},{12... | collective-permute-start | bytes 1572872 | tf_op jit(solution)/shard_map/ppermute | solution.py:461
  47.8 35.9 %collective-permute-start.3 = (bf16[2,16,8192]{2,1,0:T(8,128)(2,1)}, bf16[2,16,8192]{2,1,0:T(8,128)(2,1)S(1)}, u32[]{:S(2)}, u32[]{:S(2)}) collective-permute-start(bf16[2,16,8192]{2,1,0:T(8,128)(2,1)} %get-tuple-element.61), channel_id=1, source_target_pairs={{0,4},{2,6},{4,0},{6,2},{1,5},{3,7},{5,1},{7,3},{8,12},{10,14},{12... | collective-permute-start | bytes 1572872 | tf_op jit(solution)/shard_map/ppermute | solution.py:461
  79.7 8.4 %collective-permute-start.6 = (bf16[64,2,16,128]{3,2,1,0:T(8,128)(2,1)}, bf16[64,2,16,128]{3,2,1,0:T(8,128)(2,1)}, u32[]{:S(2)}, u32[]{:S(2)}) collective-permute-start(bf16[64,2,16,128]{3,2,1,0:T(8,128)(2,1)} %bitcast.11), channel_id=1, source_target_pairs={{0,8},{8,0},{1,9},{9,1},{2,10},{10,2},{3,11},{11,3},{4,12},{12,4},... | collective-permute-start | bytes 1572872 | tf_op jit(solution)/shard_map/ppermute | solution.py:461
  80.4 10.5 %collective-permute-start.7 = (bf16[2,16,8192]{2,1,0:T(8,128)(2,1)}, bf16[2,16,8192]{2,1,0:T(8,128)(2,1)S(1)}, u32[]{:S(2)}, u32[]{:S(2)}) collective-permute-start(bf16[2,16,8192]{2,1,0:T(8,128)(2,1)} %get-tuple-element.74), channel_id=1, source_target_pairs={{0,6},{2,0},{4,2},{6,4},{1,7},{3,1},{5,3},{7,5},{8,14},{10,8},{12,... | collective-permute-start | bytes 1572872 | tf_op jit(solution)/shard_map/ppermute | solution.py:461
  83.7 28.6 %collective-permute-start.4 = (bf16[64,2,16,128]{3,2,1,0:T(8,128)(2,1)S(1)}, bf16[64,2,16,128]{3,2,1,0:T(8,128)(2,1)S(1)}, u32[]{:S(2)}, u32[]{:S(2)}) collective-permute-start(bf16[64,2,16,128]{3,2,1,0:T(8,128)(2,1)S(1)} %bitcast.71), channel_id=1, source_target_pairs={{0,8},{8,0},{1,9},{9,1},{2,10},{10,2},{3,11},{11,3},{4,12},{12,4},... | collective-permute-start | bytes 1572872 | tf_op jit(solution)/shard_map/ppermute | solution.py:461
  91.0 21.5 %collective-permute-start.8 = (bf16[2,32,2,16,128]{4,3,2,1,0:T(8,128)(2,1)S(1)}, bf16[2,32,2,16,128]{4,3,2,1,0:T(8,128)(2,1)S(1)}, u32[]{:S(2)}, u32[]{:S(2)}) collective-permute-start(bf16[2,32,2,16,128]{4,3,2,1,0:T(8,128)(2,1)S(1)} %pad_maximum_fusion.2), channel_id=1, source_target_pairs={{0,2},{2,4},{4,6},{6,0},{1,3},{3,5},{5,7},{7,1},{8,10},{10,12},{12... | collective-permute-start | bytes 1572872 | tf_op jit(solution)/shard_map/ppermute | solution.py:461
  91.7 23.5 %collective-permute-start.10 = (bf16[2,32,2,16,128]{4,3,2,1,0:T(8,128)(2,1)S(1)}, bf16[2,32,2,16,128]{4,3,2,1,0:T(8,128)(2,1)S(1)}, u32[]{:S(2)}, u32[]{:S(2)}) collective-permute-start(bf16[2,32,2,16,128]{4,3,2,1,0:T(8,128)(2,1)S(1)} %pad_maximum_fusion.3), channel_id=1, source_target_pairs={{0,4},{2,6},{4,0},{6,2},{1,5},{3,7},{5,1},{7,3},{8,12},{10,14},{12... | collective-permute-start | bytes 1572872 | tf_op jit(solution)/shard_map/ppermute | solution.py:461
  112.5 8.4 %collective-permute-start.9 = (bf16[64,2,16,128]{3,2,1,0:T(8,128)(2,1)S(1)}, bf16[64,2,16,128]{3,2,1,0:T(8,128)(2,1)S(1)}, u32[]{:S(2)}, u32[]{:S(2)}) collective-permute-start(bf16[64,2,16,128]{3,2,1,0:T(8,128)(2,1)S(1)} %bitcast.72), channel_id=1, source_target_pairs={{0,8},{8,0},{1,9},{9,1},{2,10},{10,2},{3,11},{11,3},{4,12},{12,4},... | collective-permute-start | bytes 1572872 | tf_op jit(solution)/shard_map/ppermute | solution.py:461
  113.8 24.1 %collective-permute-start.11 = (bf16[2,32,2,16,128]{4,3,2,1,0:T(8,128)(2,1)S(1)}, bf16[2,32,2,16,128]{4,3,2,1,0:T(8,128)(2,1)S(1)}, u32[]{:S(2)}, u32[]{:S(2)}) collective-permute-start(bf16[2,32,2,16,128]{4,3,2,1,0:T(8,128)(2,1)S(1)} %pad_maximum_fusion.4), channel_id=1, source_target_pairs={{0,6},{2,0},{4,2},{6,4},{1,7},{3,1},{5,3},{7,5},{8,14},{10,8},{12,... | collective-permute-start | bytes 1572872 | tf_op jit(solution)/shard_map/ppermute | solution.py:461
  138.2 50.8 %collective-permute-start.16 = (bf16[8,32,2,16,128]{4,3,2,1,0:T(8,128)(2,1)S(1)}, bf16[8,32,2,16,128]{4,3,2,1,0:T(8,128)(2,1)S(1)}, u32[]{:S(2)}, u32[]{:S(2)}) collective-permute-start(bf16[8,32,2,16,128]{4,3,2,1,0:T(8,128)(2,1)S(1)} %bitcast.62), channel_id=1, source_target_pairs={{0,1},{1,0},{2,3},{3,2},{4,5},{5,4},{6,7},{7,6},{8,9},{9,8},{10,11... | collective-permute-start | bytes 6291464 | tf_op jit(solution)/shard_map/ppermute | solution.py:461
  154.4 13.5 %collective-permute-start.12 = (bf16[64,2,16,128]{3,2,1,0:T(8,128)(2,1)S(1)}, bf16[64,2,16,128]{3,2,1,0:T(8,128)(2,1)S(1)}, u32[]{:S(2)}, u32[]{:S(2)}) collective-permute-start(bf16[64,2,16,128]{3,2,1,0:T(8,128)(2,1)S(1)} %bitcast.70), channel_id=1, source_target_pairs={{0,8},{8,0},{1,9},{9,1},{2,10},{10,2},{3,11},{11,3},{4,12},{12,4},... | collective-permute-start | bytes 1572872 | tf_op jit(solution)/shard_map/ppermute | solution.py:461
  154.9 25.7 %collective-permute-start.13 = (bf16[2,16,2,16,128]{4,3,2,1,0:T(8,128)(2,1)S(1)}, bf16[2,16,2,16,128]{4,3,2,1,0:T(8,128)(2,1)S(1)}, u32[]{:S(2)}, u32[]{:S(2)}) collective-permute-start(bf16[2,16,2,16,128]{4,3,2,1,0:T(8,128)(2,1)S(1)} %pad_maximum_fusion.6), channel_id=1, source_target_pairs={{0,4},{2,6},{4,0},{6,2},{1,5},{3,7},{5,1},{7,3},{8,12},{10,14},{12... | collective-permute-start | bytes 786440 | tf_op jit(solution)/shard_map/ppermute | solution.py:461
  158.0 22.5 %collective-permute-start.14 = (bf16[2,16,2,16,128]{4,3,2,1,0:T(8,128)(2,1)S(1)}, bf16[2,16,2,16,128]{4,3,2,1,0:T(8,128)(2,1)S(1)}, u32[]{:S(2)}, u32[]{:S(2)}) collective-permute-start(bf16[2,16,2,16,128]{4,3,2,1,0:T(8,128)(2,1)S(1)} %pad_maximum_fusion.5), channel_id=1, source_target_pairs={{0,2},{2,4},{4,6},{6,0},{1,3},{3,5},{5,7},{7,1},{8,10},{10,12},{12... | collective-permute-start | bytes 786440 | tf_op jit(solution)/shard_map/ppermute | solution.py:461
  180.5 8.5 %collective-permute-start.15 = (bf16[2,16,2,16,128]{4,3,2,1,0:T(8,128)(2,1)S(1)}, bf16[2,16,2,16,128]{4,3,2,1,0:T(8,128)(2,1)S(1)}, u32[]{:S(2)}, u32[]{:S(2)}) collective-permute-start(bf16[2,16,2,16,128]{4,3,2,1,0:T(8,128)(2,1)S(1)} %pad_maximum_fusion.10), channel_id=1, source_target_pairs={{0,6},{2,0},{4,2},{6,4},{1,7},{3,1},{5,3},{7,5},{8,14},{10,8},{12,... | collective-permute-start | bytes 786440 | tf_op jit(solution)/shard_map/ppermute | solution.py:461
  189.1 3.9 %collective-permute-start.20 = (bf16[8,16,2,16,128]{4,3,2,1,0:T(8,128)(2,1)S(1)}, bf16[8,16,2,16,128]{4,3,2,1,0:T(8,128)(2,1)S(1)}, u32[]{:S(2)}, u32[]{:S(2)}) collective-permute-start(bf16[8,16,2,16,128]{4,3,2,1,0:T(8,128)(2,1)S(1)} %bitcast.65), channel_id=1, source_target_pairs={{0,1},{1,0},{2,3},{3,2},{4,5},{5,4},{6,7},{7,6},{8,9},{9,8},{10,11... | collective-permute-start | bytes 3145736 | tf_op jit(solution)/shard_map/ppermute | solution.py:461
  190.2 15.9 %collective-permute-start.17 = (bf16[2,16,2,16,128]{4,3,2,1,0:T(8,128)(2,1)S(1)}, bf16[2,16,2,16,128]{4,3,2,1,0:T(8,128)(2,1)S(1)}, u32[]{:S(2)}, u32[]{:S(2)}) collective-permute-start(bf16[2,16,2,16,128]{4,3,2,1,0:T(8,128)(2,1)S(1)} %pad_maximum_fusion.7), channel_id=1, source_target_pairs={{0,2},{2,4},{4,6},{6,0},{1,3},{3,5},{5,7},{7,1},{8,10},{10,12},{12... | collective-permute-start | bytes 786440 | tf_op jit(solution)/shard_map/ppermute | solution.py:461
  191.7 22.6 %collective-permute-start.18 = (bf16[2,16,2,16,128]{4,3,2,1,0:T(8,128)(2,1)S(1)}, bf16[2,16,2,16,128]{4,3,2,1,0:T(8,128)(2,1)S(1)}, u32[]{:S(2)}, u32[]{:S(2)}) collective-permute-start(bf16[2,16,2,16,128]{4,3,2,1,0:T(8,128)(2,1)S(1)} %pad_maximum_fusion.8), channel_id=1, source_target_pairs={{0,4},{2,6},{4,0},{6,2},{1,5},{3,7},{5,1},{7,3},{8,12},{10,14},{12... | collective-permute-start | bytes 786440 | tf_op jit(solution)/shard_map/ppermute | solution.py:461
  191.7 23.6 %collective-permute-start.19 = (bf16[2,16,2,16,128]{4,3,2,1,0:T(8,128)(2,1)S(1)}, bf16[2,16,2,16,128]{4,3,2,1,0:T(8,128)(2,1)S(1)}, u32[]{:S(2)}, u32[]{:S(2)}) collective-permute-start(bf16[2,16,2,16,128]{4,3,2,1,0:T(8,128)(2,1)S(1)} %pad_maximum_fusion.9), channel_id=1, source_target_pairs={{0,6},{2,0},{4,2},{6,4},{1,7},{3,1},{5,3},{7,5},{8,14},{10,8},{12,... | collective-permute-start | bytes 786440 | tf_op jit(solution)/shard_map/ppermute | solution.py:461
  215.3 1.6 collective-permute-start.21
  215.8 1.9 collective-permute-start.23
  216.3 1.8 collective-permute-start.24
  (11 other events, 196.5 us)

commit v3 on v2

--- a/solution.py
+++ b/solution.py
@@ -472,74 +472,65 @@
             place, chunk, samples, arrived, taps_filter, tables, frames, chan_count, plan
         )
 
-    sent = []
-
-    def over_tm(value, distance, guard):
-        if guard <= len(sent):
-            (value,), sent[-guard : len(sent) - guard + 1] = after([value], [sent[-guard]])
-        sent.append(travel(value, ("tm",), (distance,)))
-
-    def over_chan(values, guard):
-        values, sent[guard : guard + 1] = after(values, [sent[guard]])
-        return [travel(v, ("chan",), (1,)) for v in values]
+    def over(value, across, along):
+        return travel(value, ("chan", "tm"), (across, along))
 
     def columns(near, far):
         return jnp.stack([near, far])
 
-    hops = range(1, time_count)
     half = bands // 2
-    spans = [(0, half), (half, bands)]
-
-    values = samples
-    for distance in hops:
-        block = block_for(values, 0, distance)
-        over_tm(block, distance, 2)
-        if distance == 1:
-            (block,), (values,) = after([block], [samples])
-    for distance in hops:
-        over_tm(block_for(values, 1, distance), distance, 2)
-
-    order = [1, 2, 3, 0]
-    plan = [[(x, z, 0, bands) for z in order] for x in range(chan_count)]
-    plan = plan[:1] + [plan[1][:2], plan[1][2:]]
-    near, *far = filtered(0, sent[:3], plan)
-    near = near.reshape(time_count, bands, 2, ROWS, LANES)
-    far = over_chan(far[:1], 3) + over_chan(far[1:], 4)
-    far = [v.reshape(2, bands, 2, ROWS, LANES) for v in far]
-    mixed = {z: columns(near[i], far[i // 2][i % 2]) for i, z in enumerate(order)}
-    sent[4:5], (select, weight) = after([sent[4]], [select, weight])
-    for distance in hops:
-        over_tm(mixed[distance], distance, 2)
-    home = mixed[0]
-
-    plan = [[(x, z, *span) for z in range(time_count)] for span in spans for x in range(2)]
-    low, far_low, high, far_high = filtered(1, sent[3:6], plan)
-    far = over_chan([far_low], 6) + over_chan([far_high], 7)
-    shape = (time_count, half, 2, ROWS, LANES)
-    low, high, far_low, far_high = (v.reshape(shape) for v in (low, high, *far))
-    low = [columns(low[z], far_low[z]) for z in range(time_count)]
-    high = [columns(high[z], far_high[z]) for z in range(time_count)]
-    for distance in hops:
-        over_tm(low[distance], distance, 2)
-
-    def flat(values):
-        return jnp.stack(values).reshape((-1,) + values[0].shape[1:])
+    pairs = [(x, z) for z in range(time_count) for x in range(chan_count)]
+    early_pairs = [(x, z) for z in (1, 3) for x in range(2)] + [(1, 0)]
+    late_pairs = [(0, 2), (1, 2)]
+
+    (one,), (values,) = after([block_for(samples, 0, 1)], [samples])
+    two, three = (block_for(values, 0, distance) for distance in (2, 3))
+    one, two = over(one, 0, 1), over(two, 0, 2)
+    (three,), (one,) = after([three], [one])
+    first = [one, two, over(three, 0, 3)]
+    blocks = [block_for(values, 1, distance) for distance in (1, 2, 3)]
+    (one, two, three), first = after(blocks, first)
+    one, three = over(one, 0, 1), over(three, 0, 3)
+    (two,), (one,) = after([two], [one])
+    second = [one, over(two, 0, 2), three]
+
+    plan = [[(x, z, 0, bands)] for x, z in pairs]
+    early = dict(zip(pairs, filtered(0, first, plan)))
+    blocks, held = after([early[p] for p in early_pairs], [second[1], select, weight])
+    second[1], select, weight = held
+    early.update((p, over(block, *p)) for p, block in zip(early_pairs, blocks))
+    blocks, held = after([early[p] for p in late_pairs], [early[p] for p in early_pairs[:2]])
+    early.update(zip(early_pairs[:2], held))
+    early.update((p, over(block, *p)) for p, block in zip(late_pairs, blocks))
+
+    plan = [[(x, z, 0, half)] for x, z in pairs]
+    plan += [[(x, z, half, bands) for z in range(time_count)] for x in range(chan_count)]
+    *low, near, far = filtered(1, second, plan)
+    low = dict(zip(pairs, low))
+    blocks, held = after([low[p] for p in early_pairs] + [far], [early[p] for p in late_pairs[:1]])
+    early.update(zip(late_pairs[:1], held))
+    low.update((p, over(block, *p)) for p, block in zip(early_pairs, blocks))
+    far = over(blocks[-1], 1, 0)
+    blocks, held = after([low[p] for p in late_pairs], [low[p] for p in early_pairs[:2]])
+    low.update(zip(early_pairs[:2], held))
+    low.update((p, over(block, *p)) for p, block in zip(late_pairs, blocks))
+    near, far = (v.reshape(time_count, half, 2, ROWS, LANES) for v in (near, far))
+    high = [columns(near[z], far[z]) for z in range(time_count)]
 
     def with_other(values):
         return [side for v in values for side in (v, travel(v, ("pol",), (1,)))]
 
-    early = with_other([flat([home] + sent[6:9])])
-    blocks, held = after(high[1:], sent[10:12] + early[1:])
-    sent[10:12], early[1:] = held[:2], held[2:]
-    for distance, block in zip(hops, blocks):
-        over_tm(block, distance, len(sent) + 1)
+    early = with_other([jnp.stack([early[p] for p in pairs])])
+    blocks, held = after(high[1:], [low[late_pairs[0]], early[1]])
+    low[late_pairs[0]], early[1] = held
+    high[1:] = [over(block, 0, z) for z, block in zip((1, 2, 3), blocks)]
     visibility = correlate_tiles(
-        place, select, weight, early + with_other([flat([low[0]] + sent[9:12])]),
+        place, select, weight, early + with_other([jnp.stack([low[p] for p in pairs])]),
         [0, 0], width, 0, half, bands, None,
     )
-    last, (visibility,) = after([high[0]] + sent[12:15], [visibility])
+    high, (visibility,) = after(high, [visibility])
     return correlate_tiles(
-        place, select, weight, early + with_other(last),
+        place, select, weight, early + with_other(high),
         [half] + [0] * 4, width, half, half, bands, visibility,
     )
 

time: 234 us -> 227 us (0.970)
  waiting for transfers between devices: 114 us -> 109 us
  starting transfers between devices: 45.7 us -> 50.2 us
  local copies, waits for them, and re-layouts: 10.3 us -> 6.96 us
    ppermute x25 -> x30, waiting for transfers between devices: 114 us -> 109 us  [travel(): return lax.ppermute(value, axes, pairs)]
    ppermute x25 -> x30, starting transfers between devices: 45.7 us -> 50.2 us  [travel(): return lax.ppermute(value, axes, pairs)]
    unnamed x20 -> x32, local copies, waits for them, and re-layouts: 4.78 us -> 2.58 us
  transfers between devices with their start and end apart: 25 -> 30, of which waited for: 16 -> 15; matrix products, arithmetic and copies ran while one was open for 3% -> 2% of each run, Pallas kernels for 19% -> 20%
where the time goes in v3:
time: 227 us; the launch traced here: 226 us
  waiting for transfers between devices  109 us (48%)
  Pallas kernels  58.8 us (26%)
  starting transfers between devices  50.2 us (22%)
  local copies, waits for them, and re-layouts  6.96 us (3%)
    ppermute x30, waiting for transfers between devices, travel(): return lax.ppermute(value, axes, pairs)  109 us
    ppermute x30, starting transfers between devices, travel(): return lax.ppermute(value, axes, pairs)  50.2 us
    pallas_call x2, Pallas kernels, channelise(): pl.pallas_call(lambda *refs: channelise_kernel(frames, chunk, columns, pl...  31.1 us
    pallas_call x2, Pallas kernels, correlate_tiles(): pl.pallas_call(lambda *refs: correlate_kernel(starts, width, *refs), grid...  27.7 us
  transfers between devices with their start and end apart: 30, of which 15 were waited for; matrix products, arithmetic and copies ran while one was open for 2% of the time, Pallas kernels for 20%

profile of v3, /device:TPU:11, one launch (start us, length us, event | category | flops | bytes accessed | tf_op | source)
XLA Modules:
  0.0 225.8 jit_solution(12563018292257658387)
XLA Ops:
  2.5 3.0 %constant_dynamic-slice_fusion = (bf16[2,16,8192]{2,1,0:T(8,128)(2,1)}, bf16[2,16,8192]{2,1,0:T(8,128)(2,1)S(1)}, bf16[2,16,8192]{2,1,0:T(8,128)(2,1)S(1)}, bf16[2,16,8192]{2,1,0:T(8,128)(2,1)}, bf16[2,16,8192]{2,1,0:T(8,128)(2,1)}) fusion(bf16[2,128,8192]{2,1,0:T(8,128)(2,1)} %bitcast.67, s32[]{:T(128)S(6)} %select_n.109, s32[]{:T(128)S(6)} %select_n.108, ...), kind=kLoop, calls=%fused_computation.124 | loop fusion | bytes 5242900 | tf_op jit(solution)/shard_map/dynamic_slice | solution.py:468
  6.8 7.1 %collective-permute-done.refs_2_ = bf16[2,16,8192]{2,1,0:T(8,128)(2,1)S(1)} collective-permute-done((bf16[2,16,8192]{2,1,0:T(8,128)(2,1)S(1)}, bf16[2,16,8192]{2,1,0:T(8,128)(2,1)S(1)}, u32[]{:S(2)}, u32[]{:S(2)}) %collective-permute-start) | collective-permute-done | bytes 524320 | tf_op jit(solution)/shard_map/ppermute | solution.py:461
  16.4 30.5 %collective-permute-done.1.refs_3_ = bf16[2,16,8192]{2,1,0:T(8,128)(2,1)S(1)} collective-permute-done((bf16[2,16,8192]{2,1,0:T(8,128)(2,1)}, bf16[2,16,8192]{2,1,0:T(8,128)(2,1)S(1)}, u32[]{:S(2)}, u32[]{:S(2)}) %collective-permute-start.1) | collective-permute-done | bytes 524320 | tf_op jit(solution)/shard_map/ppermute | solution.py:461
  48.8 8.5 %collective-permute-done.3.refs_2_ = bf16[2,16,8192]{2,1,0:T(8,128)(2,1)S(1)} collective-permute-done((bf16[2,16,8192]{2,1,0:T(8,128)(2,1)}, bf16[2,16,8192]{2,1,0:T(8,128)(2,1)S(1)}, u32[]{:S(2)}, u32[]{:S(2)}) %collective-permute-start.3) | collective-permute-done | bytes 524320 | tf_op jit(solution)/shard_map/ppermute | solution.py:461
  57.3 6.7 %collective-permute-start.4 = (bf16[2,16,8192]{2,1,0:T(8,128)(2,1)}, bf16[2,16,8192]{2,1,0:T(8,128)(2,1)S(1)}, u32[]{:S(2)}, u32[]{:S(2)}) collective-permute-start(bf16[2,16,8192]{2,1,0:T(8,128)(2,1)} %get-tuple-element.82), channel_id=1, source_target_pairs={{0,4},{2,6},{4,0},{6,2},{8,12},{10,14},{12,8},{14,10},{1,5},{3,7},... | collective-permute-start | bytes 1572872 | tf_op jit(solution)/shard_map/ppermute | solution.py:461
  66.2 15.5 %channelise.2 = (bf16[1024,128]{1,0:T(8,128)(2,1)S(1)}, bf16[1024,128]{1,0:T(8,128)(2,1)S(1)}, bf16[1024,128]{1,0:T(8,128)(2,1)S(1)}, bf16[1024,128]{1,0:T(8,128...) custom-call(s32[3]{0:T(128)S(1)} %pad_add_fusion.refs_0_, ...), custom_call_target="tpu_custom_call" | custom-call | flops 8999999488 | bytes 4194304 | tf_op jit(solution)/shard_map/channelise/pallas_call | solution.py:276
  81.7 12.0 %collective-permute-done.4.refs_3_ = bf16[2,16,8192]{2,1,0:T(8,128)(2,1)S(1)} collective-permute-done((bf16[2,16,8192]{2,1,0:T(8,128)(2,1)}, bf16[2,16,8192]{2,1,0:T(8,128)(2,1)S(1)}, u32[]{:S(2)}, u32[]{:S(2)}) %collective-permute-start.4) | collective-permute-done | bytes 524320 | tf_op jit(solution)/shard_map/ppermute | solution.py:461
  95.8 2.4 %collective-permute-start.7 = (bf16[32,2,16,128]{3,2,1,0:T(8,128)(2,1)S(1)}, bf16[32,2,16,128]{3,2,1,0:T(8,128)(2,1)S(1)}, u32[]{:S(2)}, u32[]{:S(2)}) collective-permute-start(bf16[32,2,16,128]{3,2,1,0:T(8,128)(2,1)S(1)} %bitcast.78), channel_id=1, source_target_pairs={{0,10},{2,12},{4,14},{6,8},{8,2},{10,4},{12,6},{14,0},{1,11},{3,13... | collective-permute-start | bytes 786440 | tf_op jit(solution)/shard_map/ppermute | solution.py:461
  98.2 3.6 %collective-permute-start.12 = (bf16[32,2,16,128]{3,2,1,0:T(8,128)(2,1)S(1)}, bf16[32,2,16,128]{3,2,1,0:T(8,128)(2,1)S(1)}, u32[]{:S(2)}, u32[]{:S(2)}) collective-permute-start(bf16[32,2,16,128]{3,2,1,0:T(8,128)(2,1)S(1)} %bitcast.73), channel_id=1, source_target_pairs={{0,14},{2,8},{4,10},{6,12},{8,6},{10,0},{12,2},{14,4},{1,15},{3,9}... | collective-permute-start | bytes 786440 | tf_op jit(solution)/shard_map/ppermute | solution.py:461
  101.8 15.5 %channelise.3 = (bf16[512,128]{1,0:T(8,128)(2,1)S(1)}, bf16[512,128]{1,0:T(8,128)(2,1)S(1)}, bf16[512,128]{1,0:T(8,128)(2,1)S(1)}, bf16[512,128]{1,0:T(8,128)(2,...) custom-call(s32[3]{0:T(128)S(1)} %pad_add_fusion.refs_0_, ...), custom_call_target="tpu_custom_call" | custom-call | flops 8999999488 | bytes 4194304 | tf_op jit(solution)/shard_map/channelise/pallas_call | solution.py:276
  117.7 3.0 %collective-permute-start.10 = (bf16[32,2,16,128]{3,2,1,0:T(8,128)(2,1)S(1)}, bf16[32,2,16,128]{3,2,1,0:T(8,128)(2,1)S(1)}, u32[]{:S(2)}, u32[]{:S(2)}) collective-permute-start(bf16[32,2,16,128]{3,2,1,0:T(8,128)(2,1)S(1)} %bitcast.75), channel_id=1, source_target_pairs={{0,12},{2,14},{4,8},{6,10},{8,4},{10,6},{12,0},{14,2},{1,13},{3,15... | collective-permute-start | bytes 786440 | tf_op jit(solution)/shard_map/ppermute | solution.py:461
  120.8 16.2 %collective-permute-done.9 = bf16[32,2,16,128]{3,2,1,0:T(8,128)(2,1)S(1)} collective-permute-done((bf16[32,2,16,128]{3,2,1,0:T(8,128)(2,1)S(1)}, bf16[32,2,16,128]{3,2,1,0:T(8,128)(2,1)S(1)}, u32[]{:S(2)}, u32[]{:S(2)}) %collective-permute-start.9) | collective-permute-done | bytes 262176 | tf_op jit(solution)/shard_map/ppermute | solution.py:461
  137.1 5.6 %collective-permute-done.10 = bf16[32,2,16,128]{3,2,1,0:T(8,128)(2,1)S(1)} collective-permute-done((bf16[32,2,16,128]{3,2,1,0:T(8,128)(2,1)S(1)}, bf16[32,2,16,128]{3,2,1,0:T(8,128)(2,1)S(1)}, u32[]{:S(2)}, u32[]{:S(2)}) %collective-permute-start.10) | collective-permute-done | bytes 262176 | tf_op jit(solution)/shard_map/ppermute | solution.py:461
  149.0 3.4 %collective-permute-done.14 = bf16[16,2,16,128]{3,2,1,0:T(8,128)(2,1)S(1)} collective-permute-done((bf16[16,2,16,128]{3,2,1,0:T(8,128)(2,1)S(1)}, bf16[16,2,16,128]{3,2,1,0:T(8,128)(2,1)S(1)}, u32[]{:S(2)}, u32[]{:S(2)}) %collective-permute-start.14) | collective-permute-done | bytes 131104 | tf_op jit(solution)/shard_map/ppermute | solution.py:461
  152.4 3.1 %collective-permute-start.24 = (bf16[16,2,16,128]{3,2,1,0:T(8,128)(2,1)S(1)}, bf16[16,2,16,128]{3,2,1,0:T(8,128)(2,1)S(1)}, u32[]{:S(2)}, u32[]{:S(2)}) collective-permute-start(bf16[16,2,16,128]{3,2,1,0:T(8,128)(2,1)S(1)} %bitcast.80), channel_id=1, source_target_pairs={{0,14},{2,8},{4,10},{6,12},{8,6},{10,0},{12,2},{14,4},{1,15},{3,9}... | collective-permute-start | bytes 393224 | tf_op jit(solution)/shard_map/ppermute | solution.py:461
  158.2 11.7 %collective-permute-done.13 = bf16[64,2,16,128]{3,2,1,0:T(8,128)(2,1)S(1)} collective-permute-done((bf16[64,2,16,128]{3,2,1,0:T(8,128)(2,1)S(1)}, bf16[64,2,16,128]{3,2,1,0:T(8,128)(2,1)S(1)}, u32[]{:S(2)}, u32[]{:S(2)}) %collective-permute-start.13) | collective-permute-done | bytes 524320 | tf_op jit(solution)/shard_map/ppermute | solution.py:461
  169.9 2.9 %collective-permute-start.22 = (bf16[16,2,16,128]{3,2,1,0:T(8,128)(2,1)S(1)}, bf16[16,2,16,128]{3,2,1,0:T(8,128)(2,1)S(1)}, u32[]{:S(2)}, u32[]{:S(2)}) collective-permute-start(bf16[16,2,16,128]{3,2,1,0:T(8,128)(2,1)S(1)} %bitcast.82), channel_id=1, source_target_pairs={{0,12},{2,14},{4,8},{6,10},{8,4},{10,6},{12,0},{14,2},{1,13},{3,15... | collective-permute-start | bytes 393224 | tf_op jit(solution)/shard_map/ppermute | solution.py:461
  173.0 2.5 %collective-permute-done.22 = bf16[16,2,16,128]{3,2,1,0:T(8,128)(2,1)S(1)} collective-permute-done((bf16[16,2,16,128]{3,2,1,0:T(8,128)(2,1)S(1)}, bf16[16,2,16,128]{3,2,1,0:T(8,128)(2,1)S(1)}, u32[]{:S(2)}, u32[]{:S(2)}) %collective-permute-start.22) | collective-permute-done | bytes 131104 | tf_op jit(solution)/shard_map/ppermute | solution.py:461
  175.7 4.0 %collective-permute-start.25 = (bf16[8,16,2,16,128]{4,3,2,1,0:T(8,128)(2,1)S(1)}, bf16[8,16,2,16,128]{4,3,2,1,0:T(8,128)(2,1)S(1)}, u32[]{:S(2)}, u32[]{:S(2)}) collective-permute-start(bf16[8,16,2,16,128]{4,3,2,1,0:T(8,128)(2,1)S(1)} %bitcast_dynamic-update-slice_fusion.7.refs_5_), channel_id=1, source_target_pairs={{0,1},{1,0},{2,3},{3,2},{4,5},{5,4},{6,7},{7,6},{8,9},{9,8},{10,11... | collective-permute-start | bytes 3145736 | tf_op jit(solution)/shard_map/ppermute | solution.py:461
  181.3 4.3 %collective-permute-start.19 = (bf16[2,16,2,16,128]{4,3,2,1,0:T(8,128)(2,1)S(1)}, bf16[2,16,2,16,128]{4,3,2,1,0:T(8,128)(2,1)S(1)}, u32[]{:S(2)}, u32[]{:S(2)}) collective-permute-start(bf16[2,16,2,16,128]{4,3,2,1,0:T(8,128)(2,1)S(1)} %pad_maximum_fusion.1), channel_id=1, source_target_pairs={{0,4},{2,6},{4,0},{6,2},{8,12},{10,14},{12,8},{14,10},{1,5},{3,7},... | collective-permute-start | bytes 786440 | tf_op jit(solution)/shard_map/ppermute | solution.py:461
  185.7 13.2 %correlate.2.refs_13_ = f32[8,32,2,2,64,128]{5,4,3,2,1,0:T(8,128)} custom-call(s32[3]{0:T(128)S(1)} %pad_add_fusion.refs_0_, bf16[1024,256]{1,0:T(8,128)(2,1)S(1)} %fusion.refs_1_, f32[8,256]{1,0:T(8,128)S(1)} %tile.10.refs_2_, bf16[8,32,2,16,128]{4,3,2,1,0:T(8,128)(2,1)S(1)} %bitcast_dynamic-update-slice_fusion.refs_3_, ...), custom_call_target="tpu_custom_call" | custom-call | flops 6499999744 | bytes 22020096 | tf_op jit(solution)/shard_map/correlate/pallas_call | solution.py:384
  198.9 5.1 %collective-permute-done.19.refs_9_ = bf16[2,16,2,16,128]{4,3,2,1,0:T(8,128)(2,1)S(1)} collective-permute-done((bf16[2,16,2,16,128]{4,3,2,1,0:T(8,128)(2,1)S(1)}, bf16[2,16,2,16,128]{4,3,2,1,0:T(8,128)(2,1)S(1)}, u32[]{:S(2)}, u32[]{:S(2)}) %collective-permute-start.19) | collective-permute-done | bytes 262176 | tf_op jit(solution)/shard_map/ppermute | solution.py:461
  204.0 4.2 %collective-permute-done.20.refs_11_ = bf16[2,16,2,16,128]{4,3,2,1,0:T(8,128)(2,1)S(1)} collective-permute-done((bf16[2,16,2,16,128]{4,3,2,1,0:T(8,128)(2,1)S(1)}, bf16[2,16,2,16,128]{4,3,2,1,0:T(8,128)(2,1)S(1)}, u32[]{:S(2)}, u32[]{:S(2)}) %collective-permute-start.20) | collective-permute-done | bytes 262176 | tf_op jit(solution)/shard_map/ppermute | solution.py:461
  211.3 14.5 %correlate.3 = f32[8,32,2,2,64,128]{5,4,3,2,1,0:T(8,128)} custom-call(s32[3]{0:T(128)S(1)} %pad_add_fusion.refs_0_, bf16[1024,256]{1,0:T(8,128)(2,1)S(1)} %fusion.refs_1_, f32[8,256]{1,0:T(8,128)S(1)} %tile.10.refs_2_, bf16[8,32,2,16,128]{4,3,2,1,0:T(8,128)(2,1)S(1)} %bitcast_dynamic-update-slice_fusion.refs_3_, ...), custom_call_target="tpu_custom_call", output_to_operand_aliasing={{}: (13, {})} | custom-call | flops 6499999744 | bytes 22020096 | tf_op jit(solution)/shard_map/correlate/pallas_call | solution.py:384
  (98 shorter events, 26.9 us)
Async XLA Ops:
  1.1 12.8 %collective-permute-start = (bf16[2,16,8192]{2,1,0:T(8,128)(2,1)S(1)}, bf16[2,16,8192]{2,1,0:T(8,128)(2,1)S(1)}, u32[]{:S(2)}, u32[]{:S(2)}) collective-permute-start(bf16[2,16,8192]{2,1,0:T(8,128)(2,1)S(1)} %dynamic-slice_bitcast_fusion), channel_id=1, source_target_pairs={{0,2},{2,4},{4,6},{6,0},{8,10},{10,12},{12,14},{14,8},{1,3},{3,5},... | collective-permute-start | bytes 1572872 | tf_op jit(solution)/shard_map/ppermute | solution.py:461
  5.5 41.4 %collective-permute-start.1 = (bf16[2,16,8192]{2,1,0:T(8,128)(2,1)}, bf16[2,16,8192]{2,1,0:T(8,128)(2,1)S(1)}, u32[]{:S(2)}, u32[]{:S(2)}) collective-permute-start(bf16[2,16,8192]{2,1,0:T(8,128)(2,1)} %get-tuple-element.131), channel_id=1, source_target_pairs={{0,4},{2,6},{4,0},{6,2},{8,12},{10,14},{12,8},{14,10},{1,5},{3,7},... | collective-permute-start | bytes 1572872 | tf_op jit(solution)/shard_map/ppermute | solution.py:461
  13.9 32.9 %collective-permute-start.2 = (bf16[2,16,8192]{2,1,0:T(8,128)(2,1)S(1)}, bf16[2,16,8192]{2,1,0:T(8,128)(2,1)S(1)}, u32[]{:S(2)}, u32[]{:S(2)}) collective-permute-start(bf16[2,16,8192]{2,1,0:T(8,128)(2,1)S(1)} %get-tuple-element.71), channel_id=1, source_target_pairs={{0,6},{2,0},{4,2},{6,4},{8,14},{10,8},{12,10},{14,12},{1,7},{3,1},... | collective-permute-start | bytes 1572872 | tf_op jit(solution)/shard_map/ppermute | solution.py:461
  46.8 10.4 %collective-permute-start.3 = (bf16[2,16,8192]{2,1,0:T(8,128)(2,1)}, bf16[2,16,8192]{2,1,0:T(8,128)(2,1)S(1)}, u32[]{:S(2)}, u32[]{:S(2)}) collective-permute-start(bf16[2,16,8192]{2,1,0:T(8,128)(2,1)} %get-tuple-element.81), channel_id=1, source_target_pairs={{0,2},{2,4},{4,6},{6,0},{8,10},{10,12},{12,14},{14,8},{1,3},{3,5},... | collective-permute-start | bytes 1572872 | tf_op jit(solution)/shard_map/ppermute | solution.py:461
  47.2 51.0 %collective-permute-start.8 = (bf16[2,16,8192]{2,1,0:T(8,128)(2,1)S(1)}, bf16[2,16,8192]{2,1,0:T(8,128)(2,1)S(1)}, u32[]{:S(2)}, u32[]{:S(2)}) collective-permute-start(bf16[2,16,8192]{2,1,0:T(8,128)(2,1)S(1)} %get-tuple-element.95), channel_id=1, source_target_pairs={{0,6},{2,0},{4,2},{6,4},{8,14},{10,8},{12,10},{14,12},{1,7},{3,1},... | collective-permute-start | bytes 1572872 | tf_op jit(solution)/shard_map/ppermute | solution.py:461
  57.3 36.5 %collective-permute-start.4 = (bf16[2,16,8192]{2,1,0:T(8,128)(2,1)}, bf16[2,16,8192]{2,1,0:T(8,128)(2,1)S(1)}, u32[]{:S(2)}, u32[]{:S(2)}) collective-permute-start(bf16[2,16,8192]{2,1,0:T(8,128)(2,1)} %get-tuple-element.82), channel_id=1, source_target_pairs={{0,4},{2,6},{4,0},{6,2},{8,12},{10,14},{12,8},{14,10},{1,5},{3,7},... | collective-permute-start | bytes 1572872 | tf_op jit(solution)/shard_map/ppermute | solution.py:461
  93.7 26.9 %collective-permute-start.5 = (bf16[32,2,16,128]{3,2,1,0:T(8,128)(2,1)S(1)}, bf16[32,2,16,128]{3,2,1,0:T(8,128)(2,1)S(1)}, u32[]{:S(2)}, u32[]{:S(2)}) collective-permute-start(bf16[32,2,16,128]{3,2,1,0:T(8,128)(2,1)S(1)} %bitcast.77), channel_id=1, source_target_pairs={{0,8},{2,10},{4,12},{6,14},{8,0},{10,2},{12,4},{14,6},{1,9},{3,11}... | collective-permute-start | bytes 786440 | tf_op jit(solution)/shard_map/ppermute | solution.py:461
  94.0 23.3 %collective-permute-start.6 = (bf16[32,2,16,128]{3,2,1,0:T(8,128)(2,1)S(1)}, bf16[32,2,16,128]{3,2,1,0:T(8,128)(2,1)S(1)}, u32[]{:S(2)}, u32[]{:S(2)}) collective-permute-start(bf16[32,2,16,128]{3,2,1,0:T(8,128)(2,1)S(1)} %bitcast.79), channel_id=1, source_target_pairs={{0,2},{2,4},{4,6},{6,0},{8,10},{10,12},{12,14},{14,8},{1,3},{3,5},... | collective-permute-start | bytes 786440 | tf_op jit(solution)/shard_map/ppermute | solution.py:461
  95.8 21.6 %collective-permute-start.7 = (bf16[32,2,16,128]{3,2,1,0:T(8,128)(2,1)S(1)}, bf16[32,2,16,128]{3,2,1,0:T(8,128)(2,1)S(1)}, u32[]{:S(2)}, u32[]{:S(2)}) collective-permute-start(bf16[32,2,16,128]{3,2,1,0:T(8,128)(2,1)S(1)} %bitcast.78), channel_id=1, source_target_pairs={{0,10},{2,12},{4,14},{6,8},{8,2},{10,4},{12,6},{14,0},{1,11},{3,13... | collective-permute-start | bytes 786440 | tf_op jit(solution)/shard_map/ppermute | solution.py:461
  98.2 44.5 %collective-permute-start.11 = (bf16[32,2,16,128]{3,2,1,0:T(8,128)(2,1)S(1)}, bf16[32,2,16,128]{3,2,1,0:T(8,128)(2,1)S(1)}, u32[]{:S(2)}, u32[]{:S(2)}) collective-permute-start(bf16[32,2,16,128]{3,2,1,0:T(8,128)(2,1)S(1)} %bitcast.74), channel_id=1, source_target_pairs={{0,6},{2,0},{4,2},{6,4},{8,14},{10,8},{12,10},{14,12},{1,7},{3,1},... | collective-permute-start | bytes 786440 | tf_op jit(solution)/shard_map/ppermute | solution.py:461
  98.2 44.5 %collective-permute-start.12 = (bf16[32,2,16,128]{3,2,1,0:T(8,128)(2,1)S(1)}, bf16[32,2,16,128]{3,2,1,0:T(8,128)(2,1)S(1)}, u32[]{:S(2)}, u32[]{:S(2)}) collective-permute-start(bf16[32,2,16,128]{3,2,1,0:T(8,128)(2,1)S(1)} %bitcast.73), channel_id=1, source_target_pairs={{0,14},{2,8},{4,10},{6,12},{8,6},{10,0},{12,2},{14,4},{1,15},{3,9}... | collective-permute-start | bytes 786440 | tf_op jit(solution)/shard_map/ppermute | solution.py:461
  117.3 19.7 %collective-permute-start.9 = (bf16[32,2,16,128]{3,2,1,0:T(8,128)(2,1)S(1)}, bf16[32,2,16,128]{3,2,1,0:T(8,128)(2,1)S(1)}, u32[]{:S(2)}, u32[]{:S(2)}) collective-permute-start(bf16[32,2,16,128]{3,2,1,0:T(8,128)(2,1)S(1)} %bitcast.76), channel_id=1, source_target_pairs={{0,4},{2,6},{4,0},{6,2},{8,12},{10,14},{12,8},{14,10},{1,5},{3,7},... | collective-permute-start | bytes 786440 | tf_op jit(solution)/shard_map/ppermute | solution.py:461
  117.7 24.9 %collective-permute-start.10 = (bf16[32,2,16,128]{3,2,1,0:T(8,128)(2,1)S(1)}, bf16[32,2,16,128]{3,2,1,0:T(8,128)(2,1)S(1)}, u32[]{:S(2)}, u32[]{:S(2)}) collective-permute-start(bf16[32,2,16,128]{3,2,1,0:T(8,128)(2,1)S(1)} %bitcast.75), channel_id=1, source_target_pairs={{0,12},{2,14},{4,8},{6,10},{8,4},{10,6},{12,0},{14,2},{1,13},{3,15... | collective-permute-start | bytes 786440 | tf_op jit(solution)/shard_map/ppermute | solution.py:461
  142.8 30.2 %collective-permute-start.17 = (bf16[8,32,2,16,128]{4,3,2,1,0:T(8,128)(2,1)S(1)}, bf16[8,32,2,16,128]{4,3,2,1,0:T(8,128)(2,1)S(1)}, u32[]{:S(2)}, u32[]{:S(2)}) collective-permute-start(bf16[8,32,2,16,128]{4,3,2,1,0:T(8,128)(2,1)S(1)} %bitcast_dynamic-update-slice_fusion.refs_3_), channel_id=1, source_target_pairs={{0,1},{1,0},{2,3},{3,2},{4,5},{5,4},{6,7},{7,6},{8,9},{9,8},{10,11... | collective-permute-start | bytes 6291464 | tf_op jit(solution)/shard_map/ppermute | solution.py:461
  143.3 9.0 %collective-permute-start.14 = (bf16[16,2,16,128]{3,2,1,0:T(8,128)(2,1)S(1)}, bf16[16,2,16,128]{3,2,1,0:T(8,128)(2,1)S(1)}, u32[]{:S(2)}, u32[]{:S(2)}) collective-permute-start(bf16[16,2,16,128]{3,2,1,0:T(8,128)(2,1)S(1)} %bitcast.86), channel_id=1, source_target_pairs={{0,2},{2,4},{4,6},{6,0},{8,10},{10,12},{12,14},{14,8},{1,3},{3,5},... | collective-permute-start | bytes 393224 | tf_op jit(solution)/shard_map/ppermute | solution.py:461
  145.8 9.7 %collective-permute-start.15 = (bf16[16,2,16,128]{3,2,1,0:T(8,128)(2,1)S(1)}, bf16[16,2,16,128]{3,2,1,0:T(8,128)(2,1)S(1)}, u32[]{:S(2)}, u32[]{:S(2)}) collective-permute-start(bf16[16,2,16,128]{3,2,1,0:T(8,128)(2,1)S(1)} %bitcast.85), channel_id=1, source_target_pairs={{0,10},{2,12},{4,14},{6,8},{8,2},{10,4},{12,6},{14,0},{1,11},{3,13... | collective-permute-start | bytes 393224 | tf_op jit(solution)/shard_map/ppermute | solution.py:461
  148.9 26.7 %collective-permute-start.23 = (bf16[16,2,16,128]{3,2,1,0:T(8,128)(2,1)S(1)}, bf16[16,2,16,128]{3,2,1,0:T(8,128)(2,1)S(1)}, u32[]{:S(2)}, u32[]{:S(2)}) collective-permute-start(bf16[16,2,16,128]{3,2,1,0:T(8,128)(2,1)S(1)} %bitcast.81), channel_id=1, source_target_pairs={{0,6},{2,0},{4,2},{6,4},{8,14},{10,8},{12,10},{14,12},{1,7},{3,1},... | collective-permute-start | bytes 393224 | tf_op jit(solution)/shard_map/ppermute | solution.py:461
  152.4 23.3 %collective-permute-start.24 = (bf16[16,2,16,128]{3,2,1,0:T(8,128)(2,1)S(1)}, bf16[16,2,16,128]{3,2,1,0:T(8,128)(2,1)S(1)}, u32[]{:S(2)}, u32[]{:S(2)}) collective-permute-start(bf16[16,2,16,128]{3,2,1,0:T(8,128)(2,1)S(1)} %bitcast.80), channel_id=1, source_target_pairs={{0,14},{2,8},{4,10},{6,12},{8,6},{10,0},{12,2},{14,4},{1,15},{3,9}... | collective-permute-start | bytes 393224 | tf_op jit(solution)/shard_map/ppermute | solution.py:461
  155.4 14.5 %collective-permute-start.13 = (bf16[64,2,16,128]{3,2,1,0:T(8,128)(2,1)S(1)}, bf16[64,2,16,128]{3,2,1,0:T(8,128)(2,1)S(1)}, u32[]{:S(2)}, u32[]{:S(2)}) collective-permute-start(bf16[64,2,16,128]{3,2,1,0:T(8,128)(2,1)S(1)} %bitcast.72), channel_id=1, source_target_pairs={{0,8},{2,10},{4,12},{6,14},{8,0},{10,2},{12,4},{14,6},{1,9},{3,11}... | collective-permute-start | bytes 1572872 | tf_op jit(solution)/shard_map/ppermute | solution.py:461
  156.6 16.4 %collective-permute-start.16 = (bf16[16,2,16,128]{3,2,1,0:T(8,128)(2,1)S(1)}, bf16[16,2,16,128]{3,2,1,0:T(8,128)(2,1)S(1)}, u32[]{:S(2)}, u32[]{:S(2)}) collective-permute-start(bf16[16,2,16,128]{3,2,1,0:T(8,128)(2,1)S(1)} %bitcast.83), channel_id=1, source_target_pairs={{0,4},{2,6},{4,0},{6,2},{8,12},{10,14},{12,8},{14,10},{1,5},{3,7},... | collective-permute-start | bytes 393224 | tf_op jit(solution)/shard_map/ppermute | solution.py:461
  175.7 10.0 %collective-permute-start.25 = (bf16[8,16,2,16,128]{4,3,2,1,0:T(8,128)(2,1)S(1)}, bf16[8,16,2,16,128]{4,3,2,1,0:T(8,128)(2,1)S(1)}, u32[]{:S(2)}, u32[]{:S(2)}) collective-permute-start(bf16[8,16,2,16,128]{4,3,2,1,0:T(8,128)(2,1)S(1)} %bitcast_dynamic-update-slice_fusion.7.refs_5_), channel_id=1, source_target_pairs={{0,1},{1,0},{2,3},{3,2},{4,5},{5,4},{6,7},{7,6},{8,9},{9,8},{10,11... | collective-permute-start | bytes 3145736 | tf_op jit(solution)/shard_map/ppermute | solution.py:461
  179.6 19.2 %collective-permute-start.18 = (bf16[2,16,2,16,128]{4,3,2,1,0:T(8,128)(2,1)S(1)}, bf16[2,16,2,16,128]{4,3,2,1,0:T(8,128)(2,1)S(1)}, u32[]{:S(2)}, u32[]{:S(2)}) collective-permute-start(bf16[2,16,2,16,128]{4,3,2,1,0:T(8,128)(2,1)S(1)} %pad_maximum_fusion), channel_id=1, source_target_pairs={{0,2},{2,4},{4,6},{6,0},{8,10},{10,12},{12,14},{14,8},{1,3},{3,5},... | collective-permute-start | bytes 786440 | tf_op jit(solution)/shard_map/ppermute | solution.py:461
  181.3 22.6 %collective-permute-start.19 = (bf16[2,16,2,16,128]{4,3,2,1,0:T(8,128)(2,1)S(1)}, bf16[2,16,2,16,128]{4,3,2,1,0:T(8,128)(2,1)S(1)}, u32[]{:S(2)}, u32[]{:S(2)}) collective-permute-start(bf16[2,16,2,16,128]{4,3,2,1,0:T(8,128)(2,1)S(1)} %pad_maximum_fusion.1), channel_id=1, source_target_pairs={{0,4},{2,6},{4,0},{6,2},{8,12},{10,14},{12,8},{14,10},{1,5},{3,7},... | collective-permute-start | bytes 786440 | tf_op jit(solution)/shard_map/ppermute | solution.py:461
  185.7 22.5 %collective-permute-start.20 = (bf16[2,16,2,16,128]{4,3,2,1,0:T(8,128)(2,1)S(1)}, bf16[2,16,2,16,128]{4,3,2,1,0:T(8,128)(2,1)S(1)}, u32[]{:S(2)}, u32[]{:S(2)}) collective-permute-start(bf16[2,16,2,16,128]{4,3,2,1,0:T(8,128)(2,1)S(1)} %pad_maximum_fusion.2), channel_id=1, source_target_pairs={{0,6},{2,0},{4,2},{6,4},{8,14},{10,8},{12,10},{14,12},{1,7},{3,1},... | collective-permute-start | bytes 786440 | tf_op jit(solution)/shard_map/ppermute | solution.py:461
  (15 other events, 270.7 us)

commit v4 on v3

--- a/solution.py
+++ b/solution.py
@@ -299,8 +299,8 @@
     return [piece.reshape(count, 2, ROWS, LANES) for piece, count in zip(flat, counts)]
 
 
-def correlate_kernel(starts, width, place_ref, sel_ref, weight_ref, *refs):
-    x_refs, (out_ref, x_all, even_rows, odd_rows, sems) = refs[: 2 * len(starts)], refs[-5:]
+def correlate_kernel(starts, width, place_ref, left_sel_ref, right_sel_ref, weight_ref, *refs):
+    x_refs, (out_ref, x_all, *rows_refs, sems) = refs[: 2 * len(starts)], refs[-7:]
     tiles = out_ref.shape[0]
     step = pl.program_id(0)
     bands = x_all.shape[2]
@@ -323,7 +323,10 @@
                 )
             block += blocks
 
-    def gather(band, rows_ref):
+    lower = lax.broadcasted_iota(jnp.int32, (1, 2 * width), 1) < width
+
+    def gather(band, left_ref, right_ref):
+        right = []
         for pol in range(2):
             lanes = slice(pol * 2 * LANES, (pol + 1) * 2 * LANES)
             value = jnp.concatenate(
@@ -332,32 +335,42 @@
                     for block in range(x_all.shape[1])
                 ]
             )
-            picked = jnp.dot(sel_ref[...], value, preferred_element_type=jnp.float32)
+            left = jnp.dot(left_sel_ref[...], value, preferred_element_type=jnp.float32)
             for tile in range(tiles):
-                at = tile * 2 * width
-                left = picked[at : at + width] * weight_ref[pl.ds(tile, 1), :]
-                right = picked[at + width : at + 2 * width]
-                rows_ref[at : at + width, lanes] = left.astype(jnp.bfloat16)
-                rows_ref[at + width : at + 2 * width, lanes] = right.astype(jnp.bfloat16)
-
-    form = (((1,), (1,)), ((), ()))
-
-    def multiply(number, rows_ref):
+                rows = slice(tile * width, (tile + 1) * width)
+                scaled = left[rows] * weight_ref[pl.ds(tile, 1), :]
+                left_ref[rows, lanes] = scaled.astype(jnp.bfloat16)
+            right.append(
+                lax.dot_general(
+                    value,
+                    right_sel_ref[pol],
+                    (((0,), (0,)), ((), ())),
+                    preferred_element_type=jnp.float32,
+                )
+            )
+        for pair in range(tiles // 2):
+            first, second = (v[:, pair * 2 * width : (pair + 1) * 2 * width] for v in right)
+            even = jnp.where(lower, first, second)
+            odd = pltpu.roll(jnp.where(lower, second, first), width, 1)
+            right_ref[2 * pair] = even.astype(jnp.bfloat16)
+            right_ref[2 * pair + 1] = odd.astype(jnp.bfloat16)
+
+    def multiply(number, left_ref, right_ref):
         for tile in range(tiles):
-            at = tile * 2 * width
-            left, right = (
-                jnp.concatenate(
-                    [
-                        rows_ref[at + first : at + first + width, lanes : lanes + 2 * LANES]
-                        for lanes in (0, 2 * LANES)
-                    ]
-                )
-                for first in (0, width)
+            rows = slice(tile * width, (tile + 1) * width)
+            left = jnp.concatenate(
+                [left_ref[rows, lanes : lanes + 2 * LANES] for lanes in (0, 2 * LANES)]
             )
-            turned = jnp.concatenate([left[:, LANES:], -left[:, :LANES]], axis=1)
-            both = jnp.concatenate([left, turned])
-            result = lax.dot_general(both, right, form, preferred_element_type=jnp.float32)
-            out_ref[tile, number] = result.reshape(2, 2, width, 2 * width)
+            right = right_ref[tile]
+            turned = jnp.concatenate([-right[LANES:], right[:LANES]])
+            both = jnp.concatenate([right, turned], axis=1)
+            result = jnp.dot(left, both, preferred_element_type=jnp.float32)
+            for part in range(2):
+                out_ref[tile, number, part] = result[
+                    :, part * 2 * width : (part + 1) * 2 * width
+                ].reshape(2, width, 2 * width)
+
+    even, odd = rows_refs[:2], rows_refs[2:]
 
     @pl.when(step == 0)
     def _():
@@ -366,38 +379,42 @@
                 copy.start()
         for copy in copies(0):
             copy.wait()
-        gather(0, even_rows)
+        gather(0, *even)
         for copy in copies(1):
             copy.wait()
 
-    gather(2 * step + 1, odd_rows)
-    multiply(0, even_rows)
-    gather(jnp.minimum(2 * step + 2, bands - 1), even_rows)
-    multiply(1, odd_rows)
-
-
-def correlate_tiles(place, select, weight, pieces, starts, width, first, count, bands, earlier):
+    gather(2 * step + 1, *odd)
+    multiply(0, *even)
+    gather(jnp.minimum(2 * step + 2, bands - 1), *even)
+    multiply(1, *odd)
+
+
+def correlate_tiles(place, tables, pieces, starts, width, first, count, bands, earlier):
+    left_select, _, weight = tables
     tiles = weight.shape[0]
     whole = pl.BlockSpec(memory_space=pltpu.VMEM)
     more = [] if earlier is None else [earlier]
-    rows = pltpu.VMEM((tiles * 2 * width, 4 * LANES), jnp.bfloat16)
+    rows = [
+        pltpu.VMEM((tiles * width, 4 * LANES), jnp.bfloat16),
+        pltpu.VMEM((tiles, 2 * LANES, 2 * width), jnp.bfloat16),
+    ]
     return pl.pallas_call(
         lambda *refs: correlate_kernel(starts, width, *refs),
         grid=(count // 2,),
         out_shape=jax.ShapeDtypeStruct((tiles, bands, 2, 2, width, 2 * width), jnp.float32),
         in_specs=[pl.BlockSpec(memory_space=pltpu.SMEM)]
-        + [whole] * 2
+        + [whole] * len(tables)
         + [pl.BlockSpec(memory_space=pl.ANY)] * (len(pieces) + len(more)),
         out_specs=pl.BlockSpec(
             (tiles, 2, 2, 2, width, 2 * width), lambda g: (0, g + first // 2, 0, 0, 0, 0)
         ),
         scratch_shapes=[
-            pltpu.VMEM((2, select.shape[1] // ROWS, count, 2, ROWS, LANES), jnp.bfloat16),
-            rows,
-            rows,
+            pltpu.VMEM((2, left_select.shape[1] // ROWS, count, 2, ROWS, LANES), jnp.bfloat16),
+            *rows,
+            *rows,
             pltpu.SemaphoreType.DMA((2, len(pieces))),
         ],
-        input_output_aliases={3 + len(pieces): 0} if more else {},
+        input_output_aliases={1 + len(tables) + len(pieces): 0} if more else {},
         compiler_params=pltpu.CompilerParams(vmem_limit_bytes=32 * 2**20),
         cost_estimate=pl.CostEstimate(
             flops=13 * 10**9 * count // bands,
@@ -405,7 +422,7 @@
             transcendentals=0,
         ),
         name="correlate",
-    )(place, select, weight, *pieces, *more)
+    )(place, *tables, *pieces, *more)
 
 
 def tile_tables(tile_a, tile_b, tile_owner, tile_flags, row_of):
@@ -445,10 +462,15 @@
 
     rows, flags = tile_tables(tile_a, tile_b, tile_owner, tile_flags, row_of)
     total_rows = chunk_count * owners * ROWS
-    select = (rows[..., None] == jnp.arange(total_rows, dtype=jnp.int32)).astype(jnp.bfloat16)
-    select = select.reshape(CAP * 2 * width, total_rows)
+    station_rows = jnp.arange(total_rows, dtype=jnp.int32)
+    left_rows = rows[:, 0].reshape(-1)
+    left_select = (left_rows[:, None] == station_rows).astype(jnp.bfloat16)
+    right_rows = rows[:, 1].reshape(CAP // 2, 2, width)
+    right_rows = jnp.stack([right_rows, right_rows[:, ::-1]]).reshape(2, 1, -1)
+    right_select = (right_rows == station_rows[:, None]).astype(jnp.bfloat16)
     depth = AVG * time_count * frames
     weight = jnp.tile(flags * (1.0 / depth), (1, 2 * AVG))
+    tables_of_tiles = [left_select, right_select, weight]
 
     samples = voltages.reshape(2, stations, frames * length)
 
@@ -487,50 +509,57 @@
     two, three = (block_for(values, 0, distance) for distance in (2, 3))
     one, two = over(one, 0, 1), over(two, 0, 2)
     (three,), (one,) = after([three], [one])
-    first = [one, two, over(three, 0, 3)]
+    three = over(three, 0, 3)
     blocks = [block_for(values, 1, distance) for distance in (1, 2, 3)]
-    (one, two, three), first = after(blocks, first)
-    one, three = over(one, 0, 1), over(three, 0, 3)
-    (two,), (one,) = after([two], [one])
+    blocks[:1], (two,) = after(blocks[:1], [two])
+    blocks[2:], (three,) = after(blocks[2:], [three])
+    first = [one, two, three]
+    one, three = over(blocks[0], 0, 1), over(blocks[2], 0, 3)
+    (two,), (one,) = after(blocks[1:2], [one])
     second = [one, over(two, 0, 2), three]
 
     plan = [[(x, z, 0, bands)] for x, z in pairs]
     early = dict(zip(pairs, filtered(0, first, plan)))
-    blocks, held = after([early[p] for p in early_pairs], [second[1], select, weight])
-    second[1], select, weight = held
+    blocks, held = after([early[p] for p in early_pairs], [second[1], *tables_of_tiles])
+    second[1], tables_of_tiles = held[0], held[1:]
     early.update((p, over(block, *p)) for p, block in zip(early_pairs, blocks))
     blocks, held = after([early[p] for p in late_pairs], [early[p] for p in early_pairs[:2]])
     early.update(zip(early_pairs[:2], held))
     early.update((p, over(block, *p)) for p, block in zip(late_pairs, blocks))
 
-    plan = [[(x, z, 0, half)] for x, z in pairs]
-    plan += [[(x, z, half, bands) for z in range(time_count)] for x in range(chan_count)]
-    *low, near, far = filtered(1, second, plan)
-    low = dict(zip(pairs, low))
-    blocks, held = after([low[p] for p in early_pairs] + [far], [early[p] for p in late_pairs[:1]])
+    plan = [
+        [(x, z, start, start + half) for start in (0, half) for z in range(time_count)]
+        for x in range(chan_count)
+    ]
+    near, far = filtered(1, second, plan)
+    (far,), held = after([far], [early[p] for p in early_pairs[:2]])
+    early.update(zip(early_pairs[:2], held))
+    far = over(far, 1, 0)
+    shape = (2, time_count, half, 2, ROWS, LANES)
+    (near, high), (far, far_high) = (v.reshape(shape) for v in (near, far))
+    low = [columns(near[z], far[z]) for z in range(time_count)]
+    high = [columns(high[z], far_high[z]) for z in range(time_count)]
+    blocks, held = after(low[1:], [early[p] for p in late_pairs[:1]])
     early.update(zip(late_pairs[:1], held))
-    low.update((p, over(block, *p)) for p, block in zip(early_pairs, blocks))
-    far = over(blocks[-1], 1, 0)
-    blocks, held = after([low[p] for p in late_pairs], [low[p] for p in early_pairs[:2]])
-    low.update(zip(early_pairs[:2], held))
-    low.update((p, over(block, *p)) for p, block in zip(late_pairs, blocks))
-    near, far = (v.reshape(time_count, half, 2, ROWS, LANES) for v in (near, far))
-    high = [columns(near[z], far[z]) for z in range(time_count)]
+    moved = {z: over(blocks[z - 1], 0, z) for z in (2, 1, 3)}
+    low = [low[0]] + [moved[z] for z in (1, 2, 3)]
 
     def with_other(values):
         return [side for v in values for side in (v, travel(v, ("pol",), (1,)))]
 
     early = with_other([jnp.stack([early[p] for p in pairs])])
-    blocks, held = after(high[1:], [low[late_pairs[0]], early[1]])
-    low[late_pairs[0]], early[1] = held
-    high[1:] = [over(block, 0, z) for z, block in zip((1, 2, 3), blocks)]
+    blocks, held = after(high[1:], [low[2], low[1], early[1]])
+    low[2], low[1], early[1] = held
+    moved = {z: over(blocks[z - 1], 0, z) for z in (2, 1, 3)}
+    high = [high[0]] + [moved[z] for z in (1, 2, 3)]
+    low = jnp.stack(low).reshape(2 * time_count, half, 2, ROWS, LANES)
     visibility = correlate_tiles(
-        place, select, weight, early + with_other([jnp.stack([low[p] for p in pairs])]),
+        place, tables_of_tiles, early + with_other([low]),
         [0, 0], width, 0, half, bands, None,
     )
     high, (visibility,) = after(high, [visibility])
     return correlate_tiles(
-        place, select, weight, early + with_other(high),
+        place, tables_of_tiles, early + with_other(high),
         [half] + [0] * 4, width, half, half, bands, visibility,
     )
 

time: 227 us -> 221 us (0.974)
  starting transfers between devices: 50.2 us -> 32.1 us
  waiting for transfers between devices: 109 us -> 122 us
    ppermute x30 -> x26, starting transfers between devices: 50.2 us -> 32.1 us  [travel(): return lax.ppermute(value, axes, pairs)]
    ppermute x30 -> x26, waiting for transfers between devices: 109 us -> 122 us  [travel(): return lax.ppermute(value, axes, pairs)]
  transfers between devices with their start and end apart: 30 -> 26, of which waited for: 15 -> 15; matrix products, arithmetic and copies ran while one was open for 2% -> 2% of each run, Pallas kernels for 20% -> 20%
where the time goes in v4:
time: 221 us; the launch traced here: 220 us
  waiting for transfers between devices  122 us (55%)
  Pallas kernels  56.6 us (26%)
  starting transfers between devices  32.1 us (15%)
  local copies, waits for them, and re-layouts  7.11 us (3%)
    ppermute x26, waiting for transfers between devices, travel(): return lax.ppermute(value, axes, pairs)  122 us
    ppermute x26, starting transfers between devices, travel(): return lax.ppermute(value, axes, pairs)  32.1 us
    pallas_call x2, Pallas kernels, channelise(): pl.pallas_call(lambda *refs: channelise_kernel(frames, chunk, columns, pl...  31.1 us
    pallas_call x2, Pallas kernels, correlate_tiles(): pl.pallas_call(lambda *refs: correlate_kernel(starts, width, *refs), grid...  25.5 us
  transfers between devices with their start and end apart: 26, of which 15 were waited for; matrix products, arithmetic and copies ran while one was open for 2% of the time, Pallas kernels for 20%

profile of v4, /device:TPU:11, one launch (start us, length us, event | category | flops | bytes accessed | tf_op | source)
XLA Modules:
  0.0 219.8 jit_solution(12716838992525529715)
XLA Ops:
  2.5 3.0 %constant_dynamic-slice_fusion = (bf16[2,16,8192]{2,1,0:T(8,128)(2,1)}, bf16[2,16,8192]{2,1,0:T(8,128)(2,1)S(1)}, bf16[2,16,8192]{2,1,0:T(8,128)(2,1)S(1)}, bf16[2,16,8192]{2,1,0:T(8,128)(2,1)}, bf16[2,16,8192]{2,1,0:T(8,128)(2,1)}) fusion(bf16[2,128,8192]{2,1,0:T(8,128)(2,1)} %bitcast.73, s32[]{:T(128)S(6)} %select_n.109, s32[]{:T(128)S(6)} %select_n.108, ...), kind=kLoop, calls=%fused_computation.128 | loop fusion | bytes 5242900 | tf_op jit(solution)/shard_map/dynamic_slice | solution.py:490
  7.3 6.6 %collective-permute-done.refs_2_ = bf16[2,16,8192]{2,1,0:T(8,128)(2,1)S(1)} collective-permute-done((bf16[2,16,8192]{2,1,0:T(8,128)(2,1)S(1)}, bf16[2,16,8192]{2,1,0:T(8,128)(2,1)S(1)}, u32[]{:S(2)}, u32[]{:S(2)}) %collective-permute-start) | collective-permute-done | bytes 524320 | tf_op jit(solution)/shard_map/ppermute | solution.py:483
  13.9 2.1 collective-permute-start.2
  16.1 30.7 %collective-permute-done.1.refs_3_ = bf16[2,16,8192]{2,1,0:T(8,128)(2,1)S(1)} collective-permute-done((bf16[2,16,8192]{2,1,0:T(8,128)(2,1)S(1)}, bf16[2,16,8192]{2,1,0:T(8,128)(2,1)S(1)}, u32[]{:S(2)}, u32[]{:S(2)}) %collective-permute-start.1) | collective-permute-done | bytes 524320 | tf_op jit(solution)/shard_map/ppermute | solution.py:483
  47.3 1.5 collective-permute-start.6
  48.8 9.7 %collective-permute-done.3.refs_2_ = bf16[2,16,8192]{2,1,0:T(8,128)(2,1)S(1)} collective-permute-done((bf16[2,16,8192]{2,1,0:T(8,128)(2,1)}, bf16[2,16,8192]{2,1,0:T(8,128)(2,1)S(1)}, u32[]{:S(2)}, u32[]{:S(2)}) %collective-permute-start.3) | collective-permute-done | bytes 524320 | tf_op jit(solution)/shard_map/ppermute | solution.py:483
  58.4 4.1 %collective-permute-start.4 = (bf16[2,16,8192]{2,1,0:T(8,128)(2,1)}, bf16[2,16,8192]{2,1,0:T(8,128)(2,1)S(1)}, u32[]{:S(2)}, u32[]{:S(2)}) collective-permute-start(bf16[2,16,8192]{2,1,0:T(8,128)(2,1)} %get-tuple-element.68), channel_id=1, source_target_pairs={{0,4},{2,6},{4,0},{6,2},{8,12},{10,14},{12,8},{14,10},{1,5},{3,7},... | collective-permute-start | bytes 1572872 | tf_op jit(solution)/shard_map/ppermute | solution.py:483
  62.6 2.2 copy-done
  64.8 15.6 %channelise.2 = (bf16[1024,128]{1,0:T(8,128)(2,1)S(1)}, bf16[1024,128]{1,0:T(8,128)(2,1)S(1)}, bf16[1024,128]{1,0:T(8,128)(2,1)S(1)}, bf16[1024,128]{1,0:T(8,128...) custom-call(s32[3]{0:T(128)S(1)} %pad_add_fusion.refs_0_, ...), custom_call_target="tpu_custom_call" | custom-call | flops 8999999488 | bytes 4194304 | tf_op jit(solution)/shard_map/channelise/pallas_call | solution.py:276
  80.3 13.3 %collective-permute-done.4.refs_3_ = bf16[2,16,8192]{2,1,0:T(8,128)(2,1)S(1)} collective-permute-done((bf16[2,16,8192]{2,1,0:T(8,128)(2,1)}, bf16[2,16,8192]{2,1,0:T(8,128)(2,1)S(1)}, u32[]{:S(2)}, u32[]{:S(2)}) %collective-permute-start.4) | collective-permute-done | bytes 524320 | tf_op jit(solution)/shard_map/ppermute | solution.py:483
  93.9 1.9 collective-permute-start.7
  95.8 2.3 %collective-permute-start.8 = (bf16[32,2,16,128]{3,2,1,0:T(8,128)(2,1)S(1)}, bf16[32,2,16,128]{3,2,1,0:T(8,128)(2,1)S(1)}, u32[]{:S(2)}, u32[]{:S(2)}) collective-permute-start(bf16[32,2,16,128]{3,2,1,0:T(8,128)(2,1)S(1)} %bitcast.83), channel_id=1, source_target_pairs={{0,10},{2,12},{4,14},{6,8},{8,2},{10,4},{12,6},{14,0},{1,11},{3,13... | collective-permute-start | bytes 786440 | tf_op jit(solution)/shard_map/ppermute | solution.py:483
  98.1 15.6 %channelise.3 = (bf16[4096,128]{1,0:T(8,128)(2,1)S(1)}, bf16[4096,128]{1,0:T(8,128)(2,1)S(1)}) custom-call(s32[3]{0:T(128)S(1)} %pad_add_fusion.refs_0_, bf16[2,128,8192]{2,1,0:T(8,128)(2,1)S(1)} %bitcast.75, bf16[2,16,8192]{2,1,0:T(8,128)(2,1)S(1)} %collective-permute-done.3.refs_2_, bf16[2,16,8192]{2,1,0:T(8,128)(2,1)S(1)} %collective-permute-done.4.refs_3_, ...), custom_call_target="tpu_custom_call" | custom-call | flops 8999999488 | bytes 4194304 | tf_op jit(solution)/shard_map/channelise/pallas_call | solution.py:276
  114.5 4.2 %collective-permute-start.13 = (bf16[32,2,16,128]{3,2,1,0:T(8,128)(2,1)S(1)}, bf16[32,2,16,128]{3,2,1,0:T(8,128)(2,1)S(1)}, u32[]{:S(2)}, u32[]{:S(2)}) collective-permute-start(bf16[32,2,16,128]{3,2,1,0:T(8,128)(2,1)S(1)} %bitcast.78), channel_id=1, source_target_pairs={{0,14},{2,8},{4,10},{6,12},{8,6},{10,0},{12,2},{14,4},{1,15},{3,9}... | collective-permute-start | bytes 786440 | tf_op jit(solution)/shard_map/ppermute | solution.py:483
  119.2 2.0 collective-permute-start.11
  121.3 27.0 %collective-permute-done.9 = bf16[128,2,16,128]{3,2,1,0:T(8,128)(2,1)S(1)} collective-permute-done((bf16[128,2,16,128]{3,2,1,0:T(8,128)(2,1)S(1)}, bf16[128,2,16,128]{3,2,1,0:T(8,128)(2,1)S(1)}, u32[]{:S(2)}, u32[]{:S(2)}) %collective-permute-start.9) | collective-permute-done | bytes 1048608 | tf_op jit(solution)/shard_map/ppermute | solution.py:483
  148.6 3.0 %collective-permute-done.11 = bf16[32,2,16,128]{3,2,1,0:T(8,128)(2,1)S(1)} collective-permute-done((bf16[32,2,16,128]{3,2,1,0:T(8,128)(2,1)S(1)}, bf16[32,2,16,128]{3,2,1,0:T(8,128)(2,1)S(1)}, u32[]{:S(2)}, u32[]{:S(2)}) %collective-permute-start.11) | collective-permute-done | bytes 262176 | tf_op jit(solution)/shard_map/ppermute | solution.py:483
  152.3 4.0 %collective-permute-start.14 = (bf16[2,16,2,16,128]{4,3,2,1,0:T(8,128)(2,1)S(1)}, bf16[2,16,2,16,128]{4,3,2,1,0:T(8,128)(2,1)S(1)}, u32[]{:S(2)}, u32[]{:S(2)}) collective-permute-start(bf16[2,16,2,16,128]{4,3,2,1,0:T(8,128)(2,1)S(1)} %pad_maximum_fusion.2), channel_id=1, source_target_pairs={{0,4},{2,6},{4,0},{6,2},{8,12},{10,14},{12,8},{14,10},{1,5},{3,7},... | collective-permute-start | bytes 786440 | tf_op jit(solution)/shard_map/ppermute | solution.py:483
  156.3 1.5 collective-permute-start.20
  157.9 8.5 %collective-permute-done.14 = bf16[2,16,2,16,128]{4,3,2,1,0:T(8,128)(2,1)S(1)} collective-permute-done((bf16[2,16,2,16,128]{4,3,2,1,0:T(8,128)(2,1)S(1)}, bf16[2,16,2,16,128]{4,3,2,1,0:T(8,128)(2,1)S(1)}, u32[]{:S(2)}, u32[]{:S(2)}) %collective-permute-start.14) | collective-permute-done | bytes 262176 | tf_op jit(solution)/shard_map/ppermute | solution.py:483
  166.4 11.3 %collective-permute-done.15 = bf16[2,16,2,16,128]{4,3,2,1,0:T(8,128)(2,1)S(1)} collective-permute-done((bf16[2,16,2,16,128]{4,3,2,1,0:T(8,128)(2,1)S(1)}, bf16[2,16,2,16,128]{4,3,2,1,0:T(8,128)(2,1)S(1)}, u32[]{:S(2)}, u32[]{:S(2)}) %collective-permute-start.15) | collective-permute-done | bytes 262176 | tf_op jit(solution)/shard_map/ppermute | solution.py:483
  182.4 12.1 %correlate.2.refs_14_ = f32[8,32,2,2,64,128]{5,4,3,2,1,0:T(8,128)} custom-call(s32[3]{0:T(128)S(1)} %pad_add_fusion.refs_0_, bf16[512,256]{1,0:T(8,128)(2,1)S(1)} %fusion.1.refs_1_, bf16[2,256,512]{2,1,0:T(8,128)(2,1)S(1)} %fusion.refs_2_, f32[8,256]{1,0:T(8,128)S(1)} %tile.10.refs_3_, ...), custom_call_target="tpu_custom_call" | custom-call | flops 6499999744 | bytes 22020096 | tf_op jit(solution)/shard_map/correlate/pallas_call | solution.py:401
  194.5 8.7 %collective-permute-done.18.refs_10_ = bf16[2,16,2,16,128]{4,3,2,1,0:T(8,128)(2,1)S(1)} collective-permute-done((bf16[2,16,2,16,128]{4,3,2,1,0:T(8,128)(2,1)S(1)}, bf16[2,16,2,16,128]{4,3,2,1,0:T(8,128)(2,1)S(1)}, u32[]{:S(2)}, u32[]{:S(2)}) %collective-permute-start.18) | collective-permute-done | bytes 262176 | tf_op jit(solution)/shard_map/ppermute | solution.py:483
  206.3 13.5 %correlate.3 = f32[8,32,2,2,64,128]{5,4,3,2,1,0:T(8,128)} custom-call(s32[3]{0:T(128)S(1)} %pad_add_fusion.refs_0_, bf16[512,256]{1,0:T(8,128)(2,1)S(1)} %fusion.1.refs_1_, bf16[2,256,512]{2,1,0:T(8,128)(2,1)S(1)} %fusion.refs_2_, f32[8,256]{1,0:T(8,128)S(1)} %tile.10.refs_3_, ...), custom_call_target="tpu_custom_call", output_to_operand_aliasing={{}: (14, {})} | custom-call | flops 6499999744 | bytes 22020096 | tf_op jit(solution)/shard_map/correlate/pallas_call | solution.py:401
  (90 shorter events, 15.3 us)
Async XLA Ops:
  1.1 12.8 %collective-permute-start = (bf16[2,16,8192]{2,1,0:T(8,128)(2,1)S(1)}, bf16[2,16,8192]{2,1,0:T(8,128)(2,1)S(1)}, u32[]{:S(2)}, u32[]{:S(2)}) collective-permute-start(bf16[2,16,8192]{2,1,0:T(8,128)(2,1)S(1)} %dynamic-slice_bitcast_fusion), channel_id=1, source_target_pairs={{0,2},{2,4},{4,6},{6,0},{8,10},{10,12},{12,14},{14,8},{1,3},{3,5},... | collective-permute-start | bytes 1572872 | tf_op jit(solution)/shard_map/ppermute | solution.py:483
  5.5 41.3 %collective-permute-start.1 = (bf16[2,16,8192]{2,1,0:T(8,128)(2,1)S(1)}, bf16[2,16,8192]{2,1,0:T(8,128)(2,1)S(1)}, u32[]{:S(2)}, u32[]{:S(2)}) collective-permute-start(bf16[2,16,8192]{2,1,0:T(8,128)(2,1)S(1)} %get-tuple-element.109), channel_id=1, source_target_pairs={{0,4},{2,6},{4,0},{6,2},{8,12},{10,14},{12,8},{14,10},{1,5},{3,7},... | collective-permute-start | bytes 1572872 | tf_op jit(solution)/shard_map/ppermute | solution.py:483
  13.9 33.3 %collective-permute-start.2 = (bf16[2,16,8192]{2,1,0:T(8,128)(2,1)}, bf16[2,16,8192]{2,1,0:T(8,128)(2,1)S(1)}, u32[]{:S(2)}, u32[]{:S(2)}) collective-permute-start(bf16[2,16,8192]{2,1,0:T(8,128)(2,1)} %get-tuple-element.60), channel_id=1, source_target_pairs={{0,6},{2,0},{4,2},{6,4},{8,14},{10,8},{12,10},{14,12},{1,7},{3,1},... | collective-permute-start | bytes 1572872 | tf_op jit(solution)/shard_map/ppermute | solution.py:483
  46.7 11.7 %collective-permute-start.3 = (bf16[2,16,8192]{2,1,0:T(8,128)(2,1)}, bf16[2,16,8192]{2,1,0:T(8,128)(2,1)S(1)}, u32[]{:S(2)}, u32[]{:S(2)}) collective-permute-start(bf16[2,16,8192]{2,1,0:T(8,128)(2,1)} %get-tuple-element.67), channel_id=1, source_target_pairs={{0,2},{2,4},{4,6},{6,0},{8,10},{10,12},{12,14},{14,8},{1,3},{3,5},... | collective-permute-start | bytes 1572872 | tf_op jit(solution)/shard_map/ppermute | solution.py:483
  47.3 50.8 %collective-permute-start.6 = (bf16[2,16,8192]{2,1,0:T(8,128)(2,1)S(1)}, bf16[2,16,8192]{2,1,0:T(8,128)(2,1)S(1)}, u32[]{:S(2)}, u32[]{:S(2)}) collective-permute-start(bf16[2,16,8192]{2,1,0:T(8,128)(2,1)S(1)} %get-tuple-element.76), channel_id=1, source_target_pairs={{0,6},{2,0},{4,2},{6,4},{8,14},{10,8},{12,10},{14,12},{1,7},{3,1},... | collective-permute-start | bytes 1572872 | tf_op jit(solution)/shard_map/ppermute | solution.py:483
  58.4 35.2 %collective-permute-start.4 = (bf16[2,16,8192]{2,1,0:T(8,128)(2,1)}, bf16[2,16,8192]{2,1,0:T(8,128)(2,1)S(1)}, u32[]{:S(2)}, u32[]{:S(2)}) collective-permute-start(bf16[2,16,8192]{2,1,0:T(8,128)(2,1)} %get-tuple-element.68), channel_id=1, source_target_pairs={{0,4},{2,6},{4,0},{6,2},{8,12},{10,14},{12,8},{14,10},{1,5},{3,7},... | collective-permute-start | bytes 1572872 | tf_op jit(solution)/shard_map/ppermute | solution.py:483
  93.6 25.5 %collective-permute-start.5 = (bf16[32,2,16,128]{3,2,1,0:T(8,128)(2,1)S(1)}, bf16[32,2,16,128]{3,2,1,0:T(8,128)(2,1)S(1)}, u32[]{:S(2)}, u32[]{:S(2)}) collective-permute-start(bf16[32,2,16,128]{3,2,1,0:T(8,128)(2,1)S(1)} %bitcast.82), channel_id=1, source_target_pairs={{0,8},{2,10},{4,12},{6,14},{8,0},{10,2},{12,4},{14,6},{1,9},{3,11}... | collective-permute-start | bytes 786440 | tf_op jit(solution)/shard_map/ppermute | solution.py:483
  93.9 19.8 %collective-permute-start.7 = (bf16[32,2,16,128]{3,2,1,0:T(8,128)(2,1)S(1)}, bf16[32,2,16,128]{3,2,1,0:T(8,128)(2,1)S(1)}, u32[]{:S(2)}, u32[]{:S(2)}) collective-permute-start(bf16[32,2,16,128]{3,2,1,0:T(8,128)(2,1)S(1)} %bitcast.84), channel_id=1, source_target_pairs={{0,2},{2,4},{4,6},{6,0},{8,10},{10,12},{12,14},{14,8},{1,3},{3,5},... | collective-permute-start | bytes 786440 | tf_op jit(solution)/shard_map/ppermute | solution.py:483
  95.8 17.9 %collective-permute-start.8 = (bf16[32,2,16,128]{3,2,1,0:T(8,128)(2,1)S(1)}, bf16[32,2,16,128]{3,2,1,0:T(8,128)(2,1)S(1)}, u32[]{:S(2)}, u32[]{:S(2)}) collective-permute-start(bf16[32,2,16,128]{3,2,1,0:T(8,128)(2,1)S(1)} %bitcast.83), channel_id=1, source_target_pairs={{0,10},{2,12},{4,14},{6,8},{8,2},{10,4},{12,6},{14,0},{1,11},{3,13... | collective-permute-start | bytes 786440 | tf_op jit(solution)/shard_map/ppermute | solution.py:483
  113.7 34.6 %collective-permute-start.9 = (bf16[128,2,16,128]{3,2,1,0:T(8,128)(2,1)S(1)}, bf16[128,2,16,128]{3,2,1,0:T(8,128)(2,1)S(1)}, u32[]{:S(2)}, u32[]{:S(2)}) collective-permute-start(bf16[128,2,16,128]{3,2,1,0:T(8,128)(2,1)S(1)} %bitcast.77), channel_id=1, source_target_pairs={{0,8},{2,10},{4,12},{6,14},{8,0},{10,2},{12,4},{14,6},{1,9},{3,11}... | collective-permute-start | bytes 3145736 | tf_op jit(solution)/shard_map/ppermute | solution.py:483
  114.0 37.6 %collective-permute-start.12 = (bf16[32,2,16,128]{3,2,1,0:T(8,128)(2,1)S(1)}, bf16[32,2,16,128]{3,2,1,0:T(8,128)(2,1)S(1)}, u32[]{:S(2)}, u32[]{:S(2)}) collective-permute-start(bf16[32,2,16,128]{3,2,1,0:T(8,128)(2,1)S(1)} %bitcast.79), channel_id=1, source_target_pairs={{0,6},{2,0},{4,2},{6,4},{8,14},{10,8},{12,10},{14,12},{1,7},{3,1},... | collective-permute-start | bytes 786440 | tf_op jit(solution)/shard_map/ppermute | solution.py:483
  114.5 37.2 %collective-permute-start.13 = (bf16[32,2,16,128]{3,2,1,0:T(8,128)(2,1)S(1)}, bf16[32,2,16,128]{3,2,1,0:T(8,128)(2,1)S(1)}, u32[]{:S(2)}, u32[]{:S(2)}) collective-permute-start(bf16[32,2,16,128]{3,2,1,0:T(8,128)(2,1)S(1)} %bitcast.78), channel_id=1, source_target_pairs={{0,14},{2,8},{4,10},{6,12},{8,6},{10,0},{12,2},{14,4},{1,15},{3,9}... | collective-permute-start | bytes 786440 | tf_op jit(solution)/shard_map/ppermute | solution.py:483
  118.7 29.8 %collective-permute-start.10 = (bf16[32,2,16,128]{3,2,1,0:T(8,128)(2,1)S(1)}, bf16[32,2,16,128]{3,2,1,0:T(8,128)(2,1)S(1)}, u32[]{:S(2)}, u32[]{:S(2)}) collective-permute-start(bf16[32,2,16,128]{3,2,1,0:T(8,128)(2,1)S(1)} %bitcast.81), channel_id=1, source_target_pairs={{0,4},{2,6},{4,0},{6,2},{8,12},{10,14},{12,8},{14,10},{1,5},{3,7},... | collective-permute-start | bytes 786440 | tf_op jit(solution)/shard_map/ppermute | solution.py:483
  119.2 32.4 %collective-permute-start.11 = (bf16[32,2,16,128]{3,2,1,0:T(8,128)(2,1)S(1)}, bf16[32,2,16,128]{3,2,1,0:T(8,128)(2,1)S(1)}, u32[]{:S(2)}, u32[]{:S(2)}) collective-permute-start(bf16[32,2,16,128]{3,2,1,0:T(8,128)(2,1)S(1)} %bitcast.80), channel_id=1, source_target_pairs={{0,12},{2,14},{4,8},{6,10},{8,4},{10,6},{12,0},{14,2},{1,13},{3,15... | collective-permute-start | bytes 786440 | tf_op jit(solution)/shard_map/ppermute | solution.py:483
  151.7 26.0 %collective-permute-start.16 = (bf16[8,32,2,16,128]{4,3,2,1,0:T(8,128)(2,1)S(1)}, bf16[8,32,2,16,128]{4,3,2,1,0:T(8,128)(2,1)S(1)}, u32[]{:S(2)}, u32[]{:S(2)}) collective-permute-start(bf16[8,32,2,16,128]{4,3,2,1,0:T(8,128)(2,1)S(1)} %bitcast_dynamic-update-slice_fusion.refs_4_), channel_id=1, source_target_pairs={{0,1},{1,0},{2,3},{3,2},{4,5},{5,4},{6,7},{7,6},{8,9},{9,8},{10,11... | collective-permute-start | bytes 6291464 | tf_op jit(solution)/shard_map/ppermute | solution.py:483
  152.3 14.1 %collective-permute-start.14 = (bf16[2,16,2,16,128]{4,3,2,1,0:T(8,128)(2,1)S(1)}, bf16[2,16,2,16,128]{4,3,2,1,0:T(8,128)(2,1)S(1)}, u32[]{:S(2)}, u32[]{:S(2)}) collective-permute-start(bf16[2,16,2,16,128]{4,3,2,1,0:T(8,128)(2,1)S(1)} %pad_maximum_fusion.2), channel_id=1, source_target_pairs={{0,4},{2,6},{4,0},{6,2},{8,12},{10,14},{12,8},{14,10},{1,5},{3,7},... | collective-permute-start | bytes 786440 | tf_op jit(solution)/shard_map/ppermute | solution.py:483
  156.3 21.4 %collective-permute-start.15 = (bf16[2,16,2,16,128]{4,3,2,1,0:T(8,128)(2,1)S(1)}, bf16[2,16,2,16,128]{4,3,2,1,0:T(8,128)(2,1)S(1)}, u32[]{:S(2)}, u32[]{:S(2)}) collective-permute-start(bf16[2,16,2,16,128]{4,3,2,1,0:T(8,128)(2,1)S(1)} %pad_maximum_fusion.1), channel_id=1, source_target_pairs={{0,2},{2,4},{4,6},{6,0},{8,10},{10,12},{12,14},{14,8},{1,3},{3,5},... | collective-permute-start | bytes 786440 | tf_op jit(solution)/shard_map/ppermute | solution.py:483
  156.3 22.8 %collective-permute-start.20 = (bf16[2,16,2,16,128]{4,3,2,1,0:T(8,128)(2,1)S(1)}, bf16[2,16,2,16,128]{4,3,2,1,0:T(8,128)(2,1)S(1)}, u32[]{:S(2)}, u32[]{:S(2)}) collective-permute-start(bf16[2,16,2,16,128]{4,3,2,1,0:T(8,128)(2,1)S(1)} %pad_maximum_fusion.3), channel_id=1, source_target_pairs={{0,6},{2,0},{4,2},{6,4},{8,14},{10,8},{12,10},{14,12},{1,7},{3,1},... | collective-permute-start | bytes 786440 | tf_op jit(solution)/shard_map/ppermute | solution.py:483
  179.2 3.2 %collective-permute-start.21 = (bf16[8,16,2,16,128]{4,3,2,1,0:T(8,128)(2,1)S(1)}, bf16[8,16,2,16,128]{4,3,2,1,0:T(8,128)(2,1)S(1)}, u32[]{:S(2)}, u32[]{:S(2)}) collective-permute-start(bf16[8,16,2,16,128]{4,3,2,1,0:T(8,128)(2,1)S(1)} %bitcast.71), channel_id=1, source_target_pairs={{0,1},{1,0},{2,3},{3,2},{4,5},{5,4},{6,7},{7,6},{8,9},{9,8},{10,11... | collective-permute-start | bytes 3145736 | tf_op jit(solution)/shard_map/ppermute | solution.py:483
  180.2 14.3 %collective-permute-start.17 = (bf16[2,16,2,16,128]{4,3,2,1,0:T(8,128)(2,1)S(1)}, bf16[2,16,2,16,128]{4,3,2,1,0:T(8,128)(2,1)S(1)}, u32[]{:S(2)}, u32[]{:S(2)}) collective-permute-start(bf16[2,16,2,16,128]{4,3,2,1,0:T(8,128)(2,1)S(1)} %pad_maximum_fusion.4), channel_id=1, source_target_pairs={{0,2},{2,4},{4,6},{6,0},{8,10},{10,12},{12,14},{14,8},{1,3},{3,5},... | collective-permute-start | bytes 786440 | tf_op jit(solution)/shard_map/ppermute | solution.py:483
  180.7 22.5 %collective-permute-start.18 = (bf16[2,16,2,16,128]{4,3,2,1,0:T(8,128)(2,1)S(1)}, bf16[2,16,2,16,128]{4,3,2,1,0:T(8,128)(2,1)S(1)}, u32[]{:S(2)}, u32[]{:S(2)}) collective-permute-start(bf16[2,16,2,16,128]{4,3,2,1,0:T(8,128)(2,1)S(1)} %pad_maximum_fusion.5), channel_id=1, source_target_pairs={{0,4},{2,6},{4,0},{6,2},{8,12},{10,14},{12,8},{14,10},{1,5},{3,7},... | collective-permute-start | bytes 786440 | tf_op jit(solution)/shard_map/ppermute | solution.py:483
  180.7 22.5 %collective-permute-start.19 = (bf16[2,16,2,16,128]{4,3,2,1,0:T(8,128)(2,1)S(1)}, bf16[2,16,2,16,128]{4,3,2,1,0:T(8,128)(2,1)S(1)}, u32[]{:S(2)}, u32[]{:S(2)}) collective-permute-start(bf16[2,16,2,16,128]{4,3,2,1,0:T(8,128)(2,1)S(1)} %pad_maximum_fusion.6), channel_id=1, source_target_pairs={{0,6},{2,0},{4,2},{6,4},{8,14},{10,8},{12,10},{14,12},{1,7},{3,1},... | collective-permute-start | bytes 786440 | tf_op jit(solution)/shard_map/ppermute | solution.py:483
  203.2 2.0 collective-permute-start.22
  204.1 1.9 collective-permute-start.24
  (10 other events, 203.3 us)
